TPU v7x, 32 devices: a whole 2x2x4 slice. The times are simulated.
32 devices in a mesh: hist: 4 (over z), orow: 2 (over x), ocol: 4 (over y, core).
Axes of the slice: x: 2, y: 2, z: 4, core: 2. Of those that a mesh axis runs over, the one named last changes fastest.
Arguments:
- lesser_hist: float32 [2, 16, 256, 256], P(None, 'hist', 'ocol', 'orow'), may hold values from -6 to 6
- greater_hist: float32 [2, 16, 256, 256], P(None, 'hist', 'orow', 'ocol'), may hold values from -6 to 6
- advanced_hist: float32 [2, 16, 32, 256, 256], P(None, 'hist', 'ocol', None, 'orow'), may hold values from -6 to 6
- current_row: float32 [2, 32, 256, 256], P(None, 'ocol', 'hist', 'orow'), may hold values from -6 to 6
- adjacency: int32 [256, 256], P('hist'), may hold values from 0 to 1, as said below
- weight_table: int32 [16], P('hist'), may hold values from 1 to 48
- step_index: int32 [1], replicated, may hold values from 4 to 15
Outputs:
- new_row: float32 [2, 32, 256, 256], P(None, 'ocol', 'hist', 'orow')
Inputs may be any that keep to these rules, and one draw needn't show every extreme that they name: `adjacency`: symmetric, zero on the diagonal.
All inputs are finite; a program needn't handle non-finite values.
Results may differ from a plain program's by a relative error of at most 0.0001.
Values sent between devices are 32-bit elements; how exact they have to be, the bound alone decides.
No kernel may reach another device: no remote copies, remote signals or barrier semaphores. Data moves between devices by JAX's collectives and lax.ppermute only.
A program may use at most 64 MiB of HBM per device.

v0:
```python
import jax
import jax.numpy as jnp
from jax import lax
from jax.sharding import PartitionSpec as P

coupling_square = 0.25
hopping = 4.0
time_step = 0.01


def self_energy(lesser, greater_t):
    lesser_re, lesser_im = (lesser[0], lesser[1])
    greater_re, greater_im = (greater_t[0], greater_t[1])
    square_re = lesser_re * lesser_re - lesser_im * lesser_im
    square_im = 2.0 * lesser_re * lesser_im
    sigma_re = coupling_square * (square_re * greater_re - square_im * greater_im)
    sigma_im = coupling_square * (square_re * greater_im + square_im * greater_re)
    return jnp.stack([sigma_re, sigma_im])


def on_device(
    lesser_hist, greater_hist, advanced_hist, current_row, adjacency, weight_table, step_index
):
    slices_here = lesser_hist.shape[1]
    slot_ids = lax.axis_index("hist") * slices_here + lax.iota(jnp.int32, slices_here)
    weights = jnp.where(
        slot_ids <= step_index[0], weight_table.astype(jnp.float32) / 24.0, jnp.float32(0.0)
    )
    lesser_full, greater_full = (
        lax.all_gather(lesser_hist, "ocol", axis=2, tiled=True),
        lax.all_gather(greater_hist, "ocol", axis=3, tiled=True),
    )
    lesser_full, greater_full = (
        lax.all_gather(lesser_full, "orow", axis=3, tiled=True),
        lax.all_gather(greater_full, "orow", axis=2, tiled=True),
    )
    sigma = self_energy(lesser_full, jnp.swapaxes(greater_full, 2, 3))
    sigma_w = sigma * weights[None, :, None, None]
    combos = jnp.einsum(
        "csik,dstkj->cdtij",
        sigma_w,
        advanced_hist,
        precision=lax.Precision.HIGHEST,
        preferred_element_type=jnp.float32,
    )
    collision = jnp.stack([combos[0, 0] - combos[1, 1], combos[0, 1] + combos[1, 0]])
    hop_local = -hopping * adjacency.astype(jnp.float32)
    summed = lax.psum_scatter(collision, "hist", scatter_dimension=2, tiled=True)
    row_full = lax.all_gather(current_row, "hist", axis=2, tiled=True)
    summed = summed + jnp.einsum(
        "ik,ctkj->ctij",
        hop_local,
        row_full,
        precision=lax.Precision.HIGHEST,
        preferred_element_type=jnp.float32,
    )
    return jnp.stack(
        [current_row[0] + time_step * summed[1], current_row[1] - time_step * summed[0]]
    )


def solution(mesh):
    in_specs = (
        P(None, "hist", "ocol", "orow"),
        P(None, "hist", "orow", "ocol"),
        P(None, "hist", "ocol", None, "orow"),
        P(None, "ocol", "hist", "orow"),
        P("hist", None),
        P("hist"),
        P(),
    )
    out_specs = P(None, "ocol", "hist", "orow")
    return jax.shard_map(
        on_device, mesh=mesh, in_specs=in_specs, out_specs=out_specs, check_vma=False
    )
```

profile of v0, /device:TPU:0, one launch (start us, length us, event | category | flops | bytes accessed | tf_op | source)
XLA Modules:
  0.0 218.8 jit_solution(2001855699542194575)
XLA Ops:
  6.5 0.0 copy-start.2
  6.5 0.0 all-gather.6.cloned.1.call-start
  6.5 0.7 all-gather.6.cloned.1.call-update
  7.3 0.0 all-gather.10.cloned.1.call-start
  7.3 0.7 all-gather.10.cloned.1.call-update
  8.0 0.0 all-gather.8.cloned.1.call-start
  8.1 20.3 %all-gather.6.cloned.1.call-done = f32[2,4,256,128]{3,2,1,0:T(8,128)} async-done(((f32[2,4,64,128]{3,2,1,0:T(8,128)}), f32[2,4,256,128]{3,2,1,0:T(8,128)}) %all-gather.6.cloned.1.call-update) | async-done | bytes 1048592 | tf_op jit(solution)/shard_map/all_gather | solution.py:30
  28.4 0.0 all-gather.8.cloned.1.call-update
  28.4 0.0 all-gather.12.cloned.1.call-start
  28.4 18.2 %all-gather.10.cloned.1.call-done = f32[2,4,128,256]{2,3,1,0:T(8,128)} async-done(((f32[2,4,128,64]{2,3,1,0:T(8,128)}), f32[2,4,128,256]{2,3,1,0:T(8,128)}) %all-gather.10.cloned.1.call-update) | async-done | bytes 1048592 | tf_op jit(solution)/shard_map/all_gather | solution.py:31
  46.7 0.0 all-gather.12.cloned.1.call-update
  46.7 0.0 all-gather.14.cloned.1.call-start
  46.8 0.5 all-gather.14.cloned.1.call-update
  47.3 0.0 reduce-scatter.2.cloned.1.call-start
  48.0 0.0 copy-done.2
  48.0 33.3 %all-gather.8.cloned.1.call-done = f32[2,4,256,256]{3,2,1,0:T(8,128)} async-done(((f32[2,4,256,128]{3,2,1,0:T(8,128)}), f32[2,4,256,256]{3,2,1,0:T(8,128)}) %all-gather.8.cloned.1.call-update) | async-done | bytes 2097168 | tf_op jit(solution)/shard_map/all_gather | solution.py:34
  81.4 34.5 %all-gather.12.cloned.1.call-done = f32[2,4,256,256]{2,3,1,0:T(8,128)} async-done(((f32[2,4,128,256]{2,3,1,0:T(8,128)}), f32[2,4,256,256]{2,3,1,0:T(8,128)}) %all-gather.12.cloned.1.call-update) | async-done | bytes 2097168 | tf_op jit(solution)/shard_map/all_gather | solution.py:35
  115.9 2.6 %subtract_multiply_fusion = (f32[1,4,256,256]{3,2,1,0:T(8,128)S(1)}, f32[1,4,256,256]{3,2,1,0:T(8,128)S(1)}) fusion(f32[2,4,256,256]{3,2,1,0:T(8,128)} %bitcast.32, f32[2,4,256,256]{3,2,1,0:T(8,128)} %all-gather.8.cloned.1.call-done), kind=kLoop, calls=%fused_computation.17 | loop fusion | flops 3407872 | bytes 6291456 | tf_op jit(solution)/shard_map/mul | solution.py:16
  118.5 16.0 %fusion.3 = f32[2,2,8,256,128]{4,3,2,1,0:T(8,128)S(1)} fusion(f32[2,4,8,256,128]{4,3,2,1,0:T(8,128)} %param.9, f32[1,4,256,256]{3,2,1,0:T(8,128)S(1)} %get-tuple-element.8, f32[1,4,256,256]{3,2,1,0:T(8,128)S(1)} %get-tuple-element.7, f32[4]{0:T(128)S(1)} %compare_select_fusion), kind=kOutput, calls=%fused_computation.3 | convolution fusion | flops 12885950464 | bytes 14680080 | tf_op jit(solution)/shard_map/csik,dstkj->cdtij/dot_general | solution.py:39
  134.5 0.2 fusion.12
  134.7 1.4 pad_maximum_fusion
  136.2 0.0 copy-start.1
  136.2 0.0 reduce-scatter.2.cloned.1.call-update
  136.2 0.0 copy-start
  136.2 27.1 %all-gather.14.cloned.1.call-done = f32[2,8,256,128]{3,2,1,0:T(8,128)} async-done(((f32[2,8,64,128]{3,2,1,0:T(8,128)}), f32[2,8,256,128]{3,2,1,0:T(8,128)}) %all-gather.14.cloned.1.call-update) | async-done | bytes 2097168 | tf_op jit(solution)/shard_map/all_gather | solution.py:49
  163.3 44.7 %reduce-scatter.2.cloned.1.call-done = f32[2,8,64,128]{3,2,1,0:T(8,128)} async-done(((f32[2,8,256,128]{3,2,1,0:T(8,128)}), f32[2,8,64,128]{3,2,1,0:T(8,128)}) %reduce-scatter.2.cloned.1.call-update) | async-done | bytes 524304 | tf_op jit(solution)/shard_map/reduce_scatter | solution.py:48
  208.0 0.0 copy-done.1
  208.0 3.0 %fusion.10 = f32[2,8,64,128]{3,2,1,0:T(8,128)S(1)} fusion(f32[2,8,64,128]{3,2,1,0:T(8,128)} %reduce-scatter.2.cloned.1.call-done, f32[2,8,256,128]{3,2,1,0:T(8,128)} %all-gather.14.cloned.1.call-done, s32[64,256]{1,0:T(8,128)S(1)} %copy-done.1), kind=kOutput, calls=%fused_computation.10 | convolution fusion | flops 402817024 | bytes 3211264 | tf_op jit(solution)/shard_map/ik,ctkj->ctij/dot_general | solution.py:50
  211.1 0.0 copy-done
  211.1 0.1 fusion.15
  211.1 0.8 pad_maximum_fusion.1
  (1 shorter events, 0.0 us)
Async XLA Ops:
  6.5 41.5 %copy-start.2 = (s32[4]{0:T(128)S(1)}, s32[4]{0:T(128)}, u32[]{:S(2)}) copy-start(s32[4]{0:T(128)} %param.12) | copy-start | bytes 52
  6.5 21.8 %all-gather.6.cloned.1.call-start = ((), (), s32[]{:S(2)}) async-start(), calls=%async_computation.1 | async-start | bytes 1310720 | tf_op jit(solution)/shard_map/all_gather | solution.py:30
  7.3 39.4 %all-gather.10.cloned.1.call-start = ((), (), s32[]{:S(2)}) async-start(), calls=%async_computation.3 | async-start | bytes 1310720 | tf_op jit(solution)/shard_map/all_gather | solution.py:31
  8.0 73.3 %all-gather.8.cloned.1.call-start = ((), (), s32[]{:S(2)}) async-start(), calls=%async_computation.2 | async-start | bytes 3145728 | tf_op jit(solution)/shard_map/all_gather | solution.py:34
  28.4 87.5 %all-gather.12.cloned.1.call-start = ((), (), s32[]{:S(2)}) async-start(), calls=%async_computation.4 | async-start | bytes 3145728 | tf_op jit(solution)/shard_map/all_gather | solution.py:35
  46.7 116.5 %all-gather.14.cloned.1.call-start = ((), (), s32[]{:S(2)}) async-start(), calls=%async_computation.6 | async-start | bytes 2621440 | tf_op jit(solution)/shard_map/all_gather | solution.py:49
  47.3 160.7 %reduce-scatter.2.cloned.1.call-start = ((), (), s32[]{:S(2)}) async-start(), calls=%async_computation.5 | async-start | bytes 2621440 | tf_op jit(solution)/shard_map/reduce_scatter | solution.py:48
  136.2 71.8 %copy-start.1 = (s32[64,256]{1,0:T(8,128)S(1)}, s32[64,256]{1,0:T(8,128)}, u32[]{:S(2)}) copy-start(s32[64,256]{1,0:T(8,128)} %param.11) | copy-start | bytes 196612
  136.2 74.9 %copy-start = (f32[2,8,64,128]{3,2,1,0:T(8,128)S(1)}, f32[2,8,64,128]{3,2,1,0:T(8,128)}, u32[]{:S(2)}) copy-start(f32[2,8,64,128]{3,2,1,0:T(8,128)} %param.10) | copy-start | bytes 1572868
Sparse Core Ops, SparseCore 0:
  8.9 19.4 all-gather.5
  29.9 16.7 all-gather.9
  48.2 33.0 all-gather.7
  82.7 33.0 all-gather.11
  117.3 45.9 all-gather.13
  165.4 42.5 reduce-scatter.1
where the time goes:
time: 219 us
  waiting for transfers between devices  180 us (82%)
  matrix products  19 us (9%)
  between operations  14.2 us (6%)
  other arithmetic  5.2 us (2%)
    reduce_scatter x1, waiting for transfers between devices, on_device(): lax.psum_scatter(collision, 'hist', scatter_dimension=2, tiled=True)  44.7 us
    all_gather x1, waiting for transfers between devices, on_device(): lax.all_gather(greater_full, 'orow', axis=2, tiled=True)  34.5 us
    all_gather x1, waiting for transfers between devices, on_device(): lax.all_gather(lesser_full, 'orow', axis=3, tiled=True)  33.3 us
    all_gather x1, waiting for transfers between devices, on_device(): row_full = lax.all_gather(current_row, 'hist', axis=2, tiled=True)  27.1 us
    all_gather x1, waiting for transfers between devices, on_device(): lax.all_gather(lesser_hist, 'ocol', axis=2, tiled=True)  20.3 us
    all_gather x1, waiting for transfers between devices, on_device(): lax.all_gather(greater_hist, 'ocol', axis=3, tiled=True)  18.2 us
    dot_general x1, matrix products, on_device(): jnp.einsum('csik,dstkj->cdtij', sigma_w, advanced_hist, precision=lax.Pre...  16 us
  transfers between devices with their start and end apart: 6, of which 6 were waited for; matrix products, arithmetic and copies ran while one was open for 9% of the time, Pallas kernels for 0%

commit v1 on v0

v1 whole, which is shorter than its diff:
```python
import functools

import jax
import jax.numpy as jnp
from jax import lax
from jax.experimental import pallas as pl
from jax.experimental.pallas import tpu as pltpu
from jax.sharding import PartitionSpec as P

coupling_square = 0.25
hopping = 4.0
time_step = 0.01
CHUNKS = 4


def sigma_kernel(weights_ref, lesser_ref, greater_ref, out_ref):
    for s in range(lesser_ref.shape[1]):
        a_re, a_im = lesser_ref[0, s], lesser_ref[1, s]
        b_re, b_im = greater_ref[0, s].T, greater_ref[1, s].T
        square_re = a_re * a_re - a_im * a_im
        square_im = 2.0 * a_re * a_im
        scale = coupling_square * weights_ref[s]
        out_ref[0, s] = scale * (square_re * b_re - square_im * b_im)
        out_ref[1, s] = scale * (square_re * b_im + square_im * b_re)


def split(x):
    high = x.astype(jnp.bfloat16)
    return high, (x - high.astype(jnp.float32)).astype(jnp.bfloat16)


def chunk_kernel(masks, ends, where_ref, *refs):
    count = len(masks)
    blocks, refs = refs[:count], refs[count:]
    advanced_ref, row_ref, adjacency_ref = refs[:3]
    outs, (left_high, left_low, result) = refs[3:-3], refs[-3:]
    slices = advanced_ref.shape[1]
    my_orow, my_ocol, my_hist = where_ref[0], where_ref[1], where_ref[2]

    @pl.when(pl.program_id(0) == 0)
    def _():
        for (flip_orow, flip_ocol), block in zip(masks, blocks):
            at_orow = jnp.bitwise_xor(my_orow, flip_orow)
            at_ocol = jnp.bitwise_xor(my_ocol, flip_ocol)
            for s in range(slices):
                for part in range(2):
                    high, low = split(block[part, s])
                    left_high[s, at_orow, part, at_ocol] = high
                    left_low[s, at_orow, part, at_ocol] = low

    norb = advanced_ref.shape[3]
    width = advanced_ref.shape[4]
    halves = left_high.shape[1]

    def left(ref, s):
        return jnp.concatenate([ref[s, half].reshape(2 * norb, norb // halves) for half in range(halves)], axis=1)

    total = None
    for s in range(slices):
        right = jnp.concatenate([advanced_ref[0, s, 0], advanced_ref[1, s, 0]], axis=1)
        right_high, right_low = split(right)
        here = jnp.dot(
            jnp.concatenate([left(left_high, s), left(left_high, s), left(left_low, s)], axis=1),
            jnp.concatenate([right_high, right_low, right_high], axis=0),
            preferred_element_type=jnp.float32,
        )
        total = here if total is None else total + here
    hop = lax.dot_general(
        -hopping * adjacency_ref[...].astype(jnp.float32),
        jnp.concatenate([row_ref[0, 0], row_ref[1, 0]], axis=1),
        (((0,), (0,)), ((), ())),
        precision=lax.Precision.HIGHEST,
        preferred_element_type=jnp.float32,
    )
    sum_re = total[:norb, :width] - total[norb:, width:] + hop[:, :width]
    sum_im = total[:norb, width:] + total[norb:, :width] + hop[:, width:]
    if not ends:
        outs[0][0, 0] = sum_re
        outs[0][1, 0] = sum_im
        return
    rows = norb // len(outs)
    for block in range(len(outs)):
        result[block, 0] = sum_re[block * rows : (block + 1) * rows]
        result[block, 1] = sum_im[block * rows : (block + 1) * rows]
    for place, out in enumerate(outs):
        block = jnp.where(my_hist < len(outs) // 2, len(outs) - 1 - place, place)
        out[0, 0] = result[block, 0]
        out[1, 0] = result[block, 1]


def on_device(
    hist_size, orow_size, ocol_size, lesser_hist, greater_hist, advanced_hist, current_row, adjacency, weight_table, step_index
):
    slices = lesser_hist.shape[1]
    my_hist, my_orow, my_ocol = lax.axis_index("hist"), lax.axis_index("orow"), lax.axis_index("ocol")
    slot_ids = my_hist * slices + lax.iota(jnp.int32, slices)
    weights = jnp.where(
        slot_ids <= step_index[0], weight_table.astype(jnp.float32) / 24.0, jnp.float32(0.0)
    )
    vmem = pl.BlockSpec(memory_space=pltpu.VMEM)
    smem = pl.BlockSpec(memory_space=pltpu.SMEM)
    sigma = pl.pallas_call(
        sigma_kernel,
        out_shape=jax.ShapeDtypeStruct(lesser_hist.shape, jnp.float32),
        in_specs=[smem, vmem, vmem],
        out_specs=vmem,
        name="sigma",
    )(weights, lesser_hist, greater_hist)

    def flipped(x, flip_orow, flip_ocol):
        pairs = [
            (r * ocol_size + c, (r ^ flip_orow) * ocol_size + (c ^ flip_ocol))
            for r in range(orow_size)
            for c in range(ocol_size)
        ]
        return lax.ppermute(x, ("orow", "ocol"), pairs)

    masks = [(r, c) for c in range(0, ocol_size, 2) for r in range(orow_size)]
    held = {mask: sigma if mask == (0, 0) else flipped(sigma, *mask) for mask in masks}
    for r, c in masks:
        held[(r, c + 1)] = flipped(held[(r, c)], 0, 1)
    masks = tuple(held)

    times, norb, width = advanced_hist.shape[2:]
    each = times // CHUNKS
    rows = norb // hist_size
    line = hist_size == 4
    where = jnp.stack([my_orow, my_ocol, my_hist]).astype(jnp.int32)
    block_shape = lesser_hist.shape
    pieces = []
    for chunk in range(CHUNKS):
        if line:
            out_shape = [jax.ShapeDtypeStruct((2, each, rows, width), jnp.float32)] * hist_size
            out_specs = [pl.BlockSpec((2, 1, rows, width), lambda t: (0, t, 0, 0))] * hist_size
        else:
            out_shape = [jax.ShapeDtypeStruct((2, each, norb, width), jnp.float32)]
            out_specs = [pl.BlockSpec((2, 1, norb, width), lambda t: (0, t, 0, 0))]
        first = chunk * each
        parts = pl.pallas_call(
            functools.partial(chunk_kernel, masks, line),
            grid=(each,),
            out_shape=out_shape,
            in_specs=[smem]
            + [pl.BlockSpec(block_shape, lambda t: (0, 0, 0, 0))] * len(masks)
            + [
                pl.BlockSpec((2, slices, 1, norb, width), lambda t, first=first: (0, 0, first + t, 0, 0)),
                pl.BlockSpec((2, 1, current_row.shape[2], width), lambda t, first=first: (0, first + t, 0, 0)),
                pl.BlockSpec(adjacency.shape, lambda t: (0, 0)),
            ],
            out_specs=out_specs,
            scratch_shapes=[
                pltpu.VMEM((slices, orow_size, 2, ocol_size) + block_shape[2:], jnp.bfloat16),
                pltpu.VMEM((slices, orow_size, 2, ocol_size) + block_shape[2:], jnp.bfloat16),
                pltpu.VMEM((hist_size, 2, rows, width), jnp.float32),
            ],
            compiler_params=pltpu.CompilerParams(vmem_limit_bytes=40 * 1024 * 1024),
            name=f"products_{chunk}",
        )(where, *[held[mask] for mask in masks], advanced_hist, current_row, adjacency)
        if not line:
            pieces.append(lax.psum_scatter(parts[0], "hist", scatter_dimension=2, tiled=True))
            continue
        inward = [lax.ppermute(part, "hist", [(0, 1), (3, 2)]) for part in parts[:3]]
        across = [lax.ppermute(parts[m] + inward[m], "hist", [(1, 2), (2, 1)]) for m in range(2)]
        outward = lax.ppermute(parts[3] + across[0], "hist", [(2, 3), (1, 0)])
        at_end = jnp.logical_or(my_hist == 0, my_hist == hist_size - 1)
        pieces.append(jnp.where(at_end, parts[3] + outward, parts[2] + inward[2] + across[1]))
    summed = jnp.concatenate(pieces, axis=1)
    return jnp.stack(
        [current_row[0] + time_step * summed[1], current_row[1] - time_step * summed[0]]
    )


def solution(mesh):
    in_specs = (
        P(None, "hist", "ocol", "orow"),
        P(None, "hist", "orow", "ocol"),
        P(None, "hist", "ocol", None, "orow"),
        P(None, "ocol", "hist", "orow"),
        P("hist", None),
        P("hist"),
        P(),
    )
    out_specs = P(None, "ocol", "hist", "orow")
    body = functools.partial(on_device, mesh.shape["hist"], mesh.shape["orow"], mesh.shape["ocol"])
    return jax.shard_map(
        body, mesh=mesh, in_specs=in_specs, out_specs=out_specs, check_vma=False
    )
```

time: 219 us -> 102 us (0.47)
  waiting for transfers between devices: 180 us -> 23.5 us
  starting transfers between devices: 0.19 us -> 45.7 us
  matrix products: 19 us -> 0 us
  Pallas kernels: 0 us -> 16.8 us
  between operations: 14.2 us -> 1.21 us
  local copies, waits for them, and re-layouts: 0.01 us -> 8.84 us
    all_gather x5 -> x0, waiting for transfers between devices: 133 us -> none  [the longest x1 34.5 us: on_device(): lax.all_gather(greater_full, 'orow', axis=2, tiled=True)]
    ppermute x0 -> x31, starting transfers between devices: none -> 45.7 us  [the longest x12 30.2 us: on_device(): lax.ppermute(part, 'hist', [(0, 1), (3, 2)])]
    reduce_scatter x1 -> x0, waiting for transfers between devices: 44.7 us -> none  [on_device(): lax.psum_scatter(collision, 'hist', scatter_dimension=2, tiled=True)]
    ppermute x0 -> x31, waiting for transfers between devices: none -> 23.5 us  [the longest x7 13.4 us: flipped(): return lax.ppermute(x, ('orow', 'ocol'), pairs)]
    dot_general x2 -> x0, matrix products: 19 us -> none  [the longest x1 16 us: on_device(): jnp.einsum('csik,dstkj->cdtij', sigma_w, advanced_hist, precision=lax.Pre...]
    pallas_call x0 -> x5, Pallas kernels: none -> 16.8 us  [the longest x4 14.8 us: on_device(): pl.pallas_call(functools.partial(chunk_kernel, masks, line), grid=(each,)...]
    unnamed x6 -> x19, local copies, waits for them, and re-layouts: 0.01 us -> 8.84 us
    mul x1 -> x0, other arithmetic: 2.61 us -> none  [self_energy(): coupling_square * (square_re * greater_re - square_im * greater_im)]
  transfers between devices with their start and end apart: 6 -> 31, of which waited for: 6 -> 7; matrix products, arithmetic and copies ran while one was open for 9% -> 3% of each run, Pallas kernels for 0% -> 11%
where the time goes in v1:
time: 102 us; the launch traced here: 101 us
  starting transfers between devices  45.7 us (45%)
  waiting for transfers between devices  23.5 us (23%)
  Pallas kernels  16.8 us (16%)
  local copies, waits for them, and re-layouts  8.84 us (9%)
  other arithmetic  5.3 us (5%)
  between operations  1.21 us (1%)
    ppermute x12, starting transfers between devices, on_device(): lax.ppermute(part, 'hist', [(0, 1), (3, 2)])  30.2 us
    pallas_call x4, Pallas kernels, on_device(): pl.pallas_call(functools.partial(chunk_kernel, masks, line), grid=(each,)...  14.8 us
    ppermute x7, waiting for transfers between devices, flipped(): return lax.ppermute(x, ('orow', 'ocol'), pairs)  13.4 us
    ppermute x4, waiting for transfers between devices, on_device(): outward = lax.ppermute(parts[3] + across[0], 'hist', [(2, 3), (1, 0)])  10 us
    unnamed x19, local copies, waits for them, and re-layouts  8.84 us
    ppermute x8, starting transfers between devices, on_device(): lax.ppermute(parts[m] + inward[m], 'hist', [(1, 2), (2, 1)])  5.35 us
    ppermute x4, starting transfers between devices, on_device(): outward = lax.ppermute(parts[3] + across[0], 'hist', [(2, 3), (1, 0)])  5.16 us
    ppermute x7, starting transfers between devices, flipped(): return lax.ppermute(x, ('orow', 'ocol'), pairs)  4.98 us
  transfers between devices with their start and end apart: 31, of which 7 were waited for; matrix products, arithmetic and copies ran while one was open for 3% of the time, Pallas kernels for 11%

profile of v1, /device:TPU:0, one launch (start us, length us, event | category | flops | bytes accessed | tf_op | source)
XLA Modules:
  0.0 101.3 jit_solution(5167556588604708431)
XLA Ops:
  0.7 1.9 %copy.8.greater_ref = f32[2,4,128,64]{3,2,1,0:T(8,128)} copy(f32[2,4,128,64]{2,3,1,0:T(8,128)} %param.8) | data formatting | bytes 524288 | tf_op args[1]
  2.6 1.1 %compare_select_fusion.weights_ref = f32[4]{0:T(128)} fusion(s32[4]{0:T(128)} %param.12, s32[]{:T(128)} %bitcast.4, s32[]{:T(128)S(6)} %mul.11), kind=kLoop, calls=%fused_computation.10 | loop fusion | flops 20 | bytes 40 | tf_op jit(solution)/shard_map/jit(_where)/select_n | solution.py:97
  3.7 2.0 %sigma.1.refs_0_ = f32[2,4,64,128]{3,2,1,0:T(8,128)} custom-call(f32[4]{0:T(128)} %compare_select_fusion.weights_ref, f32[2,4,64,128]{3,2,1,0:T(8,128)} %lesser_ref.1, f32[2,4,128,64]{3,2,1,0:T(8,128)} %copy.8.greater_ref), custom_call_target="tpu_custom_call" | custom-call | tf_op jit(solution)/shard_map/sigma/pallas_call | solution.py:102
  5.8 2.9 %collective-permute-start = (f32[2,4,64,128]{3,2,1,0:T(8,128)}, f32[2,4,64,128]{3,2,1,0:T(8,128)S(1)}, u32[]{:S(2)}, u32[]{:S(2)}) collective-permute-start(f32[2,4,64,128]{3,2,1,0:T(8,128)} %sigma.1.refs_0_), channel_id=1, source_target_pairs={{0,4},{1,5},{2,6},{3,7},{4,0},{5,1},{6,2},{7,3},{8,12},{9,13},{10,... | collective-permute-start | bytes 786440 | tf_op jit(solution)/shard_map/ppermute | solution.py:116
  8.7 1.5 %collective-permute-start.1 = (f32[2,4,64,128]{3,2,1,0:T(8,128)}, f32[2,4,64,128]{3,2,1,0:T(8,128)S(1)}, u32[]{:S(2)}, u32[]{:S(2)}) collective-permute-start(f32[2,4,64,128]{3,2,1,0:T(8,128)} %sigma.1.refs_0_), channel_id=1, source_target_pairs={{0,2},{1,3},{2,0},{3,1},{4,6},{5,7},{6,4},{7,5},{8,10},{9,11},{10,... | collective-permute-start | bytes 786440 | tf_op jit(solution)/shard_map/ppermute | solution.py:116
  10.2 5.8 %collective-permute-done.refs_1_ = f32[2,4,64,128]{3,2,1,0:T(8,128)S(1)} collective-permute-done((f32[2,4,64,128]{3,2,1,0:T(8,128)}, f32[2,4,64,128]{3,2,1,0:T(8,128)S(1)}, u32[]{:S(2)}, u32[]{:S(2)}) %collective-permute-start) | collective-permute-done | bytes 262176 | tf_op jit(solution)/shard_map/ppermute | solution.py:116
  16.0 6.2 %collective-permute-done.1.refs_2_ = f32[2,4,64,128]{3,2,1,0:T(8,128)S(1)} collective-permute-done((f32[2,4,64,128]{3,2,1,0:T(8,128)}, f32[2,4,64,128]{3,2,1,0:T(8,128)S(1)}, u32[]{:S(2)}, u32[]{:S(2)}) %collective-permute-start.1) | collective-permute-done | bytes 262176 | tf_op jit(solution)/shard_map/ppermute | solution.py:116
  22.9 0.9 collective-permute-done.5.refs_6_
  24.2 3.4 %copy-done = f32[2,4,8,256,128]{4,3,2,1,0:T(8,128)S(1)} copy-done((f32[2,4,8,256,128]{4,3,2,1,0:T(8,128)S(1)}, f32[2,4,8,256,128]{4,3,2,1,0:T(8,128)}, u32[]{:S(2)}) %copy-start) | copy-done | bytes 8388632
  27.6 1.0 %copy-done.1 = f32[2,8,64,128]{3,2,1,0:T(8,128)S(1)} copy-done((f32[2,8,64,128]{3,2,1,0:T(8,128)S(1)}, f32[2,8,64,128]{3,2,1,0:T(8,128)}, u32[]{:S(2)}) %copy-start.1) | copy-done | bytes 524312
  28.6 0.9 copy-done.3
  29.6 0.8 copy-done.5
  30.4 4.1 %products_0.1 = (f32[2,2,64,128]{3,2,1,0:T(8,128)S(1)}, f32[2,2,64,128]{3,2,1,0:T(8,128)S(1)}, f32[2,2,64,128]{3,2,1,0:T(8,128)}, f32[2,2,64,128]{3,2,1,0:T(8,128)S(1)}) custom-call(s32[3]{0:T(128)S(1)} %pad_add_fusion.where_ref, f32[2,4,64,128]{3,2,1,0:T(8,128)S(1)} %copy-done.3, f32[2,4,64,128]{3,2,1,0:T(8,128)S(1)} %collective-permute-done.refs_1_, ...), custom_call_target="tpu_custom_call" | custom-call | tf_op jit(solution)/shard_map/products_0/pallas_call | solution.py:139
  34.5 3.5 %collective-permute-start.7 = (f32[2,2,64,128]{3,2,1,0:T(8,128)S(1)}, f32[2,2,64,128]{3,2,1,0:T(8,128)S(1)}, u32[]{:S(2)}, u32[]{:S(2)}) collective-permute-start(f32[2,2,64,128]{3,2,1,0:T(8,128)S(1)} %get-tuple-element.22), channel_id=1, source_target_pairs={{0,8},{24,16},{1,9},{25,17},{2,10},{26,18},{3,11},{27,19},{4,12},{... | collective-permute-start | bytes 393224 | tf_op jit(solution)/shard_map/ppermute | solution.py:162
  38.0 1.4 %collective-permute-start.11 = (f32[2,2,64,128]{3,2,1,0:T(8,128)S(1)}, f32[2,2,64,128]{3,2,1,0:T(8,128)S(1)}, u32[]{:S(2)}, u32[]{:S(2)}) collective-permute-start(f32[2,2,64,128]{3,2,1,0:T(8,128)S(1)} %get-tuple-element.24), channel_id=1, source_target_pairs={{0,8},{24,16},{1,9},{25,17},{2,10},{26,18},{3,11},{27,19},{4,12},{... | collective-permute-start | bytes 393224 | tf_op jit(solution)/shard_map/ppermute | solution.py:162
  39.5 3.6 %products_1.1 = (f32[2,2,64,128]{3,2,1,0:T(8,128)S(1)}, f32[2,2,64,128]{3,2,1,0:T(8,128)S(1)}, f32[2,2,64,128]{3,2,1,0:T(8,128)S(1)}, f32[2,2,64,128]{3,2,1,0:T(8,128)S(1)}) custom-call(s32[3]{0:T(128)S(1)} %pad_add_fusion.where_ref, f32[2,4,64,128]{3,2,1,0:T(8,128)S(1)} %copy-done.3, f32[2,4,64,128]{3,2,1,0:T(8,128)S(1)} %collective-permute-done.refs_1_, ...), custom_call_target="tpu_custom_call" | custom-call | tf_op jit(solution)/shard_map/products_1/pallas_call | solution.py:139
  43.0 0.6 copy-done.7
  43.7 1.3 %collective-permute-start.13 = (f32[2,2,64,128]{3,2,1,0:T(8,128)S(1)}, f32[2,2,64,128]{3,2,1,0:T(8,128)S(1)}, u32[]{:S(2)}, u32[]{:S(2)}) collective-permute-start(f32[2,2,64,128]{3,2,1,0:T(8,128)S(1)} %get-tuple-element.26), channel_id=1, source_target_pairs={{0,8},{24,16},{1,9},{25,17},{2,10},{26,18},{3,11},{27,19},{4,12},{... | collective-permute-start | bytes 393224 | tf_op jit(solution)/shard_map/ppermute | solution.py:162
  45.0 1.3 %collective-permute-start.17 = (f32[2,2,64,128]{3,2,1,0:T(8,128)S(1)}, f32[2,2,64,128]{3,2,1,0:T(8,128)S(1)}, u32[]{:S(2)}, u32[]{:S(2)}) collective-permute-start(f32[2,2,64,128]{3,2,1,0:T(8,128)S(1)} %get-tuple-element.28), channel_id=1, source_target_pairs={{0,8},{24,16},{1,9},{25,17},{2,10},{26,18},{3,11},{27,19},{4,12},{... | collective-permute-start | bytes 393224 | tf_op jit(solution)/shard_map/ppermute | solution.py:162
  46.3 3.6 %products_2.1 = (f32[2,2,64,128]{3,2,1,0:T(8,128)S(1)}, f32[2,2,64,128]{3,2,1,0:T(8,128)S(1)}, f32[2,2,64,128]{3,2,1,0:T(8,128)S(1)}, f32[2,2,64,128]{3,2,1,0:T(8,128)S(1)}) custom-call(s32[3]{0:T(128)S(1)} %pad_add_fusion.where_ref, f32[2,4,64,128]{3,2,1,0:T(8,128)S(1)} %copy-done.3, f32[2,4,64,128]{3,2,1,0:T(8,128)S(1)} %collective-permute-done.refs_1_, ...), custom_call_target="tpu_custom_call" | custom-call | tf_op jit(solution)/shard_map/products_2/pallas_call | solution.py:139
  49.9 1.4 %collective-permute-start.19 = (f32[2,2,64,128]{3,2,1,0:T(8,128)S(1)}, f32[2,2,64,128]{3,2,1,0:T(8,128)S(1)}, u32[]{:S(2)}, u32[]{:S(2)}) collective-permute-start(f32[2,2,64,128]{3,2,1,0:T(8,128)S(1)} %get-tuple-element.30), channel_id=1, source_target_pairs={{0,8},{24,16},{1,9},{25,17},{2,10},{26,18},{3,11},{27,19},{4,12},{... | collective-permute-start | bytes 393224 | tf_op jit(solution)/shard_map/ppermute | solution.py:162
  51.3 3.6 %products_3.1 = (f32[2,2,64,128]{3,2,1,0:T(8,128)S(1)}, f32[2,2,64,128]{3,2,1,0:T(8,128)S(1)}, f32[2,2,64,128]{3,2,1,0:T(8,128)S(1)}, f32[2,2,64,128]{3,2,1,0:T(8,128)S(1)}) custom-call(s32[3]{0:T(128)S(1)} %pad_add_fusion.where_ref, f32[2,4,64,128]{3,2,1,0:T(8,128)S(1)} %copy-done.4, f32[2,4,64,128]{3,2,1,0:T(8,128)S(1)} %collective-permute-done.refs_1_, ...), custom_call_target="tpu_custom_call" | custom-call | tf_op jit(solution)/shard_map/products_3/pallas_call | solution.py:139
  54.9 1.3 %collective-permute-start.25 = (f32[2,2,64,128]{3,2,1,0:T(8,128)S(1)}, f32[2,2,64,128]{3,2,1,0:T(8,128)S(1)}, u32[]{:S(2)}, u32[]{:S(2)}) collective-permute-start(f32[2,2,64,128]{3,2,1,0:T(8,128)S(1)} %get-tuple-element.34), channel_id=1, source_target_pairs={{0,8},{24,16},{1,9},{25,17},{2,10},{26,18},{3,11},{27,19},{4,12},{... | collective-permute-start | bytes 393224 | tf_op jit(solution)/shard_map/ppermute | solution.py:162
  56.2 1.3 %collective-permute-start.23 = (f32[2,2,64,128]{3,2,1,0:T(8,128)S(1)}, f32[2,2,64,128]{3,2,1,0:T(8,128)S(1)}, u32[]{:S(2)}, u32[]{:S(2)}) collective-permute-start(f32[2,2,64,128]{3,2,1,0:T(8,128)S(1)} %get-tuple-element.32), channel_id=1, source_target_pairs={{0,8},{24,16},{1,9},{25,17},{2,10},{26,18},{3,11},{27,19},{4,12},{... | collective-permute-start | bytes 393224 | tf_op jit(solution)/shard_map/ppermute | solution.py:162
  57.6 0.7 collective-permute-start.8
  58.3 4.1 %collective-permute-start.29 = (f32[2,2,64,128]{3,2,1,0:T(8,128)S(1)}, f32[2,2,64,128]{3,2,1,0:T(8,128)S(1)}, u32[]{:S(2)}, u32[]{:S(2)}) collective-permute-start(f32[2,2,64,128]{3,2,1,0:T(8,128)S(1)} %get-tuple-element.36), channel_id=1, source_target_pairs={{0,8},{24,16},{1,9},{25,17},{2,10},{26,18},{3,11},{27,19},{4,12},{... | collective-permute-start | bytes 393224 | tf_op jit(solution)/shard_map/ppermute | solution.py:162
  62.4 0.7 collective-permute-start.14
  63.1 0.7 collective-permute-start.20
  63.8 0.7 collective-permute-start.26
  64.5 7.5 %collective-permute-start.10 = (f32[2,2,64,128]{3,2,1,0:T(8,128)}, f32[2,2,64,128]{3,2,1,0:T(8,128)S(1)}, u32[]{:S(2)}, u32[]{:S(2)}) collective-permute-start(f32[2,2,64,128]{3,2,1,0:T(8,128)} %get-tuple-element.23), channel_id=1, source_target_pairs={{0,8},{24,16},{1,9},{25,17},{2,10},{26,18},{3,11},{27,19},{4,12},{... | collective-permute-start | bytes 393224 | tf_op jit(solution)/shard_map/ppermute | solution.py:162
  72.1 0.7 collective-permute-start.12
  72.8 1.3 %collective-permute-start.9 = (f32[2,2,64,128]{3,2,1,0:T(8,128)S(1)}, f32[2,2,64,128]{3,2,1,0:T(8,128)S(1)}, u32[]{:S(2)}, u32[]{:S(2)}) collective-permute-start(f32[2,2,64,128]{3,2,1,0:T(8,128)S(1)} %add.85), channel_id=1, source_target_pairs={{16,24},{8,0},{17,25},{9,1},{18,26},{10,2},{19,27},{11,3},{20,28},... | collective-permute-start | bytes 393224 | tf_op jit(solution)/shard_map/ppermute | solution.py:164
  74.1 0.9 add.94
  75.1 4.6 %collective-permute-start.16 = (f32[2,2,64,128]{3,2,1,0:T(8,128)}, f32[2,2,64,128]{3,2,1,0:T(8,128)S(1)}, u32[]{:S(2)}, u32[]{:S(2)}) collective-permute-start(f32[2,2,64,128]{3,2,1,0:T(8,128)} %copy-done.7), channel_id=1, source_target_pairs={{0,8},{24,16},{1,9},{25,17},{2,10},{26,18},{3,11},{27,19},{4,12},{... | collective-permute-start | bytes 393224 | tf_op jit(solution)/shard_map/ppermute | solution.py:162
  79.7 1.3 %collective-permute-start.22 = (f32[2,2,64,128]{3,2,1,0:T(8,128)S(1)}, f32[2,2,64,128]{3,2,1,0:T(8,128)S(1)}, u32[]{:S(2)}, u32[]{:S(2)}) collective-permute-start(f32[2,2,64,128]{3,2,1,0:T(8,128)S(1)} %get-tuple-element.31), channel_id=1, source_target_pairs={{0,8},{24,16},{1,9},{25,17},{2,10},{26,18},{3,11},{27,19},{4,12},{... | collective-permute-start | bytes 393224 | tf_op jit(solution)/shard_map/ppermute | solution.py:162
  81.0 1.3 %collective-permute-start.28 = (f32[2,2,64,128]{3,2,1,0:T(8,128)S(1)}, f32[2,2,64,128]{3,2,1,0:T(8,128)S(1)}, u32[]{:S(2)}, u32[]{:S(2)}) collective-permute-start(f32[2,2,64,128]{3,2,1,0:T(8,128)S(1)} %get-tuple-element.35), channel_id=1, source_target_pairs={{0,8},{24,16},{1,9},{25,17},{2,10},{26,18},{3,11},{27,19},{4,12},{... | collective-permute-start | bytes 393224 | tf_op jit(solution)/shard_map/ppermute | solution.py:162
  82.3 0.7 collective-permute-start.18
  83.0 1.3 %collective-permute-start.15 = (f32[2,2,64,128]{3,2,1,0:T(8,128)S(1)}, f32[2,2,64,128]{3,2,1,0:T(8,128)S(1)}, u32[]{:S(2)}, u32[]{:S(2)}) collective-permute-start(f32[2,2,64,128]{3,2,1,0:T(8,128)S(1)} %add.91), channel_id=1, source_target_pairs={{16,24},{8,0},{17,25},{9,1},{18,26},{10,2},{19,27},{11,3},{20,28},... | collective-permute-start | bytes 393224 | tf_op jit(solution)/shard_map/ppermute | solution.py:164
  84.3 0.9 add_select_fusion.3
  85.3 0.7 collective-permute-start.24
  86.0 0.7 collective-permute-start.30
  86.6 3.2 %collective-permute-done.15 = f32[2,2,64,128]{3,2,1,0:T(8,128)S(1)} collective-permute-done((f32[2,2,64,128]{3,2,1,0:T(8,128)S(1)}, f32[2,2,64,128]{3,2,1,0:T(8,128)S(1)}, u32[]{:S(2)}, u32[]{:S(2)}) %collective-permute-start.15) | collective-permute-done | bytes 131104 | tf_op jit(solution)/shard_map/ppermute | solution.py:164
  89.9 1.3 %collective-permute-start.21 = (f32[2,2,64,128]{3,2,1,0:T(8,128)S(1)}, f32[2,2,64,128]{3,2,1,0:T(8,128)S(1)}, u32[]{:S(2)}, u32[]{:S(2)}) collective-permute-start(f32[2,2,64,128]{3,2,1,0:T(8,128)S(1)} %add.97), channel_id=1, source_target_pairs={{16,24},{8,0},{17,25},{9,1},{18,26},{10,2},{19,27},{11,3},{20,28},... | collective-permute-start | bytes 393224 | tf_op jit(solution)/shard_map/ppermute | solution.py:164
  91.2 0.9 add_select_fusion.2
  92.1 1.3 %collective-permute-start.27 = (f32[2,2,64,128]{3,2,1,0:T(8,128)S(1)}, f32[2,2,64,128]{3,2,1,0:T(8,128)S(1)}, u32[]{:S(2)}, u32[]{:S(2)}) collective-permute-start(f32[2,2,64,128]{3,2,1,0:T(8,128)S(1)} %add.103), channel_id=1, source_target_pairs={{16,24},{8,0},{17,25},{9,1},{18,26},{10,2},{19,27},{11,3},{20,28},... | collective-permute-start | bytes 393224 | tf_op jit(solution)/shard_map/ppermute | solution.py:164
  93.4 4.9 %collective-permute-done.21 = f32[2,2,64,128]{3,2,1,0:T(8,128)S(1)} collective-permute-done((f32[2,2,64,128]{3,2,1,0:T(8,128)S(1)}, f32[2,2,64,128]{3,2,1,0:T(8,128)S(1)}, u32[]{:S(2)}, u32[]{:S(2)}) %collective-permute-start.21) | collective-permute-done | bytes 131104 | tf_op jit(solution)/shard_map/ppermute | solution.py:164
  98.4 1.9 %collective-permute-done.27 = f32[2,2,64,128]{3,2,1,0:T(8,128)S(1)} collective-permute-done((f32[2,2,64,128]{3,2,1,0:T(8,128)S(1)}, f32[2,2,64,128]{3,2,1,0:T(8,128)S(1)}, u32[]{:S(2)}, u32[]{:S(2)}) %collective-permute-start.27) | collective-permute-done | bytes 131104 | tf_op jit(solution)/shard_map/ppermute | solution.py:164
  100.5 0.8 pad_maximum_fusion.1
  (59 shorter events, 1.5 us)
Async XLA Ops:
  5.8 10.3 %collective-permute-start = (f32[2,4,64,128]{3,2,1,0:T(8,128)}, f32[2,4,64,128]{3,2,1,0:T(8,128)S(1)}, u32[]{:S(2)}, u32[]{:S(2)}) collective-permute-start(f32[2,4,64,128]{3,2,1,0:T(8,128)} %sigma.1.refs_0_), channel_id=1, source_target_pairs={{0,4},{1,5},{2,6},{3,7},{4,0},{5,1},{6,2},{7,3},{8,12},{9,13},{10,... | collective-permute-start | bytes 786440 | tf_op jit(solution)/shard_map/ppermute | solution.py:116
  8.7 13.6 %collective-permute-start.1 = (f32[2,4,64,128]{3,2,1,0:T(8,128)}, f32[2,4,64,128]{3,2,1,0:T(8,128)S(1)}, u32[]{:S(2)}, u32[]{:S(2)}) collective-permute-start(f32[2,4,64,128]{3,2,1,0:T(8,128)} %sigma.1.refs_0_), channel_id=1, source_target_pairs={{0,2},{1,3},{2,0},{3,1},{4,6},{5,7},{6,4},{7,5},{8,10},{9,11},{10,... | collective-permute-start | bytes 786440 | tf_op jit(solution)/shard_map/ppermute | solution.py:116
  10.2 12.1 %collective-permute-start.2 = (f32[2,4,64,128]{3,2,1,0:T(8,128)}, f32[2,4,64,128]{3,2,1,0:T(8,128)S(1)}, u32[]{:S(2)}, u32[]{:S(2)}) collective-permute-start(f32[2,4,64,128]{3,2,1,0:T(8,128)} %sigma.1.refs_0_), channel_id=1, source_target_pairs={{0,6},{1,7},{2,4},{3,5},{4,2},{5,3},{6,0},{7,1},{8,14},{9,15},{10,... | collective-permute-start | bytes 786440 | tf_op jit(solution)/shard_map/ppermute | solution.py:116
  10.2 12.7 %collective-permute-start.3 = (f32[2,4,64,128]{3,2,1,0:T(8,128)}, f32[2,4,64,128]{3,2,1,0:T(8,128)S(1)}, u32[]{:S(2)}, u32[]{:S(2)}) collective-permute-start(f32[2,4,64,128]{3,2,1,0:T(8,128)} %sigma.1.refs_0_), channel_id=1, source_target_pairs={{0,1},{1,0},{2,3},{3,2},{4,5},{5,4},{6,7},{7,6},{8,9},{9,8},{10,11... | collective-permute-start | bytes 786440 | tf_op jit(solution)/shard_map/ppermute | solution.py:116
  16.0 6.8 %collective-permute-start.4 = (f32[2,4,64,128]{3,2,1,0:T(8,128)S(1)}, f32[2,4,64,128]{3,2,1,0:T(8,128)S(1)}, u32[]{:S(2)}, u32[]{:S(2)}) collective-permute-start(f32[2,4,64,128]{3,2,1,0:T(8,128)S(1)} %collective-permute-done.refs_1_), channel_id=1, source_target_pairs={{0,1},{1,0},{2,3},{3,2},{4,5},{5,4},{6,7},{7,6},{8,9},{9,8},{10,11... | collective-permute-start | bytes 786440 | tf_op jit(solution)/shard_map/ppermute | solution.py:116
  22.3 1.5 %collective-permute-start.5 = (f32[2,4,64,128]{3,2,1,0:T(8,128)S(1)}, f32[2,4,64,128]{3,2,1,0:T(8,128)S(1)}, u32[]{:S(2)}, u32[]{:S(2)}) collective-permute-start(f32[2,4,64,128]{3,2,1,0:T(8,128)S(1)} %collective-permute-done.1.refs_2_), channel_id=1, source_target_pairs={{0,1},{1,0},{2,3},{3,2},{4,5},{5,4},{6,7},{7,6},{8,9},{9,8},{10,11... | collective-permute-start | bytes 786440 | tf_op jit(solution)/shard_map/ppermute | solution.py:116
  22.3 1.9 %collective-permute-start.6 = (f32[2,4,64,128]{3,2,1,0:T(8,128)S(1)}, f32[2,4,64,128]{3,2,1,0:T(8,128)S(1)}, u32[]{:S(2)}, u32[]{:S(2)}) collective-permute-start(f32[2,4,64,128]{3,2,1,0:T(8,128)S(1)} %collective-permute-done.2.refs_3_), channel_id=1, source_target_pairs={{0,1},{1,0},{2,3},{3,2},{4,5},{5,4},{6,7},{7,6},{8,9},{9,8},{10,11... | collective-permute-start | bytes 786440 | tf_op jit(solution)/shard_map/ppermute | solution.py:116
  24.2 3.4 %copy-start = (f32[2,4,8,256,128]{4,3,2,1,0:T(8,128)S(1)}, f32[2,4,8,256,128]{4,3,2,1,0:T(8,128)}, u32[]{:S(2)}) copy-start(f32[2,4,8,256,128]{4,3,2,1,0:T(8,128)} %refs_8_.7) | copy-start | bytes 25165828
  27.6 1.0 %copy-start.1 = (f32[2,8,64,128]{3,2,1,0:T(8,128)S(1)}, f32[2,8,64,128]{3,2,1,0:T(8,128)}, u32[]{:S(2)}) copy-start(f32[2,8,64,128]{3,2,1,0:T(8,128)} %refs_9_.7) | copy-start | bytes 1572868
  28.6 0.9 copy-start.3
  29.6 0.8 copy-start.5
  34.5 20.4 %collective-permute-start.7 = (f32[2,2,64,128]{3,2,1,0:T(8,128)S(1)}, f32[2,2,64,128]{3,2,1,0:T(8,128)S(1)}, u32[]{:S(2)}, u32[]{:S(2)}) collective-permute-start(f32[2,2,64,128]{3,2,1,0:T(8,128)S(1)} %get-tuple-element.22), channel_id=1, source_target_pairs={{0,8},{24,16},{1,9},{25,17},{2,10},{26,18},{3,11},{27,19},{4,12},{... | collective-permute-start | bytes 393224 | tf_op jit(solution)/shard_map/ppermute | solution.py:162
  38.0 13.3 %copy-start.4 = (f32[2,4,64,128]{3,2,1,0:T(8,128)S(1)}, f32[2,4,64,128]{3,2,1,0:T(8,128)}, u32[]{:S(2)}) copy-start(f32[2,4,64,128]{3,2,1,0:T(8,128)} %sigma.1.refs_0_) | copy-start | bytes 786436
  38.0 13.3 %copy-start.6 = (s32[64,256]{1,0:T(8,128)S(1)}, s32[64,256]{1,0:T(8,128)}, u32[]{:S(2)}) copy-start(s32[64,256]{1,0:T(8,128)} %refs_10_.7) | copy-start | bytes 196612
  38.0 18.2 %collective-permute-start.11 = (f32[2,2,64,128]{3,2,1,0:T(8,128)S(1)}, f32[2,2,64,128]{3,2,1,0:T(8,128)S(1)}, u32[]{:S(2)}, u32[]{:S(2)}) collective-permute-start(f32[2,2,64,128]{3,2,1,0:T(8,128)S(1)} %get-tuple-element.24), channel_id=1, source_target_pairs={{0,8},{24,16},{1,9},{25,17},{2,10},{26,18},{3,11},{27,19},{4,12},{... | collective-permute-start | bytes 393224 | tf_op jit(solution)/shard_map/ppermute | solution.py:162
  43.0 0.7 copy-start.7
  43.7 13.9 %collective-permute-start.13 = (f32[2,2,64,128]{3,2,1,0:T(8,128)S(1)}, f32[2,2,64,128]{3,2,1,0:T(8,128)S(1)}, u32[]{:S(2)}, u32[]{:S(2)}) collective-permute-start(f32[2,2,64,128]{3,2,1,0:T(8,128)S(1)} %get-tuple-element.26), channel_id=1, source_target_pairs={{0,8},{24,16},{1,9},{25,17},{2,10},{26,18},{3,11},{27,19},{4,12},{... | collective-permute-start | bytes 393224 | tf_op jit(solution)/shard_map/ppermute | solution.py:162
  45.0 13.3 %collective-permute-start.17 = (f32[2,2,64,128]{3,2,1,0:T(8,128)S(1)}, f32[2,2,64,128]{3,2,1,0:T(8,128)S(1)}, u32[]{:S(2)}, u32[]{:S(2)}) collective-permute-start(f32[2,2,64,128]{3,2,1,0:T(8,128)S(1)} %get-tuple-element.28), channel_id=1, source_target_pairs={{0,8},{24,16},{1,9},{25,17},{2,10},{26,18},{3,11},{27,19},{4,12},{... | collective-permute-start | bytes 393224 | tf_op jit(solution)/shard_map/ppermute | solution.py:162
  49.9 50.5 %copy-start.2 = (f32[2,8,64,128]{3,2,1,0:T(8,128)S(1)}, f32[2,8,64,128]{3,2,1,0:T(8,128)}, u32[]{:S(2)}) copy-start(f32[2,8,64,128]{3,2,1,0:T(8,128)} %refs_9_.7) | copy-start | bytes 1572868
  49.9 12.5 %collective-permute-start.19 = (f32[2,2,64,128]{3,2,1,0:T(8,128)S(1)}, f32[2,2,64,128]{3,2,1,0:T(8,128)S(1)}, u32[]{:S(2)}, u32[]{:S(2)}) collective-permute-start(f32[2,2,64,128]{3,2,1,0:T(8,128)S(1)} %get-tuple-element.30), channel_id=1, source_target_pairs={{0,8},{24,16},{1,9},{25,17},{2,10},{26,18},{3,11},{27,19},{4,12},{... | collective-permute-start | bytes 393224 | tf_op jit(solution)/shard_map/ppermute | solution.py:162
  54.9 8.2 %collective-permute-start.25 = (f32[2,2,64,128]{3,2,1,0:T(8,128)S(1)}, f32[2,2,64,128]{3,2,1,0:T(8,128)S(1)}, u32[]{:S(2)}, u32[]{:S(2)}) collective-permute-start(f32[2,2,64,128]{3,2,1,0:T(8,128)S(1)} %get-tuple-element.34), channel_id=1, source_target_pairs={{0,8},{24,16},{1,9},{25,17},{2,10},{26,18},{3,11},{27,19},{4,12},{... | collective-permute-start | bytes 393224 | tf_op jit(solution)/shard_map/ppermute | solution.py:162
  56.2 7.6 %collective-permute-start.23 = (f32[2,2,64,128]{3,2,1,0:T(8,128)S(1)}, f32[2,2,64,128]{3,2,1,0:T(8,128)S(1)}, u32[]{:S(2)}, u32[]{:S(2)}) collective-permute-start(f32[2,2,64,128]{3,2,1,0:T(8,128)S(1)} %get-tuple-element.32), channel_id=1, source_target_pairs={{0,8},{24,16},{1,9},{25,17},{2,10},{26,18},{3,11},{27,19},{4,12},{... | collective-permute-start | bytes 393224 | tf_op jit(solution)/shard_map/ppermute | solution.py:162
  57.6 7.0 %collective-permute-start.8 = (f32[2,2,64,128]{3,2,1,0:T(8,128)S(1)}, f32[2,2,64,128]{3,2,1,0:T(8,128)S(1)}, u32[]{:S(2)}, u32[]{:S(2)}) collective-permute-start(f32[2,2,64,128]{3,2,1,0:T(8,128)S(1)} %add.84), channel_id=1, source_target_pairs={{8,16},{16,8},{9,17},{17,9},{10,18},{18,10},{11,19},{19,11},{12,20... | collective-permute-start | bytes 393224 | tf_op jit(solution)/shard_map/ppermute | solution.py:163
  58.3 13.8 %copy-start.8 = (f32[2,2,64,128]{3,2,1,0:T(8,128)}, f32[2,2,64,128]{3,2,1,0:T(8,128)S(1)}, u32[]{:S(2)}) copy-start(f32[2,2,64,128]{3,2,1,0:T(8,128)S(1)} %collective-permute-done.17) | copy-start | bytes 393220
  58.3 13.8 %collective-permute-start.29 = (f32[2,2,64,128]{3,2,1,0:T(8,128)S(1)}, f32[2,2,64,128]{3,2,1,0:T(8,128)S(1)}, u32[]{:S(2)}, u32[]{:S(2)}) collective-permute-start(f32[2,2,64,128]{3,2,1,0:T(8,128)S(1)} %get-tuple-element.36), channel_id=1, source_target_pairs={{0,8},{24,16},{1,9},{25,17},{2,10},{26,18},{3,11},{27,19},{4,12},{... | collective-permute-start | bytes 393224 | tf_op jit(solution)/shard_map/ppermute | solution.py:162
  62.4 10.3 %collective-permute-start.14 = (f32[2,2,64,128]{3,2,1,0:T(8,128)S(1)}, f32[2,2,64,128]{3,2,1,0:T(8,128)S(1)}, u32[]{:S(2)}, u32[]{:S(2)}) collective-permute-start(f32[2,2,64,128]{3,2,1,0:T(8,128)S(1)} %add.90), channel_id=1, source_target_pairs={{8,16},{16,8},{9,17},{17,9},{10,18},{18,10},{11,19},{19,11},{12,20... | collective-permute-start | bytes 393224 | tf_op jit(solution)/shard_map/ppermute | solution.py:163
  63.1 12.0 %collective-permute-start.20 = (f32[2,2,64,128]{3,2,1,0:T(8,128)S(1)}, f32[2,2,64,128]{3,2,1,0:T(8,128)S(1)}, u32[]{:S(2)}, u32[]{:S(2)}) collective-permute-start(f32[2,2,64,128]{3,2,1,0:T(8,128)S(1)} %add.96), channel_id=1, source_target_pairs={{8,16},{16,8},{9,17},{17,9},{10,18},{18,10},{11,19},{19,11},{12,20... | collective-permute-start | bytes 393224 | tf_op jit(solution)/shard_map/ppermute | solution.py:163
  63.8 15.8 %collective-permute-start.26 = (f32[2,2,64,128]{3,2,1,0:T(8,128)S(1)}, f32[2,2,64,128]{3,2,1,0:T(8,128)S(1)}, u32[]{:S(2)}, u32[]{:S(2)}) collective-permute-start(f32[2,2,64,128]{3,2,1,0:T(8,128)S(1)} %add.102), channel_id=1, source_target_pairs={{8,16},{16,8},{9,17},{17,9},{10,18},{18,10},{11,19},{19,11},{12,20... | collective-permute-start | bytes 393224 | tf_op jit(solution)/shard_map/ppermute | solution.py:163
  64.5 16.5 %collective-permute-start.10 = (f32[2,2,64,128]{3,2,1,0:T(8,128)}, f32[2,2,64,128]{3,2,1,0:T(8,128)S(1)}, u32[]{:S(2)}, u32[]{:S(2)}) collective-permute-start(f32[2,2,64,128]{3,2,1,0:T(8,128)} %get-tuple-element.23), channel_id=1, source_target_pairs={{0,8},{24,16},{1,9},{25,17},{2,10},{26,18},{3,11},{27,19},{4,12},{... | collective-permute-start | bytes 393224 | tf_op jit(solution)/shard_map/ppermute | solution.py:162
  72.1 10.3 %collective-permute-start.12 = (f32[2,2,64,128]{3,2,1,0:T(8,128)S(1)}, f32[2,2,64,128]{3,2,1,0:T(8,128)S(1)}, u32[]{:S(2)}, u32[]{:S(2)}) collective-permute-start(f32[2,2,64,128]{3,2,1,0:T(8,128)S(1)} %add.88), channel_id=1, source_target_pairs={{8,16},{16,8},{9,17},{17,9},{10,18},{18,10},{11,19},{19,11},{12,20... | collective-permute-start | bytes 393224 | tf_op jit(solution)/shard_map/ppermute | solution.py:163
  72.8 10.3 %collective-permute-start.9 = (f32[2,2,64,128]{3,2,1,0:T(8,128)S(1)}, f32[2,2,64,128]{3,2,1,0:T(8,128)S(1)}, u32[]{:S(2)}, u32[]{:S(2)}) collective-permute-start(f32[2,2,64,128]{3,2,1,0:T(8,128)S(1)} %add.85), channel_id=1, source_target_pairs={{16,24},{8,0},{17,25},{9,1},{18,26},{10,2},{19,27},{11,3},{20,28},... | collective-permute-start | bytes 393224 | tf_op jit(solution)/shard_map/ppermute | solution.py:164
  75.1 10.2 %collective-permute-start.16 = (f32[2,2,64,128]{3,2,1,0:T(8,128)}, f32[2,2,64,128]{3,2,1,0:T(8,128)S(1)}, u32[]{:S(2)}, u32[]{:S(2)}) collective-permute-start(f32[2,2,64,128]{3,2,1,0:T(8,128)} %copy-done.7), channel_id=1, source_target_pairs={{0,8},{24,16},{1,9},{25,17},{2,10},{26,18},{3,11},{27,19},{4,12},{... | collective-permute-start | bytes 393224 | tf_op jit(solution)/shard_map/ppermute | solution.py:162
  79.7 12.4 %collective-permute-start.22 = (f32[2,2,64,128]{3,2,1,0:T(8,128)S(1)}, f32[2,2,64,128]{3,2,1,0:T(8,128)S(1)}, u32[]{:S(2)}, u32[]{:S(2)}) collective-permute-start(f32[2,2,64,128]{3,2,1,0:T(8,128)S(1)} %get-tuple-element.31), channel_id=1, source_target_pairs={{0,8},{24,16},{1,9},{25,17},{2,10},{26,18},{3,11},{27,19},{4,12},{... | collective-permute-start | bytes 393224 | tf_op jit(solution)/shard_map/ppermute | solution.py:162
  81.0 17.4 %collective-permute-start.28 = (f32[2,2,64,128]{3,2,1,0:T(8,128)S(1)}, f32[2,2,64,128]{3,2,1,0:T(8,128)S(1)}, u32[]{:S(2)}, u32[]{:S(2)}) collective-permute-start(f32[2,2,64,128]{3,2,1,0:T(8,128)S(1)} %get-tuple-element.35), channel_id=1, source_target_pairs={{0,8},{24,16},{1,9},{25,17},{2,10},{26,18},{3,11},{27,19},{4,12},{... | collective-permute-start | bytes 393224 | tf_op jit(solution)/shard_map/ppermute | solution.py:162
  82.3 3.6 %collective-permute-start.18 = (f32[2,2,64,128]{3,2,1,0:T(8,128)S(1)}, f32[2,2,64,128]{3,2,1,0:T(8,128)S(1)}, u32[]{:S(2)}, u32[]{:S(2)}) collective-permute-start(f32[2,2,64,128]{3,2,1,0:T(8,128)S(1)} %add.94), channel_id=1, source_target_pairs={{8,16},{16,8},{9,17},{17,9},{10,18},{18,10},{11,19},{19,11},{12,20... | collective-permute-start | bytes 393224 | tf_op jit(solution)/shard_map/ppermute | solution.py:163
  83.0 6.9 %collective-permute-start.15 = (f32[2,2,64,128]{3,2,1,0:T(8,128)S(1)}, f32[2,2,64,128]{3,2,1,0:T(8,128)S(1)}, u32[]{:S(2)}, u32[]{:S(2)}) collective-permute-start(f32[2,2,64,128]{3,2,1,0:T(8,128)S(1)} %add.91), channel_id=1, source_target_pairs={{16,24},{8,0},{17,25},{9,1},{18,26},{10,2},{19,27},{11,3},{20,28},... | collective-permute-start | bytes 393224 | tf_op jit(solution)/shard_map/ppermute | solution.py:164
  85.3 8.2 %collective-permute-start.24 = (f32[2,2,64,128]{3,2,1,0:T(8,128)S(1)}, f32[2,2,64,128]{3,2,1,0:T(8,128)S(1)}, u32[]{:S(2)}, u32[]{:S(2)}) collective-permute-start(f32[2,2,64,128]{3,2,1,0:T(8,128)S(1)} %add.100), channel_id=1, source_target_pairs={{8,16},{16,8},{9,17},{17,9},{10,18},{18,10},{11,19},{19,11},{12,20... | collective-permute-start | bytes 393224 | tf_op jit(solution)/shard_map/ppermute | solution.py:163
  86.0 12.4 %collective-permute-start.30 = (f32[2,2,64,128]{3,2,1,0:T(8,128)S(1)}, f32[2,2,64,128]{3,2,1,0:T(8,128)S(1)}, u32[]{:S(2)}, u32[]{:S(2)}) collective-permute-start(f32[2,2,64,128]{3,2,1,0:T(8,128)S(1)} %add.106), channel_id=1, source_target_pairs={{8,16},{16,8},{9,17},{17,9},{10,18},{18,10},{11,19},{19,11},{12,20... | collective-permute-start | bytes 393224 | tf_op jit(solution)/shard_map/ppermute | solution.py:163
  89.9 8.5 %collective-permute-start.21 = (f32[2,2,64,128]{3,2,1,0:T(8,128)S(1)}, f32[2,2,64,128]{3,2,1,0:T(8,128)S(1)}, u32[]{:S(2)}, u32[]{:S(2)}) collective-permute-start(f32[2,2,64,128]{3,2,1,0:T(8,128)S(1)} %add.97), channel_id=1, source_target_pairs={{16,24},{8,0},{17,25},{9,1},{18,26},{10,2},{19,27},{11,3},{20,28},... | collective-permute-start | bytes 393224 | tf_op jit(solution)/shard_map/ppermute | solution.py:164
  92.1 8.2 %collective-permute-start.27 = (f32[2,2,64,128]{3,2,1,0:T(8,128)S(1)}, f32[2,2,64,128]{3,2,1,0:T(8,128)S(1)}, u32[]{:S(2)}, u32[]{:S(2)}) collective-permute-start(f32[2,2,64,128]{3,2,1,0:T(8,128)S(1)} %add.103), channel_id=1, source_target_pairs={{16,24},{8,0},{17,25},{9,1},{18,26},{10,2},{19,27},{11,3},{20,28},... | collective-permute-start | bytes 393224 | tf_op jit(solution)/shard_map/ppermute | solution.py:164

commit v2 on v0

v2 whole, which is shorter than its diff:
```python
import functools

import jax
import jax.numpy as jnp
from jax import lax
from jax.experimental import pallas as pl
from jax.experimental.pallas import tpu as pltpu
from jax.sharding import PartitionSpec as P

coupling_square = 0.25
hopping = 4.0
time_step = 0.01
CHUNKS = 4
VMEM = pl.BlockSpec(memory_space=pltpu.VMEM)
SMEM = pl.BlockSpec(memory_space=pltpu.SMEM)
HBM = pl.BlockSpec(memory_space=pltpu.HBM)


def sigma_kernel(hist_ref, table_ref, step_ref, lesser_hbm, greater_hbm, out_ref, lesser, greater, sems):
    slices = lesser.shape[1]
    copies = [
        pltpu.make_async_copy(lesser_hbm, lesser, sems.at[0]),
        pltpu.make_async_copy(greater_hbm, greater, sems.at[1]),
    ]
    for copy in copies:
        copy.start()
    for copy in copies:
        copy.wait()
    for s in range(slices):
        numerator = jnp.full((1, lesser.shape[3]), table_ref[s], jnp.int32).astype(jnp.float32)
        weight = jnp.where(hist_ref[0] * slices + s <= step_ref[0], numerator / 24.0, 0.0)
        a_re, a_im = lesser[0, s], lesser[1, s]
        b_re, b_im = greater[0, s], greater[1, s]
        square_re = a_re * a_re - a_im * a_im
        square_im = 2.0 * a_re * a_im
        scale = coupling_square * weight
        out_ref[0, s] = scale * (square_re * b_re - square_im * b_im)
        out_ref[1, s] = scale * (square_re * b_im + square_im * b_re)


def split(x):
    high = x.astype(jnp.bfloat16)
    return high, (x - high.astype(jnp.float32)).astype(jnp.bfloat16)


def history_kernel(
    advanced_hbm, row_hbm, adjacency_hbm, high_ref, low_ref, hop_ref, row, advanced, adjacency, sems
):
    slices, width = advanced.shape[2], advanced.shape[4]
    times = row.shape[1]
    each = times // high_ref.shape[0]

    def fetch(t):
        return pltpu.make_async_copy(advanced_hbm.at[:, :, t], advanced.at[t % 2], sems.at[t % 2])

    small = [
        pltpu.make_async_copy(row_hbm, row, sems.at[2]),
        pltpu.make_async_copy(adjacency_hbm, adjacency, sems.at[3]),
    ]
    for copy in small:
        copy.start()
    fetch(0).start()
    fetch(1).start()
    for copy in small:
        copy.wait()
    graph = (-hopping * adjacency[...].astype(jnp.float32)).T.astype(jnp.bfloat16)
    for t in range(times):
        chunk, place = t // each, (t % each) * 2 * width
        row_high, row_low = split(jnp.concatenate([row[0, t], row[1, t]], axis=1))
        hop_ref[chunk, :, place : place + 2 * width] = jnp.dot(
            graph, row_high, preferred_element_type=jnp.float32
        ) + jnp.dot(graph, row_low, preferred_element_type=jnp.float32)
        fetch(t).wait()
        for s in range(slices):
            for part in range(2):
                high, low = split(advanced[t % 2, part, s])
                high_ref[chunk, s, :, place + part * width : place + (part + 1) * width] = high
                low_ref[chunk, s, :, place + part * width : place + (part + 1) * width] = low
        if t + 2 < times:
            fetch(t + 2).start()


def assemble(masks, my_orow, my_ocol, blocks, left_high, left_low):
    for (flip_orow, flip_ocol), block in zip(masks, blocks):
        at_orow = jnp.bitwise_xor(my_orow, flip_orow)
        at_ocol = jnp.bitwise_xor(my_ocol, flip_ocol)
        for s in range(left_high.shape[0]):
            for part in range(2):
                high, low = split(block[part, s])
                left_high[s, at_orow, part, at_ocol] = high
                left_low[s, at_orow, part, at_ocol] = low


def chunk_kernel(chunk, masks, ring, hist_ref, orow_ref, ocol_ref, right_high, right_low, hop_ref, *refs):
    if masks:
        blocks, refs = refs[: len(masks)], refs[len(masks) :]
        left_high, left_low, outs, result = refs[-3], refs[-2], refs[:-3], refs[-1]
        assemble(masks, orow_ref[0], ocol_ref[0], blocks, left_high, left_low)
    else:
        left_high, left_low, outs, result = refs[0], refs[1], refs[2:-1], refs[-1]
    slices, halves = left_high.shape[:2]
    norb = right_high.shape[2]
    width = outs[0].shape[3]

    def left(ref, s):
        return jnp.concatenate([ref[s, half].reshape(2 * norb, norb // halves) for half in range(halves)], axis=1)

    total = None
    for s in range(slices):
        high = right_high[chunk, s]
        here = jnp.dot(
            jnp.concatenate([left(left_high, s), left(left_high, s), left(left_low, s)], axis=1),
            jnp.concatenate([high, right_low[chunk, s], high], axis=0),
            preferred_element_type=jnp.float32,
        )
        total = here if total is None else total + here
    for t in range(outs[0].shape[1]):
        at = 2 * width * t
        sum_re = total[:norb, at : at + width] - total[norb:, at + width : at + 2 * width] + hop_ref[chunk, :, at : at + width]
        sum_im = total[:norb, at + width : at + 2 * width] + total[norb:, at : at + width] + hop_ref[chunk, :, at + width : at + 2 * width]
        if not ring:
            outs[0][0, t] = sum_re
            outs[0][1, t] = sum_im
            continue
        rows = norb // len(ring)
        for block in range(len(ring)):
            result[t, block, 0] = sum_re[block * rows : (block + 1) * rows]
            result[t, block, 1] = sum_im[block * rows : (block + 1) * rows]
    if not ring:
        return
    size = len(ring)
    my_hist = hist_ref[0]
    my_place = sum(jnp.where(my_hist == h, ring.index(h), 0) for h in range(size))
    for step, out in enumerate(outs):
        place = my_place + (size - 1 - step)
        place = jnp.where(place >= size, place - size, place)
        block = sum(jnp.where(place == p, ring[p], 0) for p in range(size))
        for t in range(out.shape[1]):
            out[0, t] = result[t, block, 0]
            out[1, t] = result[t, block, 1]


def step_kernel(*refs):
    chunks = (len(refs) - 4) // 2
    arrived, own = refs[:chunks], refs[chunks : 2 * chunks]
    row, out_hbm, out, sems = refs[2 * chunks :]
    each = own[0].shape[1]
    copies = []
    for chunk in range(chunks):
        here = pl.ds(chunk * each, each)
        summed_re = arrived[chunk][0] + own[chunk][0]
        summed_im = arrived[chunk][1] + own[chunk][1]
        out[0, here] = row[0, here] + time_step * summed_im
        out[1, here] = row[1, here] - time_step * summed_re
        copies.append(pltpu.make_async_copy(out.at[:, here], out_hbm.at[:, here], sems.at[chunk]))
        copies[-1].start()
    for copy in copies:
        copy.wait()


def ring_of(size):
    return [place for place in range(size) if place == 0 or place % 2 == 1] + [
        place for place in range(size - 1, 0, -1) if place % 2 == 0
    ]


def limit(mebibytes):
    return pltpu.CompilerParams(vmem_limit_bytes=mebibytes * 1024 * 1024)


def in_vmem(x):
    return pltpu.with_memory_space_constraint(x, pltpu.VMEM)


def in_hbm(x):
    return pltpu.with_memory_space_constraint(x, pltpu.HBM)


def on_device(
    hist_size, orow_size, ocol_size, lesser_hist, greater_hist, advanced_hist, current_row, adjacency, weight_table, step_index
):
    slices, times, norb, width = advanced_hist.shape[1:]
    block = lesser_hist.shape
    my_hist, my_orow, my_ocol = lax.axis_index("hist"), lax.axis_index("orow"), lax.axis_index("ocol")
    me = [index.reshape(1).astype(jnp.int32) for index in (my_hist, my_orow, my_ocol)]
    sigma = pl.pallas_call(
        sigma_kernel,
        out_shape=pltpu.VMEM(block, jnp.float32),
        in_specs=[SMEM, SMEM, SMEM, HBM, HBM],
        out_specs=VMEM,
        scratch_shapes=[
            pltpu.VMEM(block, jnp.float32),
            pltpu.VMEM(block, jnp.float32),
            pltpu.SemaphoreType.DMA((2,)),
        ],
        compiler_params=limit(4),
        name="sigma",
    )(me[0], weight_table, step_index, in_hbm(lesser_hist), in_hbm(jnp.swapaxes(greater_hist, 2, 3)))

    each = times // CHUNKS
    right_high, right_low, hop, row = pl.pallas_call(
        history_kernel,
        out_shape=[
            pltpu.VMEM((CHUNKS, slices, norb, each * 2 * width), jnp.bfloat16),
            pltpu.VMEM((CHUNKS, slices, norb, each * 2 * width), jnp.bfloat16),
            pltpu.VMEM((CHUNKS, norb, each * 2 * width), jnp.float32),
            pltpu.VMEM(current_row.shape, jnp.float32),
        ],
        in_specs=[HBM, HBM, HBM],
        out_specs=[VMEM] * 4,
        scratch_shapes=[
            pltpu.VMEM((2, 2, slices, norb, width), jnp.float32),
            pltpu.VMEM(adjacency.shape, jnp.int32),
            pltpu.SemaphoreType.DMA((4,)),
        ],
        cost_estimate=pl.CostEstimate(flops=0, bytes_accessed=16 * 1024 * 1024, transcendentals=0),
        compiler_params=limit(16),
        name="history",
    )(in_hbm(advanced_hist), in_hbm(current_row), in_hbm(adjacency))

    def moved(x, target):
        pairs = [
            (r * ocol_size + c, target(r, c)[0] * ocol_size + target(r, c)[1])
            for r in range(orow_size)
            for c in range(ocol_size)
        ]
        return lax.ppermute(x, ("orow", "ocol"), pairs)

    held = {(0, 0): sigma}
    held[(1, 0)] = moved(sigma, lambda r, c: (r ^ 1, c))
    held[(0, 2)] = moved(sigma, lambda r, c: (r, c ^ 2))
    held[(0, 1)] = moved(sigma, lambda r, c: (r, c ^ 1))
    over_orow, over_ocol, hop = lax.optimization_barrier((held[(1, 0)], held[(0, 2)], hop))
    passed_on = jnp.where(my_ocol % 2 == 0, over_orow, over_ocol)
    held[(1, 2)] = moved(passed_on, lambda r, c: (r, c ^ 2) if c % 2 == 0 else (r ^ 1, c))
    for r, c in ((1, 0), (0, 2), (1, 2)):
        held[(r, c + 1)] = moved(held[(r, c)], lambda r, c: (r, c ^ 1))
    masks = tuple(held)

    rows = norb // hist_size
    ring = ring_of(hist_size) if hist_size <= 8 else []
    left_shape = (slices, orow_size, 2, ocol_size) + block[2:]
    left = None
    arrived, own, first_come = [], [], []
    for chunk in range(CHUNKS):
        if ring:
            out_shape = [pltpu.VMEM((2, each, rows, width), jnp.float32)] * hist_size
        else:
            out_shape = [pltpu.VMEM((2, each, norb, width), jnp.float32)]
        after = me
        if chunk >= 2 and ring:
            after = me[:2] + [lax.optimization_barrier((me[2], first_come[chunk - 2]))[0]]
        if left is None:
            operands, extra = [in_vmem(held[mask]) for mask in masks], [pltpu.VMEM(left_shape, jnp.bfloat16)] * 2
        else:
            operands, extra = [in_vmem(x) for x in left], []
        parts = pl.pallas_call(
            functools.partial(chunk_kernel, chunk, masks if left is None else (), ring),
            out_shape=out_shape + extra,
            in_specs=[SMEM] * 3 + [VMEM] * (3 + len(operands)),
            out_specs=[VMEM] * (len(out_shape) + len(extra)),
            scratch_shapes=[pltpu.VMEM((each, hist_size, 2, rows, width), jnp.float32)],
            cost_estimate=pl.CostEstimate(
                flops=6 * each * slices * 2 * norb * norb * 2 * width, bytes_accessed=0, transcendentals=0
            ),
            compiler_params=limit(16),
            name=f"products_{chunk}",
        )(*after, in_vmem(right_high), in_vmem(right_low), in_vmem(hop), *operands)
        if left is None:
            left, parts = parts[-2:], parts[:-2]
        if not ring:
            total = lax.psum_scatter(parts[0], "hist", scatter_dimension=2, tiled=True)
            arrived.append(total)
            own.append(jnp.zeros_like(total))
            continue
        pairs = [(ring[p], ring[(p + 1) % hist_size]) for p in range(hist_size)]
        moving = parts[0]
        for m in range(1, hist_size):
            moving = lax.ppermute(moving, "hist", pairs)
            if m == 1:
                first_come.append(moving)
            if m < hist_size - 1:
                moving = moving + parts[m]
        arrived.append(moving)
        own.append(parts[-1])
    return pl.pallas_call(
        step_kernel,
        out_shape=jax.ShapeDtypeStruct(current_row.shape, jnp.float32),
        in_specs=[VMEM] * (2 * CHUNKS + 1),
        out_specs=HBM,
        scratch_shapes=[pltpu.VMEM(current_row.shape, jnp.float32), pltpu.SemaphoreType.DMA((CHUNKS,))],
        compiler_params=limit(4),
        name="step",
    )(*[in_vmem(x) for x in arrived], *[in_vmem(x) for x in own], in_vmem(row))


def solution(mesh):
    in_specs = (
        P(None, "hist", "ocol", "orow"),
        P(None, "hist", "orow", "ocol"),
        P(None, "hist", "ocol", None, "orow"),
        P(None, "ocol", "hist", "orow"),
        P("hist", None),
        P("hist"),
        P(),
    )
    out_specs = P(None, "ocol", "hist", "orow")
    body = functools.partial(on_device, mesh.shape["hist"], mesh.shape["orow"], mesh.shape["ocol"])
    return jax.shard_map(
        body, mesh=mesh, in_specs=in_specs, out_specs=out_specs, check_vma=False
    )
```

time: 219 us -> 76 us (0.35)
  waiting for transfers between devices: 180 us -> 20.7 us
  starting transfers between devices: 0.19 us -> 26.6 us
  matrix products: 19 us -> 0 us
  Pallas kernels: 0 us -> 18.3 us
  between operations: 14.2 us -> 0.77 us
  local copies, waits for them, and re-layouts: 0.01 us -> 8.99 us
  other arithmetic: 5.2 us -> 0.18 us
    all_gather x5 -> x0, waiting for transfers between devices: 133 us -> none  [the longest x1 34.5 us: on_device(): lax.all_gather(greater_full, 'orow', axis=2, tiled=True)]
    reduce_scatter x1 -> x0, waiting for transfers between devices: 44.7 us -> none  [on_device(): lax.psum_scatter(collision, 'hist', scatter_dimension=2, tiled=True)]
    ppermute x0 -> x19, starting transfers between devices: none -> 26.6 us  [the longest x12 21 us: on_device(): moving = lax.ppermute(moving, 'hist', pairs)]
    ppermute x0 -> x19, waiting for transfers between devices: none -> 20.7 us  [the longest x12 13.4 us: on_device(): moving = lax.ppermute(moving, 'hist', pairs)]
    dot_general x2 -> x0, matrix products: 19 us -> none  [the longest x1 16 us: on_device(): jnp.einsum('csik,dstkj->cdtij', sigma_w, advanced_hist, precision=lax.Pre...]
    pallas_call x0 -> x7, Pallas kernels: none -> 18.3 us  [the longest x4 8.87 us: on_device(): pl.pallas_call(functools.partial(chunk_kernel, chunk, masks if left is No...]
    unnamed x6 -> x10, local copies, waits for them, and re-layouts: 0.01 us -> 8.99 us
    mul x1 -> x0, other arithmetic: 2.61 us -> none  [self_energy(): coupling_square * (square_re * greater_re - square_im * greater_im)]
  transfers between devices with their start and end apart: 6 -> 19, of which waited for: 6 -> 12; matrix products, arithmetic and copies ran while one was open for 9% -> 0% of each run, Pallas kernels for 0% -> 17%
where the time goes in v2:
time: 76 us; the launch traced here: 75.6 us
  starting transfers between devices  26.6 us (35%)
  waiting for transfers between devices  20.7 us (27%)
  Pallas kernels  18.3 us (24%)
  local copies, waits for them, and re-layouts  8.99 us (12%)
  between operations  0.77 us (1%)
    ppermute x12, starting transfers between devices, on_device(): moving = lax.ppermute(moving, 'hist', pairs)  21 us
    ppermute x12, waiting for transfers between devices, on_device(): moving = lax.ppermute(moving, 'hist', pairs)  13.4 us
    unnamed x10, local copies, waits for them, and re-layouts  8.99 us
    pallas_call x4, Pallas kernels, on_device(): pl.pallas_call(functools.partial(chunk_kernel, chunk, masks if left is No...  8.87 us
    ppermute x7, waiting for transfers between devices, moved(): return lax.ppermute(x, ('orow', 'ocol'), pairs)  7.32 us
    pallas_call x1, Pallas kernels, on_device(): pl.pallas_call(history_kernel, out_shape=[pltpu.VMEM((CHUNKS, slices, nor...  6.96 us
    ppermute x7, starting transfers between devices, moved(): return lax.ppermute(x, ('orow', 'ocol'), pairs)  5.61 us
    pallas_call x1, Pallas kernels, on_device(): pl.pallas_call(sigma_kernel, out_shape=pltpu.VMEM(block, jnp.float32), in...  1.65 us
  transfers between devices with their start and end apart: 19, of which 12 were waited for; matrix products, arithmetic and copies ran while one was open for 0% of the time, Pallas kernels for 17%

profile of v2, /device:TPU:0, one launch (start us, length us, event | category | flops | bytes accessed | tf_op | source)
XLA Modules:
  0.0 75.6 jit_solution(4589193014104065501)
XLA Ops:
  0.7 0.6 copy-done.4
  1.3 1.6 %sigma.1.refs_0_ = f32[2,4,64,128]{3,2,1,0:T(8,128)S(1)} custom-call(s32[1]{0:T(128)} %bitcast.hist_ref, s32[4]{0:T(128)S(1)} %copy-done.4, s32[1]{0:T(128)S(6)} %copy.8.step_ref, f32[2,4,64,128]{3,2,1,0:T(8,128)} %lesser_hbm.1, f32[2,4,64,128]{3,2,1,0:T(8,128)} %bitcast.4), custom_call_target="tpu_custom_call" | custom-call | tf_op jit(solution)/shard_map/sigma/pallas_call | solution.py:186
  3.0 3.0 %collective-permute-start.1 = (f32[2,4,64,128]{3,2,1,0:T(8,128)S(1)}, f32[2,4,64,128]{3,2,1,0:T(8,128)S(1)}, u32[]{:S(2)}, u32[]{:S(2)}) collective-permute-start(f32[2,4,64,128]{3,2,1,0:T(8,128)S(1)} %sigma.1.refs_0_), channel_id=1, source_target_pairs={{0,2},{1,3},{2,0},{3,1},{4,6},{5,7},{6,4},{7,5},{8,10},{9,11},{10,... | collective-permute-start | bytes 786440 | tf_op jit(solution)/shard_map/ppermute | solution.py:227
  6.0 1.5 %collective-permute-start = (f32[2,4,64,128]{3,2,1,0:T(8,128)S(1)}, f32[2,4,64,128]{3,2,1,0:T(8,128)S(1)}, u32[]{:S(2)}, u32[]{:S(2)}) collective-permute-start(f32[2,4,64,128]{3,2,1,0:T(8,128)S(1)} %sigma.1.refs_0_), channel_id=1, source_target_pairs={{0,4},{1,5},{2,6},{3,7},{4,0},{5,1},{6,2},{7,3},{8,12},{9,13},{10,... | collective-permute-start | bytes 786440 | tf_op jit(solution)/shard_map/ppermute | solution.py:227
  7.5 7.0 %history.1 = (bf16[4,4,256,512]{3,2,1,0:T(8,128)(2,1)S(1)}, bf16[4,4,256,512]{3,2,1,0:T(8,128)(2,1)S(1)}, f32[4,256,512]{2,1,0:T(8,128)S(1)}, f32[2,8,64,128]{3,2,1,0:T(8,128)S(1)}) custom-call(f32[2,4,8,256,128]{4,3,2,1,0:T(8,128)} %advanced_hbm.1, f32[2,8,64,128]{3,2,1,0:T(8,128)} %row_hbm.1, s32[64,256]{1,0:T(8,128)} %adjacency_hbm.1), custom_call_target="tpu_custom_call" | custom-call | bytes 16777216 | tf_op jit(solution)/shard_map/history/pallas_call | solution.py:201
  14.5 1.9 %copy-done = bf16[4,4,256,512]{3,2,1,0:T(8,128)(2,1)} copy-done((bf16[4,4,256,512]{3,2,1,0:T(8,128)(2,1)}, bf16[4,4,256,512]{3,2,1,0:T(8,128)(2,1)S(1)}, u32[]{:S(2)}) %copy-start) | copy-done | bytes 4194328
  16.4 2.0 %copy-done.2 = bf16[4,4,256,512]{3,2,1,0:T(8,128)(2,1)} copy-done((bf16[4,4,256,512]{3,2,1,0:T(8,128)(2,1)}, bf16[4,4,256,512]{3,2,1,0:T(8,128)(2,1)S(1)}, u32[]{:S(2)}) %copy-start.2) | copy-done | bytes 4194328
  18.4 0.0 collective-permute-done.1.refs_2_
  18.4 0.0 collective-permute-done.refs_1_
  18.5 0.6 collective-permute-start.3
  19.0 0.0 collective-permute-start.2
  19.0 0.5 collective-permute-start.5
  19.6 0.0 collective-permute-start.4
  19.6 5.5 %collective-permute-done.3.refs_4_ = f32[2,4,64,128]{3,2,1,0:T(8,128)} collective-permute-done((f32[2,4,64,128]{3,2,1,0:T(8,128)S(1)}, f32[2,4,64,128]{3,2,1,0:T(8,128)}, u32[]{:S(2)}, u32[]{:S(2)}) %collective-permute-start.3) | collective-permute-done | bytes 262176 | tf_op jit(solution)/shard_map/ppermute | solution.py:227
  25.0 0.0 collective-permute-start.6
  25.0 0.0 collective-permute-done.2.refs_3_
  25.0 0.0 collective-permute-done.4.refs_5_
  25.0 1.9 %collective-permute-done.6.refs_7_ = f32[2,4,64,128]{3,2,1,0:T(8,128)} collective-permute-done((f32[2,4,64,128]{3,2,1,0:T(8,128)}, f32[2,4,64,128]{3,2,1,0:T(8,128)}, u32[]{:S(2)}, u32[]{:S(2)}) %collective-permute-start.6) | collective-permute-done | bytes 262176 | tf_op jit(solution)/shard_map/ppermute | solution.py:227
  26.9 2.2 %copy-done.1 = bf16[4,4,256,512]{3,2,1,0:T(8,128)(2,1)S(1)} copy-done((bf16[4,4,256,512]{3,2,1,0:T(8,128)(2,1)S(1)}, bf16[4,4,256,512]{3,2,1,0:T(8,128)(2,1)}, u32[]{:S(2)}) %copy-start.1) | copy-done | bytes 4194328
  29.1 2.2 %copy-done.3 = bf16[4,4,256,512]{3,2,1,0:T(8,128)(2,1)S(1)} copy-done((bf16[4,4,256,512]{3,2,1,0:T(8,128)(2,1)S(1)}, bf16[4,4,256,512]{3,2,1,0:T(8,128)(2,1)}, u32[]{:S(2)}) %copy-start.3) | copy-done | bytes 4194328
  31.3 3.3 %products_0.1 = (f32[2,2,64,128]{3,2,1,0:T(8,128)S(1)}, f32[2,2,64,128]{3,2,1,0:T(8,128)S(1)}, f32[2,2,64,128]{3,2,1,0:T(8,128)S(1)}, f32[2,2,64,128]{3,2,1,0:T(...) custom-call(s32[1]{0:T(128)} %bitcast.hist_ref, s32[1]{0:T(128)} %bitcast.1.orow_ref, ...), custom_call_target="tpu_custom_call" | custom-call | flops 1610612736 | tf_op jit(solution)/shard_map/products_0/pallas_call | solution.py:257
  34.6 1.6 %collective-permute-start.7 = (f32[2,2,64,128]{3,2,1,0:T(8,128)S(1)}, f32[2,2,64,128]{3,2,1,0:T(8,128)S(1)}, u32[]{:S(2)}, u32[]{:S(2)}) collective-permute-start(f32[2,2,64,128]{3,2,1,0:T(8,128)S(1)} %get-tuple-element.38), channel_id=1, source_target_pairs={{0,8},{8,24},{24,16},{16,0},{1,9},{9,25},{25,17},{17,1},{2,10},{10... | collective-permute-start | bytes 393224 | tf_op jit(solution)/shard_map/ppermute | solution.py:279
  36.2 1.8 %products_1.1 = (f32[2,2,64,128]{3,2,1,0:T(8,128)S(1)}, f32[2,2,64,128]{3,2,1,0:T(8,128)S(1)}, f32[2,2,64,128]{3,2,1,0:T(8,128)S(1)}, f32[2,2,64,128]{3,2,1,0:T(8,128)S(1)}) custom-call(s32[1]{0:T(128)} %bitcast.hist_ref, s32[1]{0:T(128)} %bitcast.1.orow_ref, s32[1]{0:T(128)} %bitcast.2.ocol_ref, bf16[4,4,256,512]{3,2,1,0:T(8,128)(2,1)S(1)} %copy-done.1, ...), custom_call_target="tpu_custom_call" | custom-call | flops 1610612736 | tf_op jit(solution)/shard_map/products_1/pallas_call | solution.py:257
  38.1 2.6 %collective-permute-start.10 = (f32[2,2,64,128]{3,2,1,0:T(8,128)S(1)}, f32[2,2,64,128]{3,2,1,0:T(8,128)S(1)}, u32[]{:S(2)}, u32[]{:S(2)}) collective-permute-start(f32[2,2,64,128]{3,2,1,0:T(8,128)S(1)} %get-tuple-element.43), channel_id=1, source_target_pairs={{0,8},{8,24},{24,16},{16,0},{1,9},{9,25},{25,17},{17,1},{2,10},{10... | collective-permute-start | bytes 393224 | tf_op jit(solution)/shard_map/ppermute | solution.py:279
  40.7 0.4 collective-permute-done.7
  41.1 1.8 %products_2.1 = (f32[2,2,64,128]{3,2,1,0:T(8,128)S(1)}, f32[2,2,64,128]{3,2,1,0:T(8,128)S(1)}, f32[2,2,64,128]{3,2,1,0:T(8,128)S(1)}, f32[2,2,64,128]{3,2,1,0:T(8,128)S(1)}) custom-call(s32[1]{0:T(128)} %bitcast.hist_ref, s32[1]{0:T(128)} %bitcast.1.orow_ref, s32[1]{0:T(128)} %bitcast.2.ocol_ref, bf16[4,4,256,512]{3,2,1,0:T(8,128)(2,1)S(1)} %copy-done.1, ...), custom_call_target="tpu_custom_call" | custom-call | flops 1610612736 | tf_op jit(solution)/shard_map/products_2/pallas_call | solution.py:257
  43.0 1.5 %collective-permute-start.13 = (f32[2,2,64,128]{3,2,1,0:T(8,128)S(1)}, f32[2,2,64,128]{3,2,1,0:T(8,128)S(1)}, u32[]{:S(2)}, u32[]{:S(2)}) collective-permute-start(f32[2,2,64,128]{3,2,1,0:T(8,128)S(1)} %get-tuple-element.47), channel_id=1, source_target_pairs={{0,8},{8,24},{24,16},{16,0},{1,9},{9,25},{25,17},{17,1},{2,10},{10... | collective-permute-start | bytes 393224 | tf_op jit(solution)/shard_map/ppermute | solution.py:279
  44.5 0.0 collective-permute-done.10
  44.5 1.8 %products_3.1 = (f32[2,2,64,128]{3,2,1,0:T(8,128)S(1)}, f32[2,2,64,128]{3,2,1,0:T(8,128)S(1)}, f32[2,2,64,128]{3,2,1,0:T(8,128)S(1)}, f32[2,2,64,128]{3,2,1,0:T(8,128)S(1)}) custom-call(s32[1]{0:T(128)} %bitcast.hist_ref, s32[1]{0:T(128)} %bitcast.1.orow_ref, s32[1]{0:T(128)} %bitcast.2.ocol_ref, bf16[4,4,256,512]{3,2,1,0:T(8,128)(2,1)S(1)} %copy-done.1, ...), custom_call_target="tpu_custom_call" | custom-call | flops 1610612736 | tf_op jit(solution)/shard_map/products_3/pallas_call | solution.py:257
  46.3 3.4 %collective-permute-start.16 = (f32[2,2,64,128]{3,2,1,0:T(8,128)S(1)}, f32[2,2,64,128]{3,2,1,0:T(8,128)S(1)}, u32[]{:S(2)}, u32[]{:S(2)}) collective-permute-start(f32[2,2,64,128]{3,2,1,0:T(8,128)S(1)} %get-tuple-element.51), channel_id=1, source_target_pairs={{0,8},{8,24},{24,16},{16,0},{1,9},{9,25},{25,17},{17,1},{2,10},{10... | collective-permute-start | bytes 393224 | tf_op jit(solution)/shard_map/ppermute | solution.py:279
  49.8 0.3 collective-permute-start.8
  50.1 0.1 collective-permute-start.11
  50.2 1.4 %collective-permute-start.14 = (f32[2,2,64,128]{3,2,1,0:T(8,128)S(1)}, f32[2,2,64,128]{3,2,1,0:T(8,128)S(1)}, u32[]{:S(2)}, u32[]{:S(2)}) collective-permute-start(f32[2,2,64,128]{3,2,1,0:T(8,128)S(1)} %add.33), channel_id=1, source_target_pairs={{0,8},{8,24},{24,16},{16,0},{1,9},{9,25},{25,17},{17,1},{2,10},{10... | collective-permute-start | bytes 393224 | tf_op jit(solution)/shard_map/ppermute | solution.py:279
  51.6 2.2 %collective-permute-done.16 = f32[2,2,64,128]{3,2,1,0:T(8,128)S(1)} collective-permute-done((f32[2,2,64,128]{3,2,1,0:T(8,128)S(1)}, f32[2,2,64,128]{3,2,1,0:T(8,128)S(1)}, u32[]{:S(2)}, u32[]{:S(2)}) %collective-permute-start.16) | collective-permute-done | bytes 131104 | tf_op jit(solution)/shard_map/ppermute | solution.py:279
  53.7 2.5 %collective-permute-start.17 = (f32[2,2,64,128]{3,2,1,0:T(8,128)S(1)}, f32[2,2,64,128]{3,2,1,0:T(8,128)S(1)}, u32[]{:S(2)}, u32[]{:S(2)}) collective-permute-start(f32[2,2,64,128]{3,2,1,0:T(8,128)S(1)} %add.35), channel_id=1, source_target_pairs={{0,8},{8,24},{24,16},{16,0},{1,9},{9,25},{25,17},{17,1},{2,10},{10... | collective-permute-start | bytes 393224 | tf_op jit(solution)/shard_map/ppermute | solution.py:279
  56.3 0.9 %collective-permute-done.8 = f32[2,2,64,128]{3,2,1,0:T(8,128)S(1)} collective-permute-done((f32[2,2,64,128]{3,2,1,0:T(8,128)S(1)}, f32[2,2,64,128]{3,2,1,0:T(8,128)S(1)}, u32[]{:S(2)}, u32[]{:S(2)}) %collective-permute-start.8) | collective-permute-done | bytes 131104 | tf_op jit(solution)/shard_map/ppermute | solution.py:279
  57.2 1.9 %collective-permute-start.9 = (f32[2,2,64,128]{3,2,1,0:T(8,128)S(1)}, f32[2,2,64,128]{3,2,1,0:T(8,128)S(1)}, u32[]{:S(2)}, u32[]{:S(2)}) collective-permute-start(f32[2,2,64,128]{3,2,1,0:T(8,128)S(1)} %add.30), channel_id=1, source_target_pairs={{0,8},{8,24},{24,16},{16,0},{1,9},{9,25},{25,17},{17,1},{2,10},{10... | collective-permute-start | bytes 393224 | tf_op jit(solution)/shard_map/ppermute | solution.py:279
  59.1 0.9 %collective-permute-done.11 = f32[2,2,64,128]{3,2,1,0:T(8,128)S(1)} collective-permute-done((f32[2,2,64,128]{3,2,1,0:T(8,128)S(1)}, f32[2,2,64,128]{3,2,1,0:T(8,128)S(1)}, u32[]{:S(2)}, u32[]{:S(2)}) %collective-permute-start.11) | collective-permute-done | bytes 131104 | tf_op jit(solution)/shard_map/ppermute | solution.py:279
  60.0 1.9 %collective-permute-start.12 = (f32[2,2,64,128]{3,2,1,0:T(8,128)S(1)}, f32[2,2,64,128]{3,2,1,0:T(8,128)S(1)}, u32[]{:S(2)}, u32[]{:S(2)}) collective-permute-start(f32[2,2,64,128]{3,2,1,0:T(8,128)S(1)} %add.32), channel_id=1, source_target_pairs={{0,8},{8,24},{24,16},{16,0},{1,9},{9,25},{25,17},{17,1},{2,10},{10... | collective-permute-start | bytes 393224 | tf_op jit(solution)/shard_map/ppermute | solution.py:279
  61.9 0.9 %collective-permute-done.14 = f32[2,2,64,128]{3,2,1,0:T(8,128)S(1)} collective-permute-done((f32[2,2,64,128]{3,2,1,0:T(8,128)S(1)}, f32[2,2,64,128]{3,2,1,0:T(8,128)S(1)}, u32[]{:S(2)}, u32[]{:S(2)}) %collective-permute-start.14) | collective-permute-done | bytes 131104 | tf_op jit(solution)/shard_map/ppermute | solution.py:279
  62.8 1.9 %collective-permute-start.15 = (f32[2,2,64,128]{3,2,1,0:T(8,128)S(1)}, f32[2,2,64,128]{3,2,1,0:T(8,128)S(1)}, u32[]{:S(2)}, u32[]{:S(2)}) collective-permute-start(f32[2,2,64,128]{3,2,1,0:T(8,128)S(1)} %add.34), channel_id=1, source_target_pairs={{0,8},{8,24},{24,16},{16,0},{1,9},{9,25},{25,17},{17,1},{2,10},{10... | collective-permute-start | bytes 393224 | tf_op jit(solution)/shard_map/ppermute | solution.py:279
  64.7 0.9 %collective-permute-done.17 = f32[2,2,64,128]{3,2,1,0:T(8,128)S(1)} collective-permute-done((f32[2,2,64,128]{3,2,1,0:T(8,128)S(1)}, f32[2,2,64,128]{3,2,1,0:T(8,128)S(1)}, u32[]{:S(2)}, u32[]{:S(2)}) %collective-permute-start.17) | collective-permute-done | bytes 131104 | tf_op jit(solution)/shard_map/ppermute | solution.py:279
  65.6 1.9 %collective-permute-start.18 = (f32[2,2,64,128]{3,2,1,0:T(8,128)S(1)}, f32[2,2,64,128]{3,2,1,0:T(8,128)S(1)}, u32[]{:S(2)}, u32[]{:S(2)}) collective-permute-start(f32[2,2,64,128]{3,2,1,0:T(8,128)S(1)} %add.36), channel_id=1, source_target_pairs={{0,8},{8,24},{24,16},{16,0},{1,9},{9,25},{25,17},{17,1},{2,10},{10... | collective-permute-start | bytes 393224 | tf_op jit(solution)/shard_map/ppermute | solution.py:279
  67.5 0.9 %collective-permute-done.9.refs_0_ = f32[2,2,64,128]{3,2,1,0:T(8,128)S(1)} collective-permute-done((f32[2,2,64,128]{3,2,1,0:T(8,128)S(1)}, f32[2,2,64,128]{3,2,1,0:T(8,128)S(1)}, u32[]{:S(2)}, u32[]{:S(2)}) %collective-permute-start.9) | collective-permute-done | bytes 131104 | tf_op jit(solution)/shard_map/ppermute | solution.py:279
  68.4 2.8 %collective-permute-done.12.refs_1_ = f32[2,2,64,128]{3,2,1,0:T(8,128)S(1)} collective-permute-done((f32[2,2,64,128]{3,2,1,0:T(8,128)S(1)}, f32[2,2,64,128]{3,2,1,0:T(8,128)S(1)}, u32[]{:S(2)}, u32[]{:S(2)}) %collective-permute-start.12) | collective-permute-done | bytes 131104 | tf_op jit(solution)/shard_map/ppermute | solution.py:279
  71.2 2.1 %collective-permute-done.15.refs_2_ = f32[2,2,64,128]{3,2,1,0:T(8,128)S(1)} collective-permute-done((f32[2,2,64,128]{3,2,1,0:T(8,128)S(1)}, f32[2,2,64,128]{3,2,1,0:T(8,128)S(1)}, u32[]{:S(2)}, u32[]{:S(2)}) %collective-permute-start.15) | collective-permute-done | bytes 131104 | tf_op jit(solution)/shard_map/ppermute | solution.py:279
  73.3 1.4 %collective-permute-done.18.refs_3_ = f32[2,2,64,128]{3,2,1,0:T(8,128)S(1)} collective-permute-done((f32[2,2,64,128]{3,2,1,0:T(8,128)S(1)}, f32[2,2,64,128]{3,2,1,0:T(8,128)S(1)}, u32[]{:S(2)}, u32[]{:S(2)}) %collective-permute-start.18) | collective-permute-done | bytes 131104 | tf_op jit(solution)/shard_map/ppermute | solution.py:279
  74.7 0.8 %step.1 = f32[2,8,64,128]{3,2,1,0:T(8,128)} custom-call(f32[2,2,64,128]{3,2,1,0:T(8,128)S(1)} %collective-permute-done.9.refs_0_, f32[2,2,64,128]{3,2,1,0:T(8,128)S(1)} %collective-permute-done.12.refs_1_, f32[2,2,64,128]{3,2,1,0:T(8,128)S(1)} %collective-permute-done.15.refs_2_, f32[2,2,64,128]{3,2,1,0:T(8,128)S(1)} %collective-permute-done.18.refs_3_, ...), custom_call_target="tpu_custom_call" | custom-call | tf_op jit(solution)/shard_map/step/pallas_call | solution.py:286
  (16 shorter events, 0.2 us)
Async XLA Ops:
  0.7 0.7 copy-start.4
  3.0 15.5 %collective-permute-start.1 = (f32[2,4,64,128]{3,2,1,0:T(8,128)S(1)}, f32[2,4,64,128]{3,2,1,0:T(8,128)S(1)}, u32[]{:S(2)}, u32[]{:S(2)}) collective-permute-start(f32[2,4,64,128]{3,2,1,0:T(8,128)S(1)} %sigma.1.refs_0_), channel_id=1, source_target_pairs={{0,2},{1,3},{2,0},{3,1},{4,6},{5,7},{6,4},{7,5},{8,10},{9,11},{10,... | collective-permute-start | bytes 786440 | tf_op jit(solution)/shard_map/ppermute | solution.py:227
  6.0 12.4 %collective-permute-start = (f32[2,4,64,128]{3,2,1,0:T(8,128)S(1)}, f32[2,4,64,128]{3,2,1,0:T(8,128)S(1)}, u32[]{:S(2)}, u32[]{:S(2)}) collective-permute-start(f32[2,4,64,128]{3,2,1,0:T(8,128)S(1)} %sigma.1.refs_0_), channel_id=1, source_target_pairs={{0,4},{1,5},{2,6},{3,7},{4,0},{5,1},{6,2},{7,3},{8,12},{9,13},{10,... | collective-permute-start | bytes 786440 | tf_op jit(solution)/shard_map/ppermute | solution.py:227
  14.5 1.9 %copy-start = (bf16[4,4,256,512]{3,2,1,0:T(8,128)(2,1)}, bf16[4,4,256,512]{3,2,1,0:T(8,128)(2,1)S(1)}, u32[]{:S(2)}) copy-start(bf16[4,4,256,512]{3,2,1,0:T(8,128)(2,1)S(1)} %get-tuple-element.32.right_high) | copy-start | bytes 12582916
  16.4 2.0 %copy-start.2 = (bf16[4,4,256,512]{3,2,1,0:T(8,128)(2,1)}, bf16[4,4,256,512]{3,2,1,0:T(8,128)(2,1)S(1)}, u32[]{:S(2)}) copy-start(bf16[4,4,256,512]{3,2,1,0:T(8,128)(2,1)S(1)} %get-tuple-element.33.right_low) | copy-start | bytes 12582916
  18.5 6.5 %collective-permute-start.3 = (f32[2,4,64,128]{3,2,1,0:T(8,128)S(1)}, f32[2,4,64,128]{3,2,1,0:T(8,128)}, u32[]{:S(2)}, u32[]{:S(2)}) collective-permute-start(f32[2,4,64,128]{3,2,1,0:T(8,128)S(1)} %broadcast_select_fusion), channel_id=1, source_target_pairs={{0,2},{1,5},{2,0},{3,7},{4,6},{5,1},{6,4},{7,3},{8,10},{9,13},{10,... | collective-permute-start | bytes 786440 | tf_op jit(solution)/shard_map/ppermute | solution.py:227
  19.0 6.0 %collective-permute-start.2 = (f32[2,4,64,128]{3,2,1,0:T(8,128)S(1)}, f32[2,4,64,128]{3,2,1,0:T(8,128)}, u32[]{:S(2)}, u32[]{:S(2)}) collective-permute-start(f32[2,4,64,128]{3,2,1,0:T(8,128)S(1)} %sigma.1.refs_0_), channel_id=1, source_target_pairs={{0,1},{1,0},{2,3},{3,2},{4,5},{5,4},{6,7},{7,6},{8,9},{9,8},{10,11... | collective-permute-start | bytes 786440 | tf_op jit(solution)/shard_map/ppermute | solution.py:227
  19.0 6.0 %collective-permute-start.5 = (f32[2,4,64,128]{3,2,1,0:T(8,128)S(1)}, f32[2,4,64,128]{3,2,1,0:T(8,128)}, u32[]{:S(2)}, u32[]{:S(2)}) collective-permute-start(f32[2,4,64,128]{3,2,1,0:T(8,128)S(1)} %collective-permute-done.1.refs_2_), channel_id=1, source_target_pairs={{0,1},{1,0},{2,3},{3,2},{4,5},{5,4},{6,7},{7,6},{8,9},{9,8},{10,11... | collective-permute-start | bytes 786440 | tf_op jit(solution)/shard_map/ppermute | solution.py:227
  19.6 5.5 %collective-permute-start.4 = (f32[2,4,64,128]{3,2,1,0:T(8,128)S(1)}, f32[2,4,64,128]{3,2,1,0:T(8,128)}, u32[]{:S(2)}, u32[]{:S(2)}) collective-permute-start(f32[2,4,64,128]{3,2,1,0:T(8,128)S(1)} %collective-permute-done.refs_1_), channel_id=1, source_target_pairs={{0,1},{1,0},{2,3},{3,2},{4,5},{5,4},{6,7},{7,6},{8,9},{9,8},{10,11... | collective-permute-start | bytes 786440 | tf_op jit(solution)/shard_map/ppermute | solution.py:227
  25.0 1.9 %collective-permute-start.6 = (f32[2,4,64,128]{3,2,1,0:T(8,128)}, f32[2,4,64,128]{3,2,1,0:T(8,128)}, u32[]{:S(2)}, u32[]{:S(2)}) collective-permute-start(f32[2,4,64,128]{3,2,1,0:T(8,128)} %collective-permute-done.3.refs_4_), channel_id=1, source_target_pairs={{0,1},{1,0},{2,3},{3,2},{4,5},{5,4},{6,7},{7,6},{8,9},{9,8},{10,11... | collective-permute-start | bytes 786440 | tf_op jit(solution)/shard_map/ppermute | solution.py:227
  26.9 2.2 %copy-start.1 = (bf16[4,4,256,512]{3,2,1,0:T(8,128)(2,1)S(1)}, bf16[4,4,256,512]{3,2,1,0:T(8,128)(2,1)}, u32[]{:S(2)}) copy-start(bf16[4,4,256,512]{3,2,1,0:T(8,128)(2,1)} %copy-done) | copy-start | bytes 12582916
  29.1 2.2 %copy-start.3 = (bf16[4,4,256,512]{3,2,1,0:T(8,128)(2,1)S(1)}, bf16[4,4,256,512]{3,2,1,0:T(8,128)(2,1)}, u32[]{:S(2)}) copy-start(bf16[4,4,256,512]{3,2,1,0:T(8,128)(2,1)} %copy-done.2) | copy-start | bytes 12582916
  34.6 6.5 %collective-permute-start.7 = (f32[2,2,64,128]{3,2,1,0:T(8,128)S(1)}, f32[2,2,64,128]{3,2,1,0:T(8,128)S(1)}, u32[]{:S(2)}, u32[]{:S(2)}) collective-permute-start(f32[2,2,64,128]{3,2,1,0:T(8,128)S(1)} %get-tuple-element.38), channel_id=1, source_target_pairs={{0,8},{8,24},{24,16},{16,0},{1,9},{9,25},{25,17},{17,1},{2,10},{10... | collective-permute-start | bytes 393224 | tf_op jit(solution)/shard_map/ppermute | solution.py:279
  38.1 6.4 %collective-permute-start.10 = (f32[2,2,64,128]{3,2,1,0:T(8,128)S(1)}, f32[2,2,64,128]{3,2,1,0:T(8,128)S(1)}, u32[]{:S(2)}, u32[]{:S(2)}) collective-permute-start(f32[2,2,64,128]{3,2,1,0:T(8,128)S(1)} %get-tuple-element.43), channel_id=1, source_target_pairs={{0,8},{8,24},{24,16},{16,0},{1,9},{9,25},{25,17},{17,1},{2,10},{10... | collective-permute-start | bytes 393224 | tf_op jit(solution)/shard_map/ppermute | solution.py:279
  43.0 7.2 %collective-permute-start.13 = (f32[2,2,64,128]{3,2,1,0:T(8,128)S(1)}, f32[2,2,64,128]{3,2,1,0:T(8,128)S(1)}, u32[]{:S(2)}, u32[]{:S(2)}) collective-permute-start(f32[2,2,64,128]{3,2,1,0:T(8,128)S(1)} %get-tuple-element.47), channel_id=1, source_target_pairs={{0,8},{8,24},{24,16},{16,0},{1,9},{9,25},{25,17},{17,1},{2,10},{10... | collective-permute-start | bytes 393224 | tf_op jit(solution)/shard_map/ppermute | solution.py:279
  46.3 7.4 %collective-permute-start.16 = (f32[2,2,64,128]{3,2,1,0:T(8,128)S(1)}, f32[2,2,64,128]{3,2,1,0:T(8,128)S(1)}, u32[]{:S(2)}, u32[]{:S(2)}) collective-permute-start(f32[2,2,64,128]{3,2,1,0:T(8,128)S(1)} %get-tuple-element.51), channel_id=1, source_target_pairs={{0,8},{8,24},{24,16},{16,0},{1,9},{9,25},{25,17},{17,1},{2,10},{10... | collective-permute-start | bytes 393224 | tf_op jit(solution)/shard_map/ppermute | solution.py:279
  49.8 7.4 %collective-permute-start.8 = (f32[2,2,64,128]{3,2,1,0:T(8,128)S(1)}, f32[2,2,64,128]{3,2,1,0:T(8,128)S(1)}, u32[]{:S(2)}, u32[]{:S(2)}) collective-permute-start(f32[2,2,64,128]{3,2,1,0:T(8,128)S(1)} %add.29), channel_id=1, source_target_pairs={{0,8},{8,24},{24,16},{16,0},{1,9},{9,25},{25,17},{17,1},{2,10},{10... | collective-permute-start | bytes 393224 | tf_op jit(solution)/shard_map/ppermute | solution.py:279
  50.1 9.9 %collective-permute-start.11 = (f32[2,2,64,128]{3,2,1,0:T(8,128)S(1)}, f32[2,2,64,128]{3,2,1,0:T(8,128)S(1)}, u32[]{:S(2)}, u32[]{:S(2)}) collective-permute-start(f32[2,2,64,128]{3,2,1,0:T(8,128)S(1)} %add.31), channel_id=1, source_target_pairs={{0,8},{8,24},{24,16},{16,0},{1,9},{9,25},{25,17},{17,1},{2,10},{10... | collective-permute-start | bytes 393224 | tf_op jit(solution)/shard_map/ppermute | solution.py:279
  50.2 12.6 %collective-permute-start.14 = (f32[2,2,64,128]{3,2,1,0:T(8,128)S(1)}, f32[2,2,64,128]{3,2,1,0:T(8,128)S(1)}, u32[]{:S(2)}, u32[]{:S(2)}) collective-permute-start(f32[2,2,64,128]{3,2,1,0:T(8,128)S(1)} %add.33), channel_id=1, source_target_pairs={{0,8},{8,24},{24,16},{16,0},{1,9},{9,25},{25,17},{17,1},{2,10},{10... | collective-permute-start | bytes 393224 | tf_op jit(solution)/shard_map/ppermute | solution.py:279
  53.7 11.9 %collective-permute-start.17 = (f32[2,2,64,128]{3,2,1,0:T(8,128)S(1)}, f32[2,2,64,128]{3,2,1,0:T(8,128)S(1)}, u32[]{:S(2)}, u32[]{:S(2)}) collective-permute-start(f32[2,2,64,128]{3,2,1,0:T(8,128)S(1)} %add.35), channel_id=1, source_target_pairs={{0,8},{8,24},{24,16},{16,0},{1,9},{9,25},{25,17},{17,1},{2,10},{10... | collective-permute-start | bytes 393224 | tf_op jit(solution)/shard_map/ppermute | solution.py:279
  57.2 11.2 %collective-permute-start.9 = (f32[2,2,64,128]{3,2,1,0:T(8,128)S(1)}, f32[2,2,64,128]{3,2,1,0:T(8,128)S(1)}, u32[]{:S(2)}, u32[]{:S(2)}) collective-permute-start(f32[2,2,64,128]{3,2,1,0:T(8,128)S(1)} %add.30), channel_id=1, source_target_pairs={{0,8},{8,24},{24,16},{16,0},{1,9},{9,25},{25,17},{17,1},{2,10},{10... | collective-permute-start | bytes 393224 | tf_op jit(solution)/shard_map/ppermute | solution.py:279
  60.0 11.2 %collective-permute-start.12 = (f32[2,2,64,128]{3,2,1,0:T(8,128)S(1)}, f32[2,2,64,128]{3,2,1,0:T(8,128)S(1)}, u32[]{:S(2)}, u32[]{:S(2)}) collective-permute-start(f32[2,2,64,128]{3,2,1,0:T(8,128)S(1)} %add.32), channel_id=1, source_target_pairs={{0,8},{8,24},{24,16},{16,0},{1,9},{9,25},{25,17},{17,1},{2,10},{10... | collective-permute-start | bytes 393224 | tf_op jit(solution)/shard_map/ppermute | solution.py:279
  62.8 10.5 %collective-permute-start.15 = (f32[2,2,64,128]{3,2,1,0:T(8,128)S(1)}, f32[2,2,64,128]{3,2,1,0:T(8,128)S(1)}, u32[]{:S(2)}, u32[]{:S(2)}) collective-permute-start(f32[2,2,64,128]{3,2,1,0:T(8,128)S(1)} %add.34), channel_id=1, source_target_pairs={{0,8},{8,24},{24,16},{16,0},{1,9},{9,25},{25,17},{17,1},{2,10},{10... | collective-permute-start | bytes 393224 | tf_op jit(solution)/shard_map/ppermute | solution.py:279
  65.6 9.1 %collective-permute-start.18 = (f32[2,2,64,128]{3,2,1,0:T(8,128)S(1)}, f32[2,2,64,128]{3,2,1,0:T(8,128)S(1)}, u32[]{:S(2)}, u32[]{:S(2)}) collective-permute-start(f32[2,2,64,128]{3,2,1,0:T(8,128)S(1)} %add.36), channel_id=1, source_target_pairs={{0,8},{8,24},{24,16},{16,0},{1,9},{9,25},{25,17},{17,1},{2,10},{10... | collective-permute-start | bytes 393224 | tf_op jit(solution)/shard_map/ppermute | solution.py:279

commit v3 on v2

v3 whole, which is shorter than its diff:
```python
import functools

import jax
import jax.numpy as jnp
from jax import lax
from jax.experimental import pallas as pl
from jax.experimental.pallas import tpu as pltpu
from jax.sharding import PartitionSpec as P

coupling_square = 0.25
hopping = 4.0
time_step = 0.01
VMEM = pl.BlockSpec(memory_space=pltpu.VMEM)
SMEM = pl.BlockSpec(memory_space=pltpu.SMEM)
HBM = pl.BlockSpec(memory_space=pltpu.HBM)


def sigma_kernel(hist_ref, step_ref, table_hbm, lesser_hbm, greater_hbm, out_ref, lesser, greater, table_ref, sems):
    slices = lesser.shape[1]
    copies = [
        pltpu.make_async_copy(source, target, sems.at[place])
        for place, (source, target) in enumerate(
            [(table_hbm, table_ref), (lesser_hbm, lesser), (greater_hbm, greater)]
        )
    ]
    for copy in copies:
        copy.start()
    for copy in copies:
        copy.wait()
    for s in range(slices):
        numerator = jnp.full((1, lesser.shape[3]), table_ref[s], jnp.int32).astype(jnp.float32)
        weight = jnp.where(hist_ref[0] * slices + s <= step_ref[0], numerator / 24.0, 0.0)
        a_re, a_im = lesser[0, s], lesser[1, s]
        b_re, b_im = greater[0, s], greater[1, s]
        square_re = a_re * a_re - a_im * a_im
        square_im = 2.0 * a_re * a_im
        scale = coupling_square * weight
        out_ref[0, s] = scale * (square_re * b_re - square_im * b_im)
        out_ref[1, s] = scale * (square_re * b_im + square_im * b_re)


def split(x):
    high = x.astype(jnp.bfloat16)
    return high, (x - high.astype(jnp.float32)).astype(jnp.bfloat16)


def history_kernel(
    first, advanced_hbm, row_hbm, adjacency_hbm, high_ref, low_ref, hop_ref, row, advanced, adjacency, sems
):
    slices, each, width = advanced.shape[1], advanced.shape[2], advanced.shape[4]
    near = [
        pltpu.make_async_copy(row_hbm.at[:, pl.ds(first, each)], row, sems.at[each]),
        pltpu.make_async_copy(adjacency_hbm, adjacency, sems.at[each + 1]),
    ]
    far = [
        pltpu.make_async_copy(advanced_hbm.at[:, :, first + t], advanced.at[:, :, t], sems.at[t]) for t in range(each)
    ]
    for copy in near + far:
        copy.start()
    for copy in near:
        copy.wait()
    graph = (-hopping * adjacency[...].astype(jnp.float32)).T.astype(jnp.bfloat16)
    for t in range(each):
        place = t * 2 * width
        row_high, row_low = split(jnp.concatenate([row[0, t], row[1, t]], axis=1))
        hop_ref[:, place : place + 2 * width] = jnp.dot(
            graph, row_high, preferred_element_type=jnp.float32
        ) + jnp.dot(graph, row_low, preferred_element_type=jnp.float32)
    for t in range(each):
        far[t].wait()
        for s in range(slices):
            for part in range(2):
                place = (2 * t + part) * width
                high, low = split(advanced[part, s, t])
                high_ref[s, :, place : place + width] = high
                low_ref[s, :, place : place + width] = low


def assemble(masks, my_orow, my_ocol, blocks, left_high, left_low):
    for (flip_orow, flip_ocol), block in zip(masks, blocks):
        at_orow = jnp.bitwise_xor(my_orow, flip_orow)
        at_ocol = jnp.bitwise_xor(my_ocol, flip_ocol)
        for s in range(left_high.shape[0]):
            for part in range(2):
                high, low = split(block(part, s) if callable(block) else block[part, s])
                left_high[s, at_orow, part, at_ocol] = high
                left_low[s, at_orow, part, at_ocol] = low


def assemble_kernel(masks, orow_ref, ocol_ref, *refs):
    assemble(masks, orow_ref[0], ocol_ref[0], refs[:-3], refs[-3], refs[-2])
    refs[-1][...] = jnp.zeros_like(refs[-1])


def halves_kernel(first_ref, second_ref, first_half, second_half):
    slices = first_half.shape[1]
    first_half[...] = first_ref[:, :slices]
    second_half[...] = second_ref[:, slices:]


def join(halves):
    half = halves[0].shape[1]
    return lambda part, s: halves[s // half][part, s % half]


def chunk_kernel(masks, ring, hist_ref, orow_ref, ocol_ref, right_high, right_low, hop_ref, left_high, left_low, *refs):
    outs, result = refs[2 * len(masks) : -1], refs[-1]
    if masks:
        left_high, left_low, outs = outs[-2], outs[-1], outs[:-2]
        blocks = [join(refs[2 * place : 2 * place + 2]) for place in range(len(masks))]
        assemble(masks, orow_ref[0], ocol_ref[0], blocks, left_high, left_low)
    slices, halves = left_high.shape[:2]
    norb = right_high.shape[1]
    width = outs[0].shape[3]

    def left(ref, s):
        return jnp.concatenate([ref[s, half].reshape(2 * norb, norb // halves) for half in range(halves)], axis=1)

    total = None
    for s in range(slices):
        high = right_high[s]
        here = jnp.dot(
            jnp.concatenate([left(left_high, s), left(left_high, s), left(left_low, s)], axis=1),
            jnp.concatenate([high, right_low[s], high], axis=0),
            preferred_element_type=jnp.float32,
        )
        total = here if total is None else total + here
    for t in range(outs[0].shape[1]):
        at = 2 * width * t
        sum_re = total[:norb, at : at + width] - total[norb:, at + width : at + 2 * width] + hop_ref[:, at : at + width]
        sum_im = total[:norb, at + width : at + 2 * width] + total[norb:, at : at + width] + hop_ref[:, at + width : at + 2 * width]
        if not ring:
            outs[0][0, t] = sum_re
            outs[0][1, t] = sum_im
            continue
        rows = norb // len(ring)
        for block in range(len(ring)):
            result[t, block, 0] = sum_re[block * rows : (block + 1) * rows]
            result[t, block, 1] = sum_im[block * rows : (block + 1) * rows]
    if not ring:
        return
    size = len(ring)
    my_hist = hist_ref[0]
    my_place = sum(jnp.where(my_hist == h, ring.index(h), 0) for h in range(size))
    for step, out in enumerate(outs):
        place = my_place + (size - 1 - step)
        place = jnp.where(place >= size, place - size, place)
        block = sum(jnp.where(place == p, ring[p], 0) for p in range(size))
        for t in range(out.shape[1]):
            out[0, t] = result[t, block, 0]
            out[1, t] = result[t, block, 1]


def step_kernel(*refs):
    chunks = (len(refs) - 3) // 3
    arrived, own, row = refs[:chunks], refs[chunks : 2 * chunks], refs[2 * chunks : 3 * chunks]
    out_hbm, out, sems = refs[3 * chunks :]
    copies, first = [], 0
    for chunk in range(chunks):
        here = pl.ds(first, own[chunk].shape[1])
        first += own[chunk].shape[1]
        out[0, here] = row[chunk][0] + time_step * (arrived[chunk][1] + own[chunk][1])
        out[1, here] = row[chunk][1] - time_step * (arrived[chunk][0] + own[chunk][0])
        copies.append(pltpu.make_async_copy(out.at[:, here], out_hbm.at[:, here], sems.at[chunk]))
        copies[-1].start()
    for copy in copies:
        copy.wait()


def ring_of(size):
    return [place for place in range(size) if place == 0 or place % 2 == 1] + [
        place for place in range(size - 1, 0, -1) if place % 2 == 0
    ]


def limit(mebibytes):
    return pltpu.CompilerParams(vmem_limit_bytes=mebibytes * 1024 * 1024)


def in_vmem(x):
    return pltpu.with_memory_space_constraint(x, pltpu.VMEM)


def in_hbm(x):
    return pltpu.with_memory_space_constraint(x, pltpu.HBM)


def on_device(
    hist_size, orow_size, ocol_size, lesser_hist, greater_hist, advanced_hist, current_row, adjacency, weight_table, step_index
):
    slices, times, norb, width = advanced_hist.shape[1:]
    block = lesser_hist.shape
    my_hist, my_orow, my_ocol = lax.axis_index("hist"), lax.axis_index("orow"), lax.axis_index("ocol")
    me = [index.reshape(1).astype(jnp.int32) for index in (my_hist, my_orow, my_ocol)]
    sigma = pl.pallas_call(
        sigma_kernel,
        out_shape=pltpu.VMEM(block, jnp.float32),
        in_specs=[SMEM] * 2 + [HBM] * 3,
        out_specs=VMEM,
        scratch_shapes=[
            pltpu.VMEM(block, jnp.float32),
            pltpu.VMEM(block, jnp.float32),
            pltpu.SMEM(weight_table.shape, jnp.int32),
            pltpu.SemaphoreType.DMA((3,)),
        ],
        compiler_params=limit(4),
        name="sigma",
    )(me[0], step_index, in_hbm(weight_table), in_hbm(lesser_hist), in_hbm(jnp.swapaxes(greater_hist, 2, 3)))

    short = times // 4
    sizes = [short, (times - short) // 2, times - short - (times - short) // 2]
    chunks = len(sizes)

    def history(chunk):
        each = sizes[chunk]
        return list(pl.pallas_call(
            functools.partial(history_kernel, sum(sizes[:chunk])),
            out_shape=[
                pltpu.VMEM((slices, norb, each * 2 * width), jnp.bfloat16),
                pltpu.VMEM((slices, norb, each * 2 * width), jnp.bfloat16),
                pltpu.VMEM((norb, each * 2 * width), jnp.float32),
                pltpu.VMEM((2, each) + current_row.shape[2:], jnp.float32),
            ],
            in_specs=[HBM] * 3,
            out_specs=[VMEM] * 4,
            scratch_shapes=[
                pltpu.VMEM((2, slices, each, norb, width), jnp.float32),
                pltpu.VMEM(adjacency.shape, jnp.int32),
                pltpu.SemaphoreType.DMA((each + 2,)),
            ],
            compiler_params=limit(12),
            cost_estimate=pl.CostEstimate(flops=0, bytes_accessed=4 * 1024 * 1024, transcendentals=0),
            name=f"history_{chunk}",
        )(in_hbm(advanced_hist), in_hbm(current_row), in_hbm(adjacency)))

    def moved(x, target):
        pairs = [
            (r * ocol_size + c, target(r, c)[0] * ocol_size + target(r, c)[1])
            for r in range(orow_size)
            for c in range(ocol_size)
        ]
        return lax.ppermute(x, ("orow", "ocol"), pairs)

    def over_core(x):
        return moved(x, lambda r, c: (r, c ^ 1))

    histories = [history(chunk) for chunk in range(chunks)]
    held = {(0, 0): sigma}
    held[(1, 0)] = moved(sigma, lambda r, c: (r ^ 1, c))
    held[(0, 2)] = moved(sigma, lambda r, c: (r, c ^ 2))
    held[(0, 1)] = over_core(sigma)
    over_orow, over_ocol, *_ = lax.optimization_barrier(
        (held[(1, 0)], held[(0, 2)], histories[0][3], histories[1][3])
    )
    half_shape = (2, slices // 2) + block[2:]
    halves = pl.pallas_call(
        halves_kernel,
        out_shape=[pltpu.VMEM(half_shape, jnp.float32), pltpu.VMEM((2, slices - slices // 2) + block[2:], jnp.float32)],
        in_specs=[VMEM] * 2,
        out_specs=[VMEM] * 2,
        compiler_params=limit(4),
        name="halves",
    )(in_vmem(over_orow), in_vmem(over_ocol))
    late = (moved(halves[0], lambda r, c: (r, c ^ 2)), moved(halves[1], lambda r, c: (r ^ 1, c)))
    held[(1, 1)] = over_core(held[(1, 0)])
    held[(0, 3)] = over_core(held[(0, 2)])
    left_shape = (slices, orow_size, 2, ocol_size) + block[2:]
    *left, token = pl.pallas_call(
        functools.partial(assemble_kernel, tuple(held)),
        out_shape=[pltpu.VMEM(left_shape, jnp.bfloat16)] * 2 + [pltpu.VMEM((8, 128), jnp.float32)],
        in_specs=[SMEM] * 2 + [VMEM] * len(held),
        out_specs=[VMEM] * 3,
        compiler_params=limit(4),
        cost_estimate=pl.CostEstimate(flops=0, bytes_accessed=2 * 1024 * 1024, transcendentals=0),
        name="assemble",
    )(*me[1:], *[in_vmem(x) for x in held.values()])
    *late, _, _ = lax.optimization_barrier((*late, token, histories[2][3]))
    late = {(1, 2): late, (1, 3): [over_core(x) for x in late]}

    rows = norb // hist_size
    ring = ring_of(hist_size) if hist_size <= 8 else []
    arrived, own, firsts = [], [], []
    for chunk, each in enumerate(sizes):
        if ring:
            out_shape = [pltpu.VMEM((2, each, rows, width), jnp.float32)] * hist_size
        else:
            out_shape = [pltpu.VMEM((2, each, norb, width), jnp.float32)]
        count, aliases, masks = len(out_shape), {}, ()
        after = lax.optimization_barrier((me[0], firsts[chunk - 2]))[0] if chunk >= 2 and ring else me[0]
        operands = [after, *me[1:]] + [in_vmem(x) for x in histories[chunk][:3]] + [in_vmem(x) for x in left]
        if chunk == 0:
            masks = tuple(late)
            operands += [in_vmem(x) for pair in late.values() for x in pair]
            out_shape += [pltpu.VMEM(left_shape, jnp.bfloat16)] * 2
            aliases = {6: count, 7: count + 1}
        parts = pl.pallas_call(
            functools.partial(chunk_kernel, masks, ring),
            out_shape=out_shape,
            in_specs=[SMEM] * 3 + [VMEM] * (len(operands) - 3),
            out_specs=[VMEM] * len(out_shape),
            scratch_shapes=[pltpu.VMEM((each, hist_size, 2, rows, width), jnp.float32)],
            input_output_aliases=aliases,
            cost_estimate=pl.CostEstimate(
                flops=6 * each * slices * 2 * norb * norb * 2 * width, bytes_accessed=0, transcendentals=0
            ),
            compiler_params=limit(16),
            name=f"products_{chunk}",
        )(*operands)
        if chunk == 0:
            left, parts = parts[count:], parts[:count]
        if not ring:
            total = lax.psum_scatter(parts[0], "hist", scatter_dimension=2, tiled=True)
            arrived.append(total)
            own.append(jnp.zeros_like(total))
            continue
        pairs = [(ring[p], ring[(p + 1) % hist_size]) for p in range(hist_size)]
        moving = parts[0]
        for m in range(1, hist_size):
            moving = lax.ppermute(moving, "hist", pairs)
            if m == 1:
                firsts.append(moving)
            if m < hist_size - 1:
                moving = moving + parts[m]
        arrived.append(moving)
        own.append(parts[-1])
    return pl.pallas_call(
        step_kernel,
        out_shape=jax.ShapeDtypeStruct(current_row.shape, jnp.float32),
        in_specs=[VMEM] * (3 * chunks),
        out_specs=HBM,
        scratch_shapes=[pltpu.VMEM(current_row.shape, jnp.float32), pltpu.SemaphoreType.DMA((chunks,))],
        compiler_params=limit(4),
        name="step",
    )(*[in_vmem(x) for x in arrived + own + [h[3] for h in histories]])


def solution(mesh):
    in_specs = (
        P(None, "hist", "ocol", "orow"),
        P(None, "hist", "orow", "ocol"),
        P(None, "hist", "ocol", None, "orow"),
        P(None, "ocol", "hist", "orow"),
        P("hist", None),
        P("hist"),
        P(),
    )
    out_specs = P(None, "ocol", "hist", "orow")
    body = functools.partial(on_device, mesh.shape["hist"], mesh.shape["orow"], mesh.shape["ocol"])
    return jax.shard_map(
        body, mesh=mesh, in_specs=in_specs, out_specs=out_specs, check_vma=False
    )
```

time: 76 us -> 67.6 us (0.89)
  starting transfers between devices: 26.6 us -> 19.3 us
  local copies, waits for them, and re-layouts: 8.99 us -> 7.76 us
  waiting for transfers between devices: 20.7 us -> 21.7 us
    ppermute x12 -> x9, starting transfers between devices: 21 us -> 13.1 us  [on_device(): moving = lax.ppermute(moving, 'hist', pairs)]
    ppermute x12 -> x9, waiting for transfers between devices: 13.4 us -> 21.3 us  [on_device(): moving = lax.ppermute(moving, 'hist', pairs)]
    ppermute x7 -> x9, waiting for transfers between devices: 7.32 us -> 0.46 us  [moved(): return lax.ppermute(x, ('orow', 'ocol'), pairs)]
    unnamed x10 -> x32, local copies, waits for them, and re-layouts: 8.99 us -> 7.76 us
    ppermute x7 -> x9, starting transfers between devices: 5.61 us -> 6.23 us  [moved(): return lax.ppermute(x, ('orow', 'ocol'), pairs)]
    pallas_call x5 -> x8, Pallas kernels: 15.8 us -> 15.6 us  [the longest x3 8.44 us: on_device(): pl.pallas_call(functools.partial(chunk_kernel, masks, ring), out_shape=ou...]
  transfers between devices with their start and end apart: 19 -> 18, of which waited for: 12 -> 8; matrix products, arithmetic and copies ran while one was open for 0% -> 0% of each run, Pallas kernels for 17% -> 19%
where the time goes in v3:
time: 67.6 us; the launch traced here: 67.4 us
  waiting for transfers between devices  21.7 us (32%)
  starting transfers between devices  19.3 us (29%)
  Pallas kernels  17.6 us (26%)
  local copies, waits for them, and re-layouts  7.76 us (11%)
  between operations  0.83 us (1%)
    ppermute x9, waiting for transfers between devices, on_device(): moving = lax.ppermute(moving, 'hist', pairs)  21.3 us
    ppermute x9, starting transfers between devices, on_device(): moving = lax.ppermute(moving, 'hist', pairs)  13.1 us
    pallas_call x3, Pallas kernels, on_device(): pl.pallas_call(functools.partial(chunk_kernel, masks, ring), out_shape=ou...  8.44 us
    unnamed x32, local copies, waits for them, and re-layouts  7.76 us
    pallas_call x3, Pallas kernels, history(): pl.pallas_call(functools.partial(history_kernel, sum(sizes[:chunk])), out...  6.47 us
    ppermute x9, starting transfers between devices, moved(): return lax.ppermute(x, ('orow', 'ocol'), pairs)  6.23 us
  transfers between devices with their start and end apart: 18, of which 8 were waited for; matrix products, arithmetic and copies ran while one was open for 0% of the time, Pallas kernels for 19%

profile of v3, /device:TPU:0, one launch (start us, length us, event | category | flops | bytes accessed | tf_op | source)
XLA Modules:
  0.0 67.4 jit_solution(3478965133095511734)
XLA Ops:
  0.7 1.1 %sigma.1.refs_0_ = f32[2,4,64,128]{3,2,1,0:T(8,128)S(1)} custom-call(s32[1]{0:T(128)} %bitcast.hist_ref, s32[1]{0:T(128)S(6)} %copy.12.step_ref, s32[4]{0:T(128)} %table_hbm.1, f32[2,4,64,128]{3,2,1,0:T(8,128)} %lesser_hbm.1, f32[2,4,64,128]{3,2,1,0:T(8,128)} %bitcast.4), custom_call_target="tpu_custom_call" | custom-call | tf_op jit(solution)/shard_map/sigma/pallas_call | solution.py:195
  1.8 3.0 %collective-permute-start.1 = (f32[2,4,64,128]{3,2,1,0:T(8,128)S(1)}, f32[2,4,64,128]{3,2,1,0:T(8,128)S(1)}, u32[]{:S(2)}, u32[]{:S(2)}) collective-permute-start(f32[2,4,64,128]{3,2,1,0:T(8,128)S(1)} %sigma.1.refs_0_), channel_id=1, source_target_pairs={{0,2},{1,3},{2,0},{3,1},{4,6},{5,7},{6,4},{7,5},{8,10},{9,11},{10,... | collective-permute-start | bytes 786440 | tf_op jit(solution)/shard_map/ppermute | solution.py:242
  4.8 1.5 %collective-permute-start = (f32[2,4,64,128]{3,2,1,0:T(8,128)S(1)}, f32[2,4,64,128]{3,2,1,0:T(8,128)S(1)}, u32[]{:S(2)}, u32[]{:S(2)}) collective-permute-start(f32[2,4,64,128]{3,2,1,0:T(8,128)S(1)} %sigma.1.refs_0_), channel_id=1, source_target_pairs={{0,4},{1,5},{2,6},{3,7},{4,0},{5,1},{6,2},{7,3},{8,12},{9,13},{10,... | collective-permute-start | bytes 786440 | tf_op jit(solution)/shard_map/ppermute | solution.py:242
  6.3 0.0 collective-permute-start.2
  6.3 1.9 %history_0.1 = (bf16[4,256,512]{2,1,0:T(8,128)(2,1)S(1)}, bf16[4,256,512]{2,1,0:T(8,128)(2,1)S(1)}, f32[256,512]{1,0:T(8,128)S(1)}, f32[2,2,64,128]{3,2,1,0:T(8,128)S(1)}) custom-call(f32[2,4,8,256,128]{4,3,2,1,0:T(8,128)} %advanced_hbm.5, f32[2,8,64,128]{3,2,1,0:T(8,128)} %row_hbm.5, s32[64,256]{1,0:T(8,128)} %adjacency_hbm.5), custom_call_target="tpu_custom_call" | custom-call | bytes 4194304 | tf_op jit(solution)/shard_map/history_0/pallas_call | solution.py:216
  8.2 1.0 %copy-done.8 = bf16[4,256,512]{2,1,0:T(8,128)(2,1)} copy-done((bf16[4,256,512]{2,1,0:T(8,128)(2,1)}, bf16[4,256,512]{2,1,0:T(8,128)(2,1)S(1)}, u32[]{:S(2)}) %copy-start.8) | copy-done | bytes 1048600
  9.2 2.4 %history_1.1 = (bf16[4,256,768]{2,1,0:T(8,128)(2,1)S(1)}, bf16[4,256,768]{2,1,0:T(8,128)(2,1)S(1)}, f32[256,768]{1,0:T(8,128)S(1)}, f32[2,3,64,128]{3,2,1,0:T(8,128)S(1)}) custom-call(f32[2,4,8,256,128]{4,3,2,1,0:T(8,128)} %advanced_hbm.5, f32[2,8,64,128]{3,2,1,0:T(8,128)} %row_hbm.5, s32[64,256]{1,0:T(8,128)} %adjacency_hbm.5), custom_call_target="tpu_custom_call" | custom-call | bytes 4194304 | tf_op jit(solution)/shard_map/history_1/pallas_call | solution.py:216
  11.6 1.2 %copy-done = bf16[4,256,768]{2,1,0:T(8,128)(2,1)} copy-done((bf16[4,256,768]{2,1,0:T(8,128)(2,1)}, bf16[4,256,768]{2,1,0:T(8,128)(2,1)S(1)}, u32[]{:S(2)}) %copy-start) | copy-done | bytes 1572888
  12.7 1.2 %copy-done.2 = bf16[4,256,768]{2,1,0:T(8,128)(2,1)} copy-done((bf16[4,256,768]{2,1,0:T(8,128)(2,1)}, bf16[4,256,768]{2,1,0:T(8,128)(2,1)S(1)}, u32[]{:S(2)}) %copy-start.2) | copy-done | bytes 1572888
  13.9 1.0 %copy-done.10 = f32[256,768]{1,0:T(8,128)} copy-done((f32[256,768]{1,0:T(8,128)}, f32[256,768]{1,0:T(8,128)S(1)}, u32[]{:S(2)}) %copy-start.10) | copy-done | bytes 786456
  14.9 0.6 collective-permute-start.5
  15.5 0.1 collective-permute-start.6
  15.6 0.2 collective-permute-start.4
  15.8 0.3 collective-permute-start.3
  16.1 2.2 %history_2.1 = (bf16[4,256,768]{2,1,0:T(8,128)(2,1)S(1)}, bf16[4,256,768]{2,1,0:T(8,128)(2,1)S(1)}, f32[256,768]{1,0:T(8,128)S(1)}, f32[2,3,64,128]{3,2,1,0:T(8,128)S(1)}) custom-call(f32[2,4,8,256,128]{4,3,2,1,0:T(8,128)} %advanced_hbm.5, f32[2,8,64,128]{3,2,1,0:T(8,128)} %row_hbm.5, s32[64,256]{1,0:T(8,128)} %adjacency_hbm.5), custom_call_target="tpu_custom_call" | custom-call | bytes 4194304 | tf_op jit(solution)/shard_map/history_2/pallas_call | solution.py:216
  18.3 1.1 %copy-done.4 = bf16[4,256,768]{2,1,0:T(8,128)(2,1)} copy-done((bf16[4,256,768]{2,1,0:T(8,128)(2,1)}, bf16[4,256,768]{2,1,0:T(8,128)(2,1)S(1)}, u32[]{:S(2)}) %copy-start.4) | copy-done | bytes 1572888
  19.5 1.2 %copy-done.6 = bf16[4,256,768]{2,1,0:T(8,128)(2,1)} copy-done((bf16[4,256,768]{2,1,0:T(8,128)(2,1)}, bf16[4,256,768]{2,1,0:T(8,128)(2,1)S(1)}, u32[]{:S(2)}) %copy-start.6) | copy-done | bytes 1572888
  20.7 1.0 %copy-done.12 = f32[256,768]{1,0:T(8,128)} copy-done((f32[256,768]{1,0:T(8,128)}, f32[256,768]{1,0:T(8,128)S(1)}, u32[]{:S(2)}) %copy-start.12) | copy-done | bytes 786456
  21.6 0.0 collective-permute-done.6.refs_1_
  21.6 0.2 collective-permute-start.7
  21.9 0.3 collective-permute-start.8
  22.1 0.0 collective-permute-done.2.refs_3_
  22.2 0.0 collective-permute-done.4.refs_5_
  22.2 0.7 %assemble.1 = (bf16[4,2,2,4,64,128]{5,4,3,2,1,0:T(8,128)(2,1)S(1)}, bf16[4,2,2,4,64,128]{5,4,3,2,1,0:T(8,128)(2,1)S(1)}, f32[8,128]{1,0:T(8,128)}) custom-call(s32[1]{0:T(128)} %bitcast.1.orow_ref, s32[1]{0:T(128)} %bitcast.2.ocol_ref, f32[2,4,64,128]{3,2,1,0:T(8,128)S(1)} %sigma.1.refs_0_, f32[2,4,64,128]{3,2,1,0:T(8,128)S(1)} %collective-permute-done.refs_1_.first_ref, ...), custom_call_target="tpu_custom_call" | custom-call | bytes 2097152 | tf_op jit(solution)/shard_map/assemble/pallas_call | solution.py:268
  22.9 0.1 collective-permute-done.7.refs_2_
  23.0 0.4 collective-permute-done.8.refs_3_
  23.3 0.0 copy-done.9
  23.4 0.1 copy-done.15
  23.5 2.9 %products_0.1 = (f32[2,2,64,128]{3,2,1,0:T(8,128)S(1)}, f32[2,2,64,128]{3,2,1,0:T(8,128)S(1)}, f32[2,2,64,128]{3,2,1,0:T(8,128)S(1)}, f32[2,2,64,128]{3,2,1,0:T(...) custom-call(s32[1]{0:T(128)} %bitcast.hist_ref, ...), custom_call_target="tpu_custom_call", output_to_operand_aliasing={{4}: (6, {}), {5}: (7, {})} | custom-call | flops 1610612736 | tf_op jit(solution)/shard_map/products_0/pallas_call | solution.py:296
  26.4 2.1 %collective-permute-start.9 = (f32[2,2,64,128]{3,2,1,0:T(8,128)S(1)}, f32[2,2,64,128]{3,2,1,0:T(8,128)S(1)}, u32[]{:S(2)}, u32[]{:S(2)}) collective-permute-start(f32[2,2,64,128]{3,2,1,0:T(8,128)S(1)} %get-tuple-element.54), channel_id=1, source_target_pairs={{0,8},{8,24},{24,16},{16,0},{1,9},{9,25},{25,17},{17,1},{2,10},{10... | collective-permute-start | bytes 393224 | tf_op jit(solution)/shard_map/ppermute | solution.py:319
  28.5 2.8 %products_1.1 = (f32[2,3,64,128]{3,2,1,0:T(8,128)S(1)}, f32[2,3,64,128]{3,2,1,0:T(8,128)S(1)}, f32[2,3,64,128]{3,2,1,0:T(8,128)S(1)}, f32[2,3,64,128]{3,2,1,0:T(8,128)S(1)}) custom-call(s32[1]{0:T(128)} %bitcast.hist_ref, s32[1]{0:T(128)} %bitcast.1.orow_ref, s32[1]{0:T(128)} %bitcast.2.ocol_ref, bf16[4,256,768]{2,1,0:T(8,128)(2,1)S(1)} %copy-done.1, ...), custom_call_target="tpu_custom_call" | custom-call | flops 2415919104 | tf_op jit(solution)/shard_map/products_1/pallas_call | solution.py:296
  31.3 2.6 %collective-permute-start.12 = (f32[2,3,64,128]{3,2,1,0:T(8,128)S(1)}, f32[2,3,64,128]{3,2,1,0:T(8,128)S(1)}, u32[]{:S(2)}, u32[]{:S(2)}) collective-permute-start(f32[2,3,64,128]{3,2,1,0:T(8,128)S(1)} %get-tuple-element.62), channel_id=1, source_target_pairs={{0,8},{8,24},{24,16},{16,0},{1,9},{9,25},{25,17},{17,1},{2,10},{10... | collective-permute-start | bytes 589832 | tf_op jit(solution)/shard_map/ppermute | solution.py:319
  34.0 2.8 %products_2.1 = (f32[2,3,64,128]{3,2,1,0:T(8,128)S(1)}, f32[2,3,64,128]{3,2,1,0:T(8,128)S(1)}, f32[2,3,64,128]{3,2,1,0:T(8,128)S(1)}, f32[2,3,64,128]{3,2,1,0:T(8,128)S(1)}) custom-call(s32[1]{0:T(128)} %bitcast.hist_ref, s32[1]{0:T(128)} %bitcast.1.orow_ref, s32[1]{0:T(128)} %bitcast.2.ocol_ref, bf16[4,256,768]{2,1,0:T(8,128)(2,1)S(1)} %copy-done.5, ...), custom_call_target="tpu_custom_call" | custom-call | flops 2415919104 | tf_op jit(solution)/shard_map/products_2/pallas_call | solution.py:296
  36.7 0.5 collective-permute-start.15
  37.2 2.0 %collective-permute-done.12 = f32[2,3,64,128]{3,2,1,0:T(8,128)S(1)} collective-permute-done((f32[2,3,64,128]{3,2,1,0:T(8,128)S(1)}, f32[2,3,64,128]{3,2,1,0:T(8,128)S(1)}, u32[]{:S(2)}, u32[]{:S(2)}) %collective-permute-start.12) | collective-permute-done | bytes 196640 | tf_op jit(solution)/shard_map/ppermute | solution.py:319
  39.3 2.5 %collective-permute-start.13 = (f32[2,3,64,128]{3,2,1,0:T(8,128)S(1)}, f32[2,3,64,128]{3,2,1,0:T(8,128)S(1)}, u32[]{:S(2)}, u32[]{:S(2)}) collective-permute-start(f32[2,3,64,128]{3,2,1,0:T(8,128)S(1)} %add.20), channel_id=1, source_target_pairs={{0,8},{8,24},{24,16},{16,0},{1,9},{9,25},{25,17},{17,1},{2,10},{10... | collective-permute-start | bytes 589832 | tf_op jit(solution)/shard_map/ppermute | solution.py:319
  41.8 3.7 %collective-permute-done.15 = f32[2,3,64,128]{3,2,1,0:T(8,128)S(1)} collective-permute-done((f32[2,3,64,128]{3,2,1,0:T(8,128)S(1)}, f32[2,3,64,128]{3,2,1,0:T(8,128)S(1)}, u32[]{:S(2)}, u32[]{:S(2)}) %collective-permute-start.15) | collective-permute-done | bytes 196640 | tf_op jit(solution)/shard_map/ppermute | solution.py:319
  45.5 0.5 collective-permute-start.16
  46.0 3.2 %collective-permute-start.10 = (f32[2,2,64,128]{3,2,1,0:T(8,128)S(1)}, f32[2,2,64,128]{3,2,1,0:T(8,128)S(1)}, u32[]{:S(2)}, u32[]{:S(2)}) collective-permute-start(f32[2,2,64,128]{3,2,1,0:T(8,128)S(1)} %add.18), channel_id=1, source_target_pairs={{0,8},{8,24},{24,16},{16,0},{1,9},{9,25},{25,17},{17,1},{2,10},{10... | collective-permute-start | bytes 393224 | tf_op jit(solution)/shard_map/ppermute | solution.py:319
  49.2 0.5 collective-permute-done.13
  49.7 0.5 collective-permute-start.14
  50.2 4.1 %collective-permute-done.16 = f32[2,3,64,128]{3,2,1,0:T(8,128)S(1)} collective-permute-done((f32[2,3,64,128]{3,2,1,0:T(8,128)S(1)}, f32[2,3,64,128]{3,2,1,0:T(8,128)S(1)}, u32[]{:S(2)}, u32[]{:S(2)}) %collective-permute-start.16) | collective-permute-done | bytes 196640 | tf_op jit(solution)/shard_map/ppermute | solution.py:319
  54.3 0.3 collective-permute-start.17
  54.6 2.5 %collective-permute-done.10 = f32[2,2,64,128]{3,2,1,0:T(8,128)S(1)} collective-permute-done((f32[2,2,64,128]{3,2,1,0:T(8,128)S(1)}, f32[2,2,64,128]{3,2,1,0:T(8,128)S(1)}, u32[]{:S(2)}, u32[]{:S(2)}) %collective-permute-start.10) | collective-permute-done | bytes 131104 | tf_op jit(solution)/shard_map/ppermute | solution.py:319
  57.1 0.9 %collective-permute-start.11 = (f32[2,2,64,128]{3,2,1,0:T(8,128)S(1)}, f32[2,2,64,128]{3,2,1,0:T(8,128)S(1)}, u32[]{:S(2)}, u32[]{:S(2)}) collective-permute-start(f32[2,2,64,128]{3,2,1,0:T(8,128)S(1)} %add.19), channel_id=1, source_target_pairs={{0,8},{8,24},{24,16},{16,0},{1,9},{9,25},{25,17},{17,1},{2,10},{10... | collective-permute-start | bytes 393224 | tf_op jit(solution)/shard_map/ppermute | solution.py:319
  58.1 8.5 %collective-permute-done.11.refs_0_ = f32[2,2,64,128]{3,2,1,0:T(8,128)S(1)} collective-permute-done((f32[2,2,64,128]{3,2,1,0:T(8,128)S(1)}, f32[2,2,64,128]{3,2,1,0:T(8,128)S(1)}, u32[]{:S(2)}, u32[]{:S(2)}) %collective-permute-start.11) | collective-permute-done | bytes 131104 | tf_op jit(solution)/shard_map/ppermute | solution.py:319
  66.5 0.0 collective-permute-done.14.refs_1_
  66.5 0.9 %step.1 = f32[2,8,64,128]{3,2,1,0:T(8,128)} custom-call(f32[2,2,64,128]{3,2,1,0:T(8,128)S(1)} %collective-permute-done.11.refs_0_, f32[2,3,64,128]{3,2,1,0:T(8,128)S(1)} %collective-permute-done.14.refs_1_, f32[2,3,64,128]{3,2,1,0:T(8,128)S(1)} %collective-permute-done.17.refs_2_, f32[2,2,64,128]{3,2,1,0:T(8,128)S(1)} %get-tuple-element.72.refs_3_, ...), custom_call_target="tpu_custom_call" | custom-call | tf_op jit(solution)/shard_map/step/pallas_call | solution.py:326
  (36 shorter events, 0.2 us)
Async XLA Ops:
  1.8 13.1 %collective-permute-start.1 = (f32[2,4,64,128]{3,2,1,0:T(8,128)S(1)}, f32[2,4,64,128]{3,2,1,0:T(8,128)S(1)}, u32[]{:S(2)}, u32[]{:S(2)}) collective-permute-start(f32[2,4,64,128]{3,2,1,0:T(8,128)S(1)} %sigma.1.refs_0_), channel_id=1, source_target_pairs={{0,2},{1,3},{2,0},{3,1},{4,6},{5,7},{6,4},{7,5},{8,10},{9,11},{10,... | collective-permute-start | bytes 786440 | tf_op jit(solution)/shard_map/ppermute | solution.py:242
  4.8 10.1 %collective-permute-start = (f32[2,4,64,128]{3,2,1,0:T(8,128)S(1)}, f32[2,4,64,128]{3,2,1,0:T(8,128)S(1)}, u32[]{:S(2)}, u32[]{:S(2)}) collective-permute-start(f32[2,4,64,128]{3,2,1,0:T(8,128)S(1)} %sigma.1.refs_0_), channel_id=1, source_target_pairs={{0,4},{1,5},{2,6},{3,7},{4,0},{5,1},{6,2},{7,3},{8,12},{9,13},{10,... | collective-permute-start | bytes 786440 | tf_op jit(solution)/shard_map/ppermute | solution.py:242
  6.3 15.8 %collective-permute-start.2 = (f32[2,4,64,128]{3,2,1,0:T(8,128)S(1)}, f32[2,4,64,128]{3,2,1,0:T(8,128)S(1)}, u32[]{:S(2)}, u32[]{:S(2)}) collective-permute-start(f32[2,4,64,128]{3,2,1,0:T(8,128)S(1)} %sigma.1.refs_0_), channel_id=1, source_target_pairs={{0,1},{1,0},{2,3},{3,2},{4,5},{5,4},{6,7},{7,6},{8,9},{9,8},{10,11... | collective-permute-start | bytes 786440 | tf_op jit(solution)/shard_map/ppermute | solution.py:242
  8.2 1.0 %copy-start.8 = (bf16[4,256,512]{2,1,0:T(8,128)(2,1)}, bf16[4,256,512]{2,1,0:T(8,128)(2,1)S(1)}, u32[]{:S(2)}) copy-start(bf16[4,256,512]{2,1,0:T(8,128)(2,1)S(1)} %get-tuple-element.41.right_low) | copy-start | bytes 3145732
  9.1 2.4 %copy-start.14 = (f32[256,512]{1,0:T(8,128)}, f32[256,512]{1,0:T(8,128)S(1)}, u32[]{:S(2)}) copy-start(f32[256,512]{1,0:T(8,128)S(1)} %get-tuple-element.42.hop_ref) | copy-start | bytes 1572868
  11.6 1.2 %copy-start = (bf16[4,256,768]{2,1,0:T(8,128)(2,1)}, bf16[4,256,768]{2,1,0:T(8,128)(2,1)S(1)}, u32[]{:S(2)}) copy-start(bf16[4,256,768]{2,1,0:T(8,128)(2,1)S(1)} %get-tuple-element.57.right_high) | copy-start | bytes 4718596
  12.7 1.2 %copy-start.2 = (bf16[4,256,768]{2,1,0:T(8,128)(2,1)}, bf16[4,256,768]{2,1,0:T(8,128)(2,1)S(1)}, u32[]{:S(2)}) copy-start(bf16[4,256,768]{2,1,0:T(8,128)(2,1)S(1)} %get-tuple-element.58.right_low) | copy-start | bytes 4718596
  13.9 1.0 %copy-start.10 = (f32[256,768]{1,0:T(8,128)}, f32[256,768]{1,0:T(8,128)S(1)}, u32[]{:S(2)}) copy-start(f32[256,768]{1,0:T(8,128)S(1)} %get-tuple-element.59.hop_ref) | copy-start | bytes 2359300
  14.9 6.7 %collective-permute-start.5 = (f32[2,2,64,128]{3,2,1,0:T(8,128)S(1)}, f32[2,2,64,128]{3,2,1,0:T(8,128)S(1)}, u32[]{:S(2)}, u32[]{:S(2)}) collective-permute-start(f32[2,2,64,128]{3,2,1,0:T(8,128)S(1)} %get-tuple-element.49), channel_id=1, source_target_pairs={{0,2},{1,3},{2,0},{3,1},{4,6},{5,7},{6,4},{7,5},{8,10},{9,11},{10,... | collective-permute-start | bytes 393224 | tf_op jit(solution)/shard_map/ppermute | solution.py:242
  15.5 6.2 %collective-permute-start.6 = (f32[2,2,64,128]{3,2,1,0:T(8,128)S(1)}, f32[2,2,64,128]{3,2,1,0:T(8,128)S(1)}, u32[]{:S(2)}, u32[]{:S(2)}) collective-permute-start(f32[2,2,64,128]{3,2,1,0:T(8,128)S(1)} %get-tuple-element.50), channel_id=1, source_target_pairs={{0,4},{1,5},{2,6},{3,7},{4,0},{5,1},{6,2},{7,3},{8,12},{9,13},{10,... | collective-permute-start | bytes 393224 | tf_op jit(solution)/shard_map/ppermute | solution.py:242
  15.6 6.6 %collective-permute-start.4 = (f32[2,4,64,128]{3,2,1,0:T(8,128)S(1)}, f32[2,4,64,128]{3,2,1,0:T(8,128)S(1)}, u32[]{:S(2)}, u32[]{:S(2)}) collective-permute-start(f32[2,4,64,128]{3,2,1,0:T(8,128)S(1)} %collective-permute-done.1.refs_2_.second_ref), channel_id=1, source_target_pairs={{0,1},{1,0},{2,3},{3,2},{4,5},{5,4},{6,7},{7,6},{8,9},{9,8},{10,11... | collective-permute-start | bytes 786440 | tf_op jit(solution)/shard_map/ppermute | solution.py:242
  15.8 6.4 %collective-permute-start.3 = (f32[2,4,64,128]{3,2,1,0:T(8,128)S(1)}, f32[2,4,64,128]{3,2,1,0:T(8,128)S(1)}, u32[]{:S(2)}, u32[]{:S(2)}) collective-permute-start(f32[2,4,64,128]{3,2,1,0:T(8,128)S(1)} %collective-permute-done.refs_1_.first_ref), channel_id=1, source_target_pairs={{0,1},{1,0},{2,3},{3,2},{4,5},{5,4},{6,7},{7,6},{8,9},{9,8},{10,11... | collective-permute-start | bytes 786440 | tf_op jit(solution)/shard_map/ppermute | solution.py:242
  18.3 1.1 %copy-start.4 = (bf16[4,256,768]{2,1,0:T(8,128)(2,1)}, bf16[4,256,768]{2,1,0:T(8,128)(2,1)S(1)}, u32[]{:S(2)}) copy-start(bf16[4,256,768]{2,1,0:T(8,128)(2,1)S(1)} %get-tuple-element.66.right_high) | copy-start | bytes 4718596
  19.4 1.2 %copy-start.6 = (bf16[4,256,768]{2,1,0:T(8,128)(2,1)}, bf16[4,256,768]{2,1,0:T(8,128)(2,1)S(1)}, u32[]{:S(2)}) copy-start(bf16[4,256,768]{2,1,0:T(8,128)(2,1)S(1)} %get-tuple-element.67.right_low) | copy-start | bytes 4718596
  20.7 1.0 %copy-start.12 = (f32[256,768]{1,0:T(8,128)}, f32[256,768]{1,0:T(8,128)S(1)}, u32[]{:S(2)}) copy-start(f32[256,768]{1,0:T(8,128)S(1)} %get-tuple-element.68.hop_ref) | copy-start | bytes 2359300
  21.6 1.4 %collective-permute-start.7 = (f32[2,2,64,128]{3,2,1,0:T(8,128)S(1)}, f32[2,2,64,128]{3,2,1,0:T(8,128)S(1)}, u32[]{:S(2)}, u32[]{:S(2)}) collective-permute-start(f32[2,2,64,128]{3,2,1,0:T(8,128)S(1)} %collective-permute-done.5.refs_0_), channel_id=1, source_target_pairs={{0,1},{1,0},{2,3},{3,2},{4,5},{5,4},{6,7},{7,6},{8,9},{9,8},{10,11... | collective-permute-start | bytes 393224 | tf_op jit(solution)/shard_map/ppermute | solution.py:242
  21.9 1.5 %collective-permute-start.8 = (f32[2,2,64,128]{3,2,1,0:T(8,128)S(1)}, f32[2,2,64,128]{3,2,1,0:T(8,128)}, u32[]{:S(2)}, u32[]{:S(2)}) collective-permute-start(f32[2,2,64,128]{3,2,1,0:T(8,128)S(1)} %collective-permute-done.6.refs_1_), channel_id=1, source_target_pairs={{0,1},{1,0},{2,3},{3,2},{4,5},{5,4},{6,7},{7,6},{8,9},{9,8},{10,11... | collective-permute-start | bytes 393224 | tf_op jit(solution)/shard_map/ppermute | solution.py:242
  22.1 1.2 %copy-start.9 = (bf16[4,256,512]{2,1,0:T(8,128)(2,1)S(1)}, bf16[4,256,512]{2,1,0:T(8,128)(2,1)}, u32[]{:S(2)}) copy-start(bf16[4,256,512]{2,1,0:T(8,128)(2,1)} %copy-done.8) | copy-start | bytes 3145732
  22.1 1.4 %copy-start.15 = (f32[256,512]{1,0:T(8,128)S(1)}, f32[256,512]{1,0:T(8,128)}, u32[]{:S(2)}) copy-start(f32[256,512]{1,0:T(8,128)} %copy-done.14) | copy-start | bytes 1572868
  23.5 5.0 %copy-start.1 = (bf16[4,256,768]{2,1,0:T(8,128)(2,1)S(1)}, bf16[4,256,768]{2,1,0:T(8,128)(2,1)}, u32[]{:S(2)}) copy-start(bf16[4,256,768]{2,1,0:T(8,128)(2,1)} %copy-done) | copy-start | bytes 4718596
  23.5 5.0 %copy-start.3 = (bf16[4,256,768]{2,1,0:T(8,128)(2,1)S(1)}, bf16[4,256,768]{2,1,0:T(8,128)(2,1)}, u32[]{:S(2)}) copy-start(bf16[4,256,768]{2,1,0:T(8,128)(2,1)} %copy-done.2) | copy-start | bytes 4718596
  23.5 5.0 %copy-start.11 = (f32[256,768]{1,0:T(8,128)S(1)}, f32[256,768]{1,0:T(8,128)}, u32[]{:S(2)}) copy-start(f32[256,768]{1,0:T(8,128)} %copy-done.10) | copy-start | bytes 2359300
  26.4 7.5 %collective-permute-start.9 = (f32[2,2,64,128]{3,2,1,0:T(8,128)S(1)}, f32[2,2,64,128]{3,2,1,0:T(8,128)S(1)}, u32[]{:S(2)}, u32[]{:S(2)}) collective-permute-start(f32[2,2,64,128]{3,2,1,0:T(8,128)S(1)} %get-tuple-element.54), channel_id=1, source_target_pairs={{0,8},{8,24},{24,16},{16,0},{1,9},{9,25},{25,17},{17,1},{2,10},{10... | collective-permute-start | bytes 393224 | tf_op jit(solution)/shard_map/ppermute | solution.py:319
  28.5 5.4 %copy-start.5 = (bf16[4,256,768]{2,1,0:T(8,128)(2,1)S(1)}, bf16[4,256,768]{2,1,0:T(8,128)(2,1)}, u32[]{:S(2)}) copy-start(bf16[4,256,768]{2,1,0:T(8,128)(2,1)} %copy-done.4) | copy-start | bytes 4718596
  28.5 5.4 %copy-start.7 = (bf16[4,256,768]{2,1,0:T(8,128)(2,1)S(1)}, bf16[4,256,768]{2,1,0:T(8,128)(2,1)}, u32[]{:S(2)}) copy-start(bf16[4,256,768]{2,1,0:T(8,128)(2,1)} %copy-done.6) | copy-start | bytes 4718596
  28.5 5.4 %copy-start.13 = (f32[256,768]{1,0:T(8,128)S(1)}, f32[256,768]{1,0:T(8,128)}, u32[]{:S(2)}) copy-start(f32[256,768]{1,0:T(8,128)} %copy-done.12) | copy-start | bytes 2359300
  31.3 7.9 %collective-permute-start.12 = (f32[2,3,64,128]{3,2,1,0:T(8,128)S(1)}, f32[2,3,64,128]{3,2,1,0:T(8,128)S(1)}, u32[]{:S(2)}, u32[]{:S(2)}) collective-permute-start(f32[2,3,64,128]{3,2,1,0:T(8,128)S(1)} %get-tuple-element.62), channel_id=1, source_target_pairs={{0,8},{8,24},{24,16},{16,0},{1,9},{9,25},{25,17},{17,1},{2,10},{10... | collective-permute-start | bytes 589832 | tf_op jit(solution)/shard_map/ppermute | solution.py:319
  36.7 8.8 %collective-permute-start.15 = (f32[2,3,64,128]{3,2,1,0:T(8,128)S(1)}, f32[2,3,64,128]{3,2,1,0:T(8,128)S(1)}, u32[]{:S(2)}, u32[]{:S(2)}) collective-permute-start(f32[2,3,64,128]{3,2,1,0:T(8,128)S(1)} %get-tuple-element.69), channel_id=1, source_target_pairs={{0,8},{8,24},{24,16},{16,0},{1,9},{9,25},{25,17},{17,1},{2,10},{10... | collective-permute-start | bytes 589832 | tf_op jit(solution)/shard_map/ppermute | solution.py:319
  39.3 10.4 %collective-permute-start.13 = (f32[2,3,64,128]{3,2,1,0:T(8,128)S(1)}, f32[2,3,64,128]{3,2,1,0:T(8,128)S(1)}, u32[]{:S(2)}, u32[]{:S(2)}) collective-permute-start(f32[2,3,64,128]{3,2,1,0:T(8,128)S(1)} %add.20), channel_id=1, source_target_pairs={{0,8},{8,24},{24,16},{16,0},{1,9},{9,25},{25,17},{17,1},{2,10},{10... | collective-permute-start | bytes 589832 | tf_op jit(solution)/shard_map/ppermute | solution.py:319
  45.5 8.8 %collective-permute-start.16 = (f32[2,3,64,128]{3,2,1,0:T(8,128)S(1)}, f32[2,3,64,128]{3,2,1,0:T(8,128)S(1)}, u32[]{:S(2)}, u32[]{:S(2)}) collective-permute-start(f32[2,3,64,128]{3,2,1,0:T(8,128)S(1)} %add.22), channel_id=1, source_target_pairs={{0,8},{8,24},{24,16},{16,0},{1,9},{9,25},{25,17},{17,1},{2,10},{10... | collective-permute-start | bytes 589832 | tf_op jit(solution)/shard_map/ppermute | solution.py:319
  46.0 11.1 %collective-permute-start.10 = (f32[2,2,64,128]{3,2,1,0:T(8,128)S(1)}, f32[2,2,64,128]{3,2,1,0:T(8,128)S(1)}, u32[]{:S(2)}, u32[]{:S(2)}) collective-permute-start(f32[2,2,64,128]{3,2,1,0:T(8,128)S(1)} %add.18), channel_id=1, source_target_pairs={{0,8},{8,24},{24,16},{16,0},{1,9},{9,25},{25,17},{17,1},{2,10},{10... | collective-permute-start | bytes 393224 | tf_op jit(solution)/shard_map/ppermute | solution.py:319
  49.7 16.8 %collective-permute-start.14 = (f32[2,3,64,128]{3,2,1,0:T(8,128)S(1)}, f32[2,3,64,128]{3,2,1,0:T(8,128)S(1)}, u32[]{:S(2)}, u32[]{:S(2)}) collective-permute-start(f32[2,3,64,128]{3,2,1,0:T(8,128)S(1)} %add.21), channel_id=1, source_target_pairs={{0,8},{8,24},{24,16},{16,0},{1,9},{9,25},{25,17},{17,1},{2,10},{10... | collective-permute-start | bytes 589832 | tf_op jit(solution)/shard_map/ppermute | solution.py:319
  54.3 12.2 %collective-permute-start.17 = (f32[2,3,64,128]{3,2,1,0:T(8,128)S(1)}, f32[2,3,64,128]{3,2,1,0:T(8,128)S(1)}, u32[]{:S(2)}, u32[]{:S(2)}) collective-permute-start(f32[2,3,64,128]{3,2,1,0:T(8,128)S(1)} %add.23), channel_id=1, source_target_pairs={{0,8},{8,24},{24,16},{16,0},{1,9},{9,25},{25,17},{17,1},{2,10},{10... | collective-permute-start | bytes 589832 | tf_op jit(solution)/shard_map/ppermute | solution.py:319
  57.1 9.4 %collective-permute-start.11 = (f32[2,2,64,128]{3,2,1,0:T(8,128)S(1)}, f32[2,2,64,128]{3,2,1,0:T(8,128)S(1)}, u32[]{:S(2)}, u32[]{:S(2)}) collective-permute-start(f32[2,2,64,128]{3,2,1,0:T(8,128)S(1)} %add.19), channel_id=1, source_target_pairs={{0,8},{8,24},{24,16},{16,0},{1,9},{9,25},{25,17},{17,1},{2,10},{10... | collective-permute-start | bytes 393224 | tf_op jit(solution)/shard_map/ppermute | solution.py:319

commit v4 on v3

--- a/solution.py
+++ b/solution.py
@@ -15,7 +15,7 @@
 HBM = pl.BlockSpec(memory_space=pltpu.HBM)
 
 
-def sigma_kernel(hist_ref, step_ref, table_hbm, lesser_hbm, greater_hbm, out_ref, lesser, greater, table_ref, sems):
+def sigma_kernel(hist_ref, orow_ref, ocol_ref, step_ref, table_hbm, lesser_hbm, greater_hbm, out_ref, lesser, greater, table_ref, sems):
     slices = lesser.shape[1]
     copies = [
         pltpu.make_async_copy(source, target, sems.at[place])
@@ -185,6 +185,21 @@
     return pltpu.with_memory_space_constraint(x, pltpu.HBM)
 
 
+def add_kernel(left_ref, right_ref, out_ref):
+    out_ref[...] = left_ref[...] + right_ref[...]
+
+
+def add(left, right):
+    return pl.pallas_call(
+        add_kernel,
+        out_shape=pltpu.VMEM(left.shape, left.dtype),
+        in_specs=[VMEM] * 2,
+        out_specs=VMEM,
+        compiler_params=limit(4),
+        name="add",
+    )(in_vmem(left), in_vmem(right))
+
+
 def on_device(
     hist_size, orow_size, ocol_size, lesser_hist, greater_hist, advanced_hist, current_row, adjacency, weight_table, step_index
 ):
@@ -195,7 +210,7 @@
     sigma = pl.pallas_call(
         sigma_kernel,
         out_shape=pltpu.VMEM(block, jnp.float32),
-        in_specs=[SMEM] * 2 + [HBM] * 3,
+        in_specs=[SMEM] * 4 + [HBM] * 3,
         out_specs=VMEM,
         scratch_shapes=[
             pltpu.VMEM(block, jnp.float32),
@@ -205,7 +220,7 @@
         ],
         compiler_params=limit(4),
         name="sigma",
-    )(me[0], step_index, in_hbm(weight_table), in_hbm(lesser_hist), in_hbm(jnp.swapaxes(greater_hist, 2, 3)))
+    )(*me, step_index, in_hbm(weight_table), in_hbm(lesser_hist), in_hbm(jnp.swapaxes(greater_hist, 2, 3)))
 
     short = times // 4
     sizes = [short, (times - short) // 2, times - short - (times - short) // 2]
@@ -320,7 +335,7 @@
             if m == 1:
                 firsts.append(moving)
             if m < hist_size - 1:
-                moving = moving + parts[m]
+                moving = add(moving, parts[m])
         arrived.append(moving)
         own.append(parts[-1])
     return pl.pallas_call(

time: 67.6 us -> 62.4 us (0.923)
  local copies, waits for them, and re-layouts: 7.76 us -> 0 us
  waiting for transfers between devices: 21.7 us -> 23.7 us
  starting transfers between devices: 19.3 us -> 21.2 us
  Pallas kernels: 17.6 us -> 16.5 us
    unnamed x32 -> x0, local copies, waits for them, and re-layouts: 7.76 us -> none
    ppermute x9, waiting for transfers between devices: 0.46 us -> 3.05 us  [moved(): return lax.ppermute(x, ('orow', 'ocol'), pairs)]
    ppermute x9, starting transfers between devices: 6.23 us -> 7.61 us  [moved(): return lax.ppermute(x, ('orow', 'ocol'), pairs)]
    pallas_call x3, Pallas kernels: 8.44 us -> 7.36 us  [on_device(): pl.pallas_call(functools.partial(chunk_kernel, masks, ring), out_shape=ou...]
  transfers between devices with their start and end apart: 18 -> 18, of which waited for: 8 -> 12; matrix products, arithmetic and copies ran while one was open for 0% -> 0% of each run, Pallas kernels for 19% -> 20%
where the time goes in v4:
time: 62.4 us; the launch traced here: 62.2 us
  waiting for transfers between devices  23.7 us (38%)
  starting transfers between devices  21.2 us (34%)
  Pallas kernels  16.5 us (26%)
  between operations  0.75 us (1%)
    ppermute x9, waiting for transfers between devices, on_device(): moving = lax.ppermute(moving, 'hist', pairs)  20.7 us
    ppermute x9, starting transfers between devices, on_device(): moving = lax.ppermute(moving, 'hist', pairs)  13.6 us
    ppermute x9, starting transfers between devices, moved(): return lax.ppermute(x, ('orow', 'ocol'), pairs)  7.61 us
    pallas_call x3, Pallas kernels, on_device(): pl.pallas_call(functools.partial(chunk_kernel, masks, ring), out_shape=ou...  7.36 us
    pallas_call x3, Pallas kernels, history(): pl.pallas_call(functools.partial(history_kernel, sum(sizes[:chunk])), out...  6.31 us
    ppermute x9, waiting for transfers between devices, moved(): return lax.ppermute(x, ('orow', 'ocol'), pairs)  3.05 us
  transfers between devices with their start and end apart: 18, of which 12 were waited for; matrix products, arithmetic and copies ran while one was open for 0% of the time, Pallas kernels for 20%

profile of v4, /device:TPU:0, one launch (start us, length us, event | category | flops | bytes accessed | tf_op | source)
XLA Modules:
  0.0 62.2 jit_solution(14142596880586530406)
XLA Ops:
  0.7 1.1 %sigma.1.refs_0_ = f32[2,4,64,128]{3,2,1,0:T(8,128)S(1)} custom-call(s32[1]{0:T(128)} %bitcast.hist_ref, s32[1]{0:T(128)} %bitcast.1.orow_ref, s32[1]{0:T(128)} %bitcast.2.ocol_ref, s32[1]{0:T(128)S(6)} %copy.12.step_ref, s32[4]{0:T(128)} %table_hbm.1, f32[2,4,64,128]{3,2,1,0:T(8,128)} %lesser_hbm.1, f32[2,4,64,128]{3,2,1,0:T(8,128)} %bitcast.4), custom_call_target="tpu_custom_call" | custom-call | tf_op jit(solution)/shard_map/sigma/pallas_call | solution.py:210
  1.8 3.0 %collective-permute-start.1 = (f32[2,4,64,128]{3,2,1,0:T(8,128)S(1)}, f32[2,4,64,128]{3,2,1,0:T(8,128)S(1)}, u32[]{:S(2)}, u32[]{:S(2)}) collective-permute-start(f32[2,4,64,128]{3,2,1,0:T(8,128)S(1)} %sigma.1.refs_0_), channel_id=1, source_target_pairs={{0,2},{1,3},{2,0},{3,1},{4,6},{5,7},{6,4},{7,5},{8,10},{9,11},{10,... | collective-permute-start | bytes 786440 | tf_op jit(solution)/shard_map/ppermute | solution.py:257
  4.8 1.5 %collective-permute-start = (f32[2,4,64,128]{3,2,1,0:T(8,128)S(1)}, f32[2,4,64,128]{3,2,1,0:T(8,128)S(1)}, u32[]{:S(2)}, u32[]{:S(2)}) collective-permute-start(f32[2,4,64,128]{3,2,1,0:T(8,128)S(1)} %sigma.1.refs_0_), channel_id=1, source_target_pairs={{0,4},{1,5},{2,6},{3,7},{4,0},{5,1},{6,2},{7,3},{8,12},{9,13},{10,... | collective-permute-start | bytes 786440 | tf_op jit(solution)/shard_map/ppermute | solution.py:257
  6.3 1.9 %history_0.1 = (bf16[4,256,512]{2,1,0:T(8,128)(2,1)S(1)}, bf16[4,256,512]{2,1,0:T(8,128)(2,1)S(1)}, f32[256,512]{1,0:T(8,128)S(1)}, f32[2,2,64,128]{3,2,1,0:T(8,128)S(1)}) custom-call(f32[2,4,8,256,128]{4,3,2,1,0:T(8,128)} %advanced_hbm.5, f32[2,8,64,128]{3,2,1,0:T(8,128)} %row_hbm.5, s32[64,256]{1,0:T(8,128)} %adjacency_hbm.5), custom_call_target="tpu_custom_call" | custom-call | bytes 4194304 | tf_op jit(solution)/shard_map/history_0/pallas_call | solution.py:231
  8.2 2.2 %history_1.1 = (bf16[4,256,768]{2,1,0:T(8,128)(2,1)S(1)}, bf16[4,256,768]{2,1,0:T(8,128)(2,1)S(1)}, f32[256,768]{1,0:T(8,128)S(1)}, f32[2,3,64,128]{3,2,1,0:T(8,128)S(1)}) custom-call(f32[2,4,8,256,128]{4,3,2,1,0:T(8,128)} %advanced_hbm.5, f32[2,8,64,128]{3,2,1,0:T(8,128)} %row_hbm.5, s32[64,256]{1,0:T(8,128)} %adjacency_hbm.5), custom_call_target="tpu_custom_call" | custom-call | bytes 4194304 | tf_op jit(solution)/shard_map/history_1/pallas_call | solution.py:231
  10.4 0.7 %collective-permute-done.1.refs_2_.second_ref = f32[2,4,64,128]{3,2,1,0:T(8,128)S(1)} collective-permute-done((f32[2,4,64,128]{3,2,1,0:T(8,128)S(1)}, f32[2,4,64,128]{3,2,1,0:T(8,128)S(1)}, u32[]{:S(2)}, u32[]{:S(2)}) %collective-permute-start.1) | collective-permute-done | bytes 262176 | tf_op jit(solution)/shard_map/ppermute | solution.py:257
  11.1 1.5 %collective-permute-done.refs_1_.first_ref = f32[2,4,64,128]{3,2,1,0:T(8,128)S(1)} collective-permute-done((f32[2,4,64,128]{3,2,1,0:T(8,128)S(1)}, f32[2,4,64,128]{3,2,1,0:T(8,128)S(1)}, u32[]{:S(2)}, u32[]{:S(2)}) %collective-permute-start) | collective-permute-done | bytes 262176 | tf_op jit(solution)/shard_map/ppermute | solution.py:257
  12.6 0.4 collective-permute-start.5
  13.0 1.6 %collective-permute-start.6 = (f32[2,2,64,128]{3,2,1,0:T(8,128)S(1)}, f32[2,2,64,128]{3,2,1,0:T(8,128)S(1)}, u32[]{:S(2)}, u32[]{:S(2)}) collective-permute-start(f32[2,2,64,128]{3,2,1,0:T(8,128)S(1)} %get-tuple-element.50), channel_id=1, source_target_pairs={{0,4},{1,5},{2,6},{3,7},{4,0},{5,1},{6,2},{7,3},{8,12},{9,13},{10,... | collective-permute-start | bytes 393224 | tf_op jit(solution)/shard_map/ppermute | solution.py:257
  14.7 0.0 collective-permute-start.2
  14.7 0.5 collective-permute-start.4
  15.2 0.0 collective-permute-start.3
  15.2 2.2 %history_2.1 = (bf16[4,256,768]{2,1,0:T(8,128)(2,1)S(1)}, bf16[4,256,768]{2,1,0:T(8,128)(2,1)S(1)}, f32[256,768]{1,0:T(8,128)S(1)}, f32[2,3,64,128]{3,2,1,0:T(8,128)S(1)}) custom-call(f32[2,4,8,256,128]{4,3,2,1,0:T(8,128)} %advanced_hbm.5, f32[2,8,64,128]{3,2,1,0:T(8,128)} %row_hbm.5, s32[64,256]{1,0:T(8,128)} %adjacency_hbm.5), custom_call_target="tpu_custom_call" | custom-call | bytes 4194304 | tf_op jit(solution)/shard_map/history_2/pallas_call | solution.py:231
  17.4 0.2 collective-permute-done.5.refs_0_
  17.6 0.4 collective-permute-done.6.refs_1_
  18.0 0.0 collective-permute-start.7
  18.0 0.5 collective-permute-start.8
  18.5 0.0 collective-permute-done.2.refs_3_
  18.5 0.0 collective-permute-done.4.refs_5_
  18.5 0.0 collective-permute-done.3.refs_4_
  18.5 0.7 %assemble.1 = (bf16[4,2,2,4,64,128]{5,4,3,2,1,0:T(8,128)(2,1)S(1)}, bf16[4,2,2,4,64,128]{5,4,3,2,1,0:T(8,128)(2,1)S(1)}, f32[8,128]{1,0:T(8,128)}) custom-call(s32[1]{0:T(128)} %bitcast.1.orow_ref, s32[1]{0:T(128)} %bitcast.2.ocol_ref, f32[2,4,64,128]{3,2,1,0:T(8,128)S(1)} %sigma.1.refs_0_, f32[2,4,64,128]{3,2,1,0:T(8,128)S(1)} %collective-permute-done.refs_1_.first_ref, ...), custom_call_target="tpu_custom_call" | custom-call | bytes 2097152 | tf_op jit(solution)/shard_map/assemble/pallas_call | solution.py:283
  19.2 0.1 collective-permute-done.7.refs_2_
  19.3 0.2 collective-permute-done.8.refs_3_
  19.5 1.9 %products_0.1 = (f32[2,2,64,128]{3,2,1,0:T(8,128)S(1)}, f32[2,2,64,128]{3,2,1,0:T(8,128)S(1)}, f32[2,2,64,128]{3,2,1,0:T(8,128)S(1)}, f32[2,2,64,128]{3,2,1,0:T(...) custom-call(s32[1]{0:T(128)} %bitcast.hist_ref, ...), custom_call_target="tpu_custom_call", output_to_operand_aliasing={{4}: (6, {}), {5}: (7, {})} | custom-call | flops 1610612736 | tf_op jit(solution)/shard_map/products_0/pallas_call | solution.py:311
  21.4 1.8 %collective-permute-start.9 = (f32[2,2,64,128]{3,2,1,0:T(8,128)S(1)}, f32[2,2,64,128]{3,2,1,0:T(8,128)S(1)}, u32[]{:S(2)}, u32[]{:S(2)}) collective-permute-start(f32[2,2,64,128]{3,2,1,0:T(8,128)S(1)} %get-tuple-element.54), channel_id=1, source_target_pairs={{0,8},{8,24},{24,16},{16,0},{1,9},{9,25},{25,17},{17,1},{2,10},{10... | collective-permute-start | bytes 393224 | tf_op jit(solution)/shard_map/ppermute | solution.py:334
  23.2 2.8 %products_1.1 = (f32[2,3,64,128]{3,2,1,0:T(8,128)S(1)}, f32[2,3,64,128]{3,2,1,0:T(8,128)S(1)}, f32[2,3,64,128]{3,2,1,0:T(8,128)S(1)}, f32[2,3,64,128]{3,2,1,0:T(8,128)S(1)}) custom-call(s32[1]{0:T(128)} %bitcast.hist_ref, s32[1]{0:T(128)} %bitcast.1.orow_ref, s32[1]{0:T(128)} %bitcast.2.ocol_ref, bf16[4,256,768]{2,1,0:T(8,128)(2,1)S(1)} %get-tuple-element.57.right_high, ...), custom_call_target="tpu_custom_call" | custom-call | flops 2415919104 | tf_op jit(solution)/shard_map/products_1/pallas_call | solution.py:311
  25.9 2.6 %collective-permute-start.12 = (f32[2,3,64,128]{3,2,1,0:T(8,128)S(1)}, f32[2,3,64,128]{3,2,1,0:T(8,128)S(1)}, u32[]{:S(2)}, u32[]{:S(2)}) collective-permute-start(f32[2,3,64,128]{3,2,1,0:T(8,128)S(1)} %get-tuple-element.62), channel_id=1, source_target_pairs={{0,8},{8,24},{24,16},{16,0},{1,9},{9,25},{25,17},{17,1},{2,10},{10... | collective-permute-start | bytes 589832 | tf_op jit(solution)/shard_map/ppermute | solution.py:334
  28.6 0.0 collective-permute-done.9.left_ref
  28.6 2.8 %products_2.1 = (f32[2,3,64,128]{3,2,1,0:T(8,128)S(1)}, f32[2,3,64,128]{3,2,1,0:T(8,128)S(1)}, f32[2,3,64,128]{3,2,1,0:T(8,128)S(1)}, f32[2,3,64,128]{3,2,1,0:T(8,128)S(1)}) custom-call(s32[1]{0:T(128)} %bitcast.hist_ref, s32[1]{0:T(128)} %bitcast.1.orow_ref, s32[1]{0:T(128)} %bitcast.2.ocol_ref, bf16[4,256,768]{2,1,0:T(8,128)(2,1)S(1)} %get-tuple-element.66.right_high, ...), custom_call_target="tpu_custom_call" | custom-call | flops 2415919104 | tf_op jit(solution)/shard_map/products_2/pallas_call | solution.py:311
  31.3 0.5 collective-permute-start.15
  31.8 2.0 %collective-permute-done.12.left_ref = f32[2,3,64,128]{3,2,1,0:T(8,128)S(1)} collective-permute-done((f32[2,3,64,128]{3,2,1,0:T(8,128)S(1)}, f32[2,3,64,128]{3,2,1,0:T(8,128)S(1)}, u32[]{:S(2)}, u32[]{:S(2)}) %collective-permute-start.12) | collective-permute-done | bytes 196640 | tf_op jit(solution)/shard_map/ppermute | solution.py:334
  33.9 2.5 %collective-permute-start.13 = (f32[2,3,64,128]{3,2,1,0:T(8,128)S(1)}, f32[2,3,64,128]{3,2,1,0:T(8,128)S(1)}, u32[]{:S(2)}, u32[]{:S(2)}) collective-permute-start(f32[2,3,64,128]{3,2,1,0:T(8,128)S(1)} %add.8), channel_id=1, source_target_pairs={{0,8},{8,24},{24,16},{16,0},{1,9},{9,25},{25,17},{17,1},{2,10},{10... | collective-permute-start | bytes 589832 | tf_op jit(solution)/shard_map/ppermute | solution.py:334
  36.4 3.7 %collective-permute-done.15.left_ref = f32[2,3,64,128]{3,2,1,0:T(8,128)S(1)} collective-permute-done((f32[2,3,64,128]{3,2,1,0:T(8,128)S(1)}, f32[2,3,64,128]{3,2,1,0:T(8,128)S(1)}, u32[]{:S(2)}, u32[]{:S(2)}) %collective-permute-start.15) | collective-permute-done | bytes 196640 | tf_op jit(solution)/shard_map/ppermute | solution.py:334
  40.1 0.5 collective-permute-start.16
  40.6 3.4 %collective-permute-start.10 = (f32[2,2,64,128]{3,2,1,0:T(8,128)S(1)}, f32[2,2,64,128]{3,2,1,0:T(8,128)S(1)}, u32[]{:S(2)}, u32[]{:S(2)}) collective-permute-start(f32[2,2,64,128]{3,2,1,0:T(8,128)S(1)} %add.6), channel_id=1, source_target_pairs={{0,8},{8,24},{24,16},{16,0},{1,9},{9,25},{25,17},{17,1},{2,10},{10... | collective-permute-start | bytes 393224 | tf_op jit(solution)/shard_map/ppermute | solution.py:334
  44.1 0.2 collective-permute-done.13.left_ref
  44.3 0.5 collective-permute-start.14
  44.8 4.1 %collective-permute-done.16.left_ref = f32[2,3,64,128]{3,2,1,0:T(8,128)S(1)} collective-permute-done((f32[2,3,64,128]{3,2,1,0:T(8,128)S(1)}, f32[2,3,64,128]{3,2,1,0:T(8,128)S(1)}, u32[]{:S(2)}, u32[]{:S(2)}) %collective-permute-start.16) | collective-permute-done | bytes 196640 | tf_op jit(solution)/shard_map/ppermute | solution.py:334
  48.9 0.5 collective-permute-start.17
  49.4 2.3 %collective-permute-done.10.left_ref = f32[2,2,64,128]{3,2,1,0:T(8,128)S(1)} collective-permute-done((f32[2,2,64,128]{3,2,1,0:T(8,128)S(1)}, f32[2,2,64,128]{3,2,1,0:T(8,128)S(1)}, u32[]{:S(2)}, u32[]{:S(2)}) %collective-permute-start.10) | collective-permute-done | bytes 131104 | tf_op jit(solution)/shard_map/ppermute | solution.py:334
  51.7 1.2 %collective-permute-start.11 = (f32[2,2,64,128]{3,2,1,0:T(8,128)S(1)}, f32[2,2,64,128]{3,2,1,0:T(8,128)S(1)}, u32[]{:S(2)}, u32[]{:S(2)}) collective-permute-start(f32[2,2,64,128]{3,2,1,0:T(8,128)S(1)} %add.7), channel_id=1, source_target_pairs={{0,8},{8,24},{24,16},{16,0},{1,9},{9,25},{25,17},{17,1},{2,10},{10... | collective-permute-start | bytes 393224 | tf_op jit(solution)/shard_map/ppermute | solution.py:334
  52.9 8.4 %collective-permute-done.11.refs_0_ = f32[2,2,64,128]{3,2,1,0:T(8,128)S(1)} collective-permute-done((f32[2,2,64,128]{3,2,1,0:T(8,128)S(1)}, f32[2,2,64,128]{3,2,1,0:T(8,128)S(1)}, u32[]{:S(2)}, u32[]{:S(2)}) %collective-permute-start.11) | collective-permute-done | bytes 131104 | tf_op jit(solution)/shard_map/ppermute | solution.py:334
  61.3 0.0 collective-permute-done.14.refs_1_
  61.3 0.0 collective-permute-done.17.refs_2_
  61.3 0.8 %step.1 = f32[2,8,64,128]{3,2,1,0:T(8,128)} custom-call(f32[2,2,64,128]{3,2,1,0:T(8,128)S(1)} %collective-permute-done.11.refs_0_, f32[2,3,64,128]{3,2,1,0:T(8,128)S(1)} %collective-permute-done.14.refs_1_, f32[2,3,64,128]{3,2,1,0:T(8,128)S(1)} %collective-permute-done.17.refs_2_, f32[2,2,64,128]{3,2,1,0:T(8,128)S(1)} %get-tuple-element.72.refs_3_, ...), custom_call_target="tpu_custom_call" | custom-call | tf_op jit(solution)/shard_map/step/pallas_call | solution.py:341
  (7 shorter events, 0.1 us)
Async XLA Ops:
  1.8 9.3 %collective-permute-start.1 = (f32[2,4,64,128]{3,2,1,0:T(8,128)S(1)}, f32[2,4,64,128]{3,2,1,0:T(8,128)S(1)}, u32[]{:S(2)}, u32[]{:S(2)}) collective-permute-start(f32[2,4,64,128]{3,2,1,0:T(8,128)S(1)} %sigma.1.refs_0_), channel_id=1, source_target_pairs={{0,2},{1,3},{2,0},{3,1},{4,6},{5,7},{6,4},{7,5},{8,10},{9,11},{10,... | collective-permute-start | bytes 786440 | tf_op jit(solution)/shard_map/ppermute | solution.py:257
  4.8 7.8 %collective-permute-start = (f32[2,4,64,128]{3,2,1,0:T(8,128)S(1)}, f32[2,4,64,128]{3,2,1,0:T(8,128)S(1)}, u32[]{:S(2)}, u32[]{:S(2)}) collective-permute-start(f32[2,4,64,128]{3,2,1,0:T(8,128)S(1)} %sigma.1.refs_0_), channel_id=1, source_target_pairs={{0,4},{1,5},{2,6},{3,7},{4,0},{5,1},{6,2},{7,3},{8,12},{9,13},{10,... | collective-permute-start | bytes 786440 | tf_op jit(solution)/shard_map/ppermute | solution.py:257
  12.6 5.0 %collective-permute-start.5 = (f32[2,2,64,128]{3,2,1,0:T(8,128)S(1)}, f32[2,2,64,128]{3,2,1,0:T(8,128)S(1)}, u32[]{:S(2)}, u32[]{:S(2)}) collective-permute-start(f32[2,2,64,128]{3,2,1,0:T(8,128)S(1)} %get-tuple-element.49), channel_id=1, source_target_pairs={{0,2},{1,3},{2,0},{3,1},{4,6},{5,7},{6,4},{7,5},{8,10},{9,11},{10,... | collective-permute-start | bytes 393224 | tf_op jit(solution)/shard_map/ppermute | solution.py:257
  13.0 5.0 %collective-permute-start.6 = (f32[2,2,64,128]{3,2,1,0:T(8,128)S(1)}, f32[2,2,64,128]{3,2,1,0:T(8,128)S(1)}, u32[]{:S(2)}, u32[]{:S(2)}) collective-permute-start(f32[2,2,64,128]{3,2,1,0:T(8,128)S(1)} %get-tuple-element.50), channel_id=1, source_target_pairs={{0,4},{1,5},{2,6},{3,7},{4,0},{5,1},{6,2},{7,3},{8,12},{9,13},{10,... | collective-permute-start | bytes 393224 | tf_op jit(solution)/shard_map/ppermute | solution.py:257
  14.7 3.8 %collective-permute-start.2 = (f32[2,4,64,128]{3,2,1,0:T(8,128)S(1)}, f32[2,4,64,128]{3,2,1,0:T(8,128)S(1)}, u32[]{:S(2)}, u32[]{:S(2)}) collective-permute-start(f32[2,4,64,128]{3,2,1,0:T(8,128)S(1)} %sigma.1.refs_0_), channel_id=1, source_target_pairs={{0,1},{1,0},{2,3},{3,2},{4,5},{5,4},{6,7},{7,6},{8,9},{9,8},{10,11... | collective-permute-start | bytes 786440 | tf_op jit(solution)/shard_map/ppermute | solution.py:257
  14.7 3.8 %collective-permute-start.4 = (f32[2,4,64,128]{3,2,1,0:T(8,128)S(1)}, f32[2,4,64,128]{3,2,1,0:T(8,128)S(1)}, u32[]{:S(2)}, u32[]{:S(2)}) collective-permute-start(f32[2,4,64,128]{3,2,1,0:T(8,128)S(1)} %collective-permute-done.1.refs_2_.second_ref), channel_id=1, source_target_pairs={{0,1},{1,0},{2,3},{3,2},{4,5},{5,4},{6,7},{7,6},{8,9},{9,8},{10,11... | collective-permute-start | bytes 786440 | tf_op jit(solution)/shard_map/ppermute | solution.py:257
  15.2 3.3 %collective-permute-start.3 = (f32[2,4,64,128]{3,2,1,0:T(8,128)S(1)}, f32[2,4,64,128]{3,2,1,0:T(8,128)S(1)}, u32[]{:S(2)}, u32[]{:S(2)}) collective-permute-start(f32[2,4,64,128]{3,2,1,0:T(8,128)S(1)} %collective-permute-done.refs_1_.first_ref), channel_id=1, source_target_pairs={{0,1},{1,0},{2,3},{3,2},{4,5},{5,4},{6,7},{7,6},{8,9},{9,8},{10,11... | collective-permute-start | bytes 786440 | tf_op jit(solution)/shard_map/ppermute | solution.py:257
  18.0 1.3 %collective-permute-start.7 = (f32[2,2,64,128]{3,2,1,0:T(8,128)S(1)}, f32[2,2,64,128]{3,2,1,0:T(8,128)S(1)}, u32[]{:S(2)}, u32[]{:S(2)}) collective-permute-start(f32[2,2,64,128]{3,2,1,0:T(8,128)S(1)} %collective-permute-done.5.refs_0_), channel_id=1, source_target_pairs={{0,1},{1,0},{2,3},{3,2},{4,5},{5,4},{6,7},{7,6},{8,9},{9,8},{10,11... | collective-permute-start | bytes 393224 | tf_op jit(solution)/shard_map/ppermute | solution.py:257
  18.0 1.5 %collective-permute-start.8 = (f32[2,2,64,128]{3,2,1,0:T(8,128)S(1)}, f32[2,2,64,128]{3,2,1,0:T(8,128)S(1)}, u32[]{:S(2)}, u32[]{:S(2)}) collective-permute-start(f32[2,2,64,128]{3,2,1,0:T(8,128)S(1)} %collective-permute-done.6.refs_1_), channel_id=1, source_target_pairs={{0,1},{1,0},{2,3},{3,2},{4,5},{5,4},{6,7},{7,6},{8,9},{9,8},{10,11... | collective-permute-start | bytes 393224 | tf_op jit(solution)/shard_map/ppermute | solution.py:257
  21.4 7.2 %collective-permute-start.9 = (f32[2,2,64,128]{3,2,1,0:T(8,128)S(1)}, f32[2,2,64,128]{3,2,1,0:T(8,128)S(1)}, u32[]{:S(2)}, u32[]{:S(2)}) collective-permute-start(f32[2,2,64,128]{3,2,1,0:T(8,128)S(1)} %get-tuple-element.54), channel_id=1, source_target_pairs={{0,8},{8,24},{24,16},{16,0},{1,9},{9,25},{25,17},{17,1},{2,10},{10... | collective-permute-start | bytes 393224 | tf_op jit(solution)/shard_map/ppermute | solution.py:334
  25.9 7.9 %collective-permute-start.12 = (f32[2,3,64,128]{3,2,1,0:T(8,128)S(1)}, f32[2,3,64,128]{3,2,1,0:T(8,128)S(1)}, u32[]{:S(2)}, u32[]{:S(2)}) collective-permute-start(f32[2,3,64,128]{3,2,1,0:T(8,128)S(1)} %get-tuple-element.62), channel_id=1, source_target_pairs={{0,8},{8,24},{24,16},{16,0},{1,9},{9,25},{25,17},{17,1},{2,10},{10... | collective-permute-start | bytes 589832 | tf_op jit(solution)/shard_map/ppermute | solution.py:334
  31.3 8.8 %collective-permute-start.15 = (f32[2,3,64,128]{3,2,1,0:T(8,128)S(1)}, f32[2,3,64,128]{3,2,1,0:T(8,128)S(1)}, u32[]{:S(2)}, u32[]{:S(2)}) collective-permute-start(f32[2,3,64,128]{3,2,1,0:T(8,128)S(1)} %get-tuple-element.69), channel_id=1, source_target_pairs={{0,8},{8,24},{24,16},{16,0},{1,9},{9,25},{25,17},{17,1},{2,10},{10... | collective-permute-start | bytes 589832 | tf_op jit(solution)/shard_map/ppermute | solution.py:334
  33.9 10.4 %collective-permute-start.13 = (f32[2,3,64,128]{3,2,1,0:T(8,128)S(1)}, f32[2,3,64,128]{3,2,1,0:T(8,128)S(1)}, u32[]{:S(2)}, u32[]{:S(2)}) collective-permute-start(f32[2,3,64,128]{3,2,1,0:T(8,128)S(1)} %add.8), channel_id=1, source_target_pairs={{0,8},{8,24},{24,16},{16,0},{1,9},{9,25},{25,17},{17,1},{2,10},{10... | collective-permute-start | bytes 589832 | tf_op jit(solution)/shard_map/ppermute | solution.py:334
  40.1 8.8 %collective-permute-start.16 = (f32[2,3,64,128]{3,2,1,0:T(8,128)S(1)}, f32[2,3,64,128]{3,2,1,0:T(8,128)S(1)}, u32[]{:S(2)}, u32[]{:S(2)}) collective-permute-start(f32[2,3,64,128]{3,2,1,0:T(8,128)S(1)} %add.10), channel_id=1, source_target_pairs={{0,8},{8,24},{24,16},{16,0},{1,9},{9,25},{25,17},{17,1},{2,10},{10... | collective-permute-start | bytes 589832 | tf_op jit(solution)/shard_map/ppermute | solution.py:334
  40.6 11.1 %collective-permute-start.10 = (f32[2,2,64,128]{3,2,1,0:T(8,128)S(1)}, f32[2,2,64,128]{3,2,1,0:T(8,128)S(1)}, u32[]{:S(2)}, u32[]{:S(2)}) collective-permute-start(f32[2,2,64,128]{3,2,1,0:T(8,128)S(1)} %add.6), channel_id=1, source_target_pairs={{0,8},{8,24},{24,16},{16,0},{1,9},{9,25},{25,17},{17,1},{2,10},{10... | collective-permute-start | bytes 393224 | tf_op jit(solution)/shard_map/ppermute | solution.py:334
  44.3 17.0 %collective-permute-start.14 = (f32[2,3,64,128]{3,2,1,0:T(8,128)S(1)}, f32[2,3,64,128]{3,2,1,0:T(8,128)S(1)}, u32[]{:S(2)}, u32[]{:S(2)}) collective-permute-start(f32[2,3,64,128]{3,2,1,0:T(8,128)S(1)} %add.9), channel_id=1, source_target_pairs={{0,8},{8,24},{24,16},{16,0},{1,9},{9,25},{25,17},{17,1},{2,10},{10... | collective-permute-start | bytes 589832 | tf_op jit(solution)/shard_map/ppermute | solution.py:334
  48.9 12.4 %collective-permute-start.17 = (f32[2,3,64,128]{3,2,1,0:T(8,128)S(1)}, f32[2,3,64,128]{3,2,1,0:T(8,128)S(1)}, u32[]{:S(2)}, u32[]{:S(2)}) collective-permute-start(f32[2,3,64,128]{3,2,1,0:T(8,128)S(1)} %add.11), channel_id=1, source_target_pairs={{0,8},{8,24},{24,16},{16,0},{1,9},{9,25},{25,17},{17,1},{2,10},{10... | collective-permute-start | bytes 589832 | tf_op jit(solution)/shard_map/ppermute | solution.py:334
  51.7 9.6 %collective-permute-start.11 = (f32[2,2,64,128]{3,2,1,0:T(8,128)S(1)}, f32[2,2,64,128]{3,2,1,0:T(8,128)S(1)}, u32[]{:S(2)}, u32[]{:S(2)}) collective-permute-start(f32[2,2,64,128]{3,2,1,0:T(8,128)S(1)} %add.7), channel_id=1, source_target_pairs={{0,8},{8,24},{24,16},{16,0},{1,9},{9,25},{25,17},{17,1},{2,10},{10... | collective-permute-start | bytes 393224 | tf_op jit(solution)/shard_map/ppermute | solution.py:334

commit v5 on v4

--- a/solution.py
+++ b/solution.py
@@ -15,7 +15,7 @@
 HBM = pl.BlockSpec(memory_space=pltpu.HBM)
 
 
-def sigma_kernel(hist_ref, orow_ref, ocol_ref, step_ref, table_hbm, lesser_hbm, greater_hbm, out_ref, lesser, greater, table_ref, sems):
+def sigma_kernel(hist_ref, orow_ref, ocol_ref, step_ref, table_hbm, lesser_hbm, greater_hbm, out_ref, early_ref, late_ref, lesser, greater, table_ref, sems):
     slices = lesser.shape[1]
     copies = [
         pltpu.make_async_copy(source, target, sems.at[place])
@@ -35,8 +35,11 @@
         square_re = a_re * a_re - a_im * a_im
         square_im = 2.0 * a_re * a_im
         scale = coupling_square * weight
-        out_ref[0, s] = scale * (square_re * b_re - square_im * b_im)
-        out_ref[1, s] = scale * (square_re * b_im + square_im * b_re)
+        half = early_ref.shape[1]
+        part_ref = early_ref if s < half else late_ref
+        for part, value in enumerate((square_re * b_re - square_im * b_im, square_re * b_im + square_im * b_re)):
+            out_ref[part, s] = scale * value
+            part_ref[part, s % half] = scale * value
 
 
 def split(x):
@@ -45,7 +48,7 @@
 
 
 def history_kernel(
-    first, advanced_hbm, row_hbm, adjacency_hbm, high_ref, low_ref, hop_ref, row, advanced, adjacency, sems
+    first, order_ref, advanced_hbm, row_hbm, adjacency_hbm, high_ref, low_ref, hop_ref, row, advanced, adjacency, sems
 ):
     slices, each, width = advanced.shape[1], advanced.shape[2], advanced.shape[4]
     near = [
@@ -87,15 +90,17 @@
                 left_low[s, at_orow, part, at_ocol] = low
 
 
-def assemble_kernel(masks, orow_ref, ocol_ref, *refs):
-    assemble(masks, orow_ref[0], ocol_ref[0], refs[:-3], refs[-3], refs[-2])
-    refs[-1][...] = jnp.zeros_like(refs[-1])
-
-
-def halves_kernel(first_ref, second_ref, first_half, second_half):
-    slices = first_half.shape[1]
-    first_half[...] = first_ref[:, :slices]
-    second_half[...] = second_ref[:, slices:]
+def assemble_kernel(masks, orow_ref, ocol_ref, own, own_partner, both, both_partner, left_high, left_low, token):
+    blocks = [own, own_partner, both.at[0], both.at[1], both_partner.at[0], both_partner.at[1]]
+    assemble(masks, orow_ref[0], ocol_ref[0], blocks, left_high, left_low)
+    token[...] = jnp.zeros_like(token)
+
+
+def collect_kernel(a_early, a_late, b_early, b_late, out_ref):
+    half = a_early.shape[1]
+    for place, (early, late) in enumerate(((a_early, a_late), (b_early, b_late))):
+        out_ref[place, :, :half] = early[...]
+        out_ref[place, :, half:] = late[...]
 
 
 def join(halves):
@@ -207,11 +212,12 @@
     block = lesser_hist.shape
     my_hist, my_orow, my_ocol = lax.axis_index("hist"), lax.axis_index("orow"), lax.axis_index("ocol")
     me = [index.reshape(1).astype(jnp.int32) for index in (my_hist, my_orow, my_ocol)]
-    sigma = pl.pallas_call(
+    half_shape = (2, slices // 2) + block[2:]
+    sigma, early, late = pl.pallas_call(
         sigma_kernel,
-        out_shape=pltpu.VMEM(block, jnp.float32),
+        out_shape=[pltpu.VMEM(shape, jnp.float32) for shape in (block, half_shape, half_shape)],
         in_specs=[SMEM] * 4 + [HBM] * 3,
-        out_specs=VMEM,
+        out_specs=[VMEM] * 3,
         scratch_shapes=[
             pltpu.VMEM(block, jnp.float32),
             pltpu.VMEM(block, jnp.float32),
@@ -223,10 +229,10 @@
     )(*me, step_index, in_hbm(weight_table), in_hbm(lesser_hist), in_hbm(jnp.swapaxes(greater_hist, 2, 3)))
 
     short = times // 4
-    sizes = [short, (times - short) // 2, times - short - (times - short) // 2]
+    sizes = [(times - short) // 2, times - short - (times - short) // 2, short]
     chunks = len(sizes)
 
-    def history(chunk):
+    def history(chunk, order):
         each = sizes[chunk]
         return list(pl.pallas_call(
             functools.partial(history_kernel, sum(sizes[:chunk])),
@@ -236,7 +242,7 @@
                 pltpu.VMEM((norb, each * 2 * width), jnp.float32),
                 pltpu.VMEM((2, each) + current_row.shape[2:], jnp.float32),
             ],
-            in_specs=[HBM] * 3,
+            in_specs=[SMEM] + [HBM] * 3,
             out_specs=[VMEM] * 4,
             scratch_shapes=[
                 pltpu.VMEM((2, slices, each, norb, width), jnp.float32),
@@ -246,7 +252,7 @@
             compiler_params=limit(12),
             cost_estimate=pl.CostEstimate(flops=0, bytes_accessed=4 * 1024 * 1024, transcendentals=0),
             name=f"history_{chunk}",
-        )(in_hbm(advanced_hist), in_hbm(current_row), in_hbm(adjacency)))
+        )(order, in_hbm(advanced_hist), in_hbm(current_row), in_hbm(adjacency)))
 
     def moved(x, target):
         pairs = [
@@ -259,38 +265,42 @@
     def over_core(x):
         return moved(x, lambda r, c: (r, c ^ 1))
 
-    histories = [history(chunk) for chunk in range(chunks)]
-    held = {(0, 0): sigma}
-    held[(1, 0)] = moved(sigma, lambda r, c: (r ^ 1, c))
-    held[(0, 2)] = moved(sigma, lambda r, c: (r, c ^ 2))
-    held[(0, 1)] = over_core(sigma)
-    over_orow, over_ocol, *_ = lax.optimization_barrier(
-        (held[(1, 0)], held[(0, 2)], histories[0][3], histories[1][3])
-    )
-    half_shape = (2, slices // 2) + block[2:]
-    halves = pl.pallas_call(
-        halves_kernel,
-        out_shape=[pltpu.VMEM(half_shape, jnp.float32), pltpu.VMEM((2, slices - slices // 2) + block[2:], jnp.float32)],
-        in_specs=[VMEM] * 2,
-        out_specs=[VMEM] * 2,
-        compiler_params=limit(4),
-        name="halves",
-    )(in_vmem(over_orow), in_vmem(over_ocol))
-    late = (moved(halves[0], lambda r, c: (r, c ^ 2)), moved(halves[1], lambda r, c: (r ^ 1, c)))
-    held[(1, 1)] = over_core(held[(1, 0)])
-    held[(0, 3)] = over_core(held[(0, 2)])
+    def over_orow(x):
+        return moved(x, lambda r, c: (r ^ 1, c))
+
+    def over_ocol(x):
+        return moved(x, lambda r, c: (r, c ^ 2))
+
+    orow_early, ocol_late, orow_late, ocol_early = over_orow(early), over_ocol(late), over_orow(late), over_ocol(early)
+    own_partner = over_core(sigma)
+    histories = [history(0, me[0])]
+    far_early, far_late, _ = lax.optimization_barrier((orow_early, ocol_late, histories[0][3]))
+    far = [over_ocol(far_early), over_orow(far_late)]
+    order = lax.optimization_barrier((me[0], far_early, histories[0][3]))[0]
+    histories += [history(chunk, order) for chunk in range(1, chunks)]
+    orow_late, ocol_early, _ = lax.optimization_barrier((orow_late, ocol_early, histories[1][3]))
+    both = pl.pallas_call(
+        collect_kernel,
+        out_shape=pltpu.VMEM((2,) + block, jnp.float32),
+        in_specs=[VMEM] * 4,
+        out_specs=VMEM,
+        compiler_params=limit(4),
+        name="collect",
+    )(*[in_vmem(x) for x in (orow_early, orow_late, ocol_early, ocol_late)])
+    both_partner = over_core(both)
     left_shape = (slices, orow_size, 2, ocol_size) + block[2:]
     *left, token = pl.pallas_call(
-        functools.partial(assemble_kernel, tuple(held)),
+        functools.partial(assemble_kernel, ((0, 0), (0, 1), (1, 0), (0, 2), (1, 1), (0, 3))),
         out_shape=[pltpu.VMEM(left_shape, jnp.bfloat16)] * 2 + [pltpu.VMEM((8, 128), jnp.float32)],
-        in_specs=[SMEM] * 2 + [VMEM] * len(held),
+        in_specs=[SMEM] * 2 + [VMEM] * 4,
         out_specs=[VMEM] * 3,
         compiler_params=limit(4),
         cost_estimate=pl.CostEstimate(flops=0, bytes_accessed=2 * 1024 * 1024, transcendentals=0),
         name="assemble",
-    )(*me[1:], *[in_vmem(x) for x in held.values()])
-    *late, _, _ = lax.optimization_barrier((*late, token, histories[2][3]))
-    late = {(1, 2): late, (1, 3): [over_core(x) for x in late]}
+    )(*me[1:], *[in_vmem(x) for x in (sigma, own_partner, both, both_partner)])
+    *far, _, _ = lax.optimization_barrier((*far, *[h[3] for h in histories[1:]]))
+    far_partner = [over_core(x) for x in far]
+    late = {(1, 2): far, (1, 3): far_partner}
 
     rows = norb // hist_size
     ring = ring_of(hist_size) if hist_size <= 8 else []

time: 62.4 us -> 63.5 us (1.018)
  starting transfers between devices: 21.2 us -> 24 us
  waiting for transfers between devices: 23.7 us -> 22 us
    ppermute x9, waiting for transfers between devices: 20.7 us -> 17.7 us  [on_device(): moving = lax.ppermute(moving, 'hist', pairs)]
    ppermute x9, starting transfers between devices: 13.6 us -> 16.2 us  [on_device(): moving = lax.ppermute(moving, 'hist', pairs)]
    ppermute x9 -> x10, waiting for transfers between devices: 3.05 us -> 4.28 us  [moved(): return lax.ppermute(x, ('orow', 'ocol'), pairs)]
    ppermute x9 -> x10, starting transfers between devices: 7.61 us -> 7.81 us  [moved(): return lax.ppermute(x, ('orow', 'ocol'), pairs)]
  transfers between devices with their start and end apart: 18 -> 19, of which waited for: 12 -> 10; matrix products, arithmetic and copies ran while one was open for 0% -> 0% of each run, Pallas kernels for 20% -> 19%
where the time goes in v5:
time: 63.5 us; the launch traced here: 63.3 us
  starting transfers between devices  24 us (38%)
  waiting for transfers between devices  22 us (35%)
  Pallas kernels  16.5 us (26%)
  between operations  0.79 us (1%)
    ppermute x9, waiting for transfers between devices, on_device(): moving = lax.ppermute(moving, 'hist', pairs)  17.7 us
    ppermute x9, starting transfers between devices, on_device(): moving = lax.ppermute(moving, 'hist', pairs)  16.2 us
    ppermute x10, starting transfers between devices, moved(): return lax.ppermute(x, ('orow', 'ocol'), pairs)  7.81 us
    pallas_call x3, Pallas kernels, on_device(): pl.pallas_call(functools.partial(chunk_kernel, masks, ring), out_shape=ou...  7.37 us
    pallas_call x3, Pallas kernels, history(): pl.pallas_call(functools.partial(history_kernel, sum(sizes[:chunk])), out...  6.3 us
    ppermute x10, waiting for transfers between devices, moved(): return lax.ppermute(x, ('orow', 'ocol'), pairs)  4.28 us
  transfers between devices with their start and end apart: 19, of which 10 were waited for; matrix products, arithmetic and copies ran while one was open for 0% of the time, Pallas kernels for 19%

profile of v5, /device:TPU:0, one launch (start us, length us, event | category | flops | bytes accessed | tf_op | source)
XLA Modules:
  0.0 63.3 jit_solution(7748416197768207242)
XLA Ops:
  0.7 1.1 %sigma.1 = (f32[2,4,64,128]{3,2,1,0:T(8,128)S(1)}, f32[2,2,64,128]{3,2,1,0:T(8,128)S(1)}, f32[2,2,64,128]{3,2,1,0:T(8,128)S(1)}) custom-call(s32[1]{0:T(128)} %bitcast.order_ref.hist_ref, s32[1]{0:T(128)} %bitcast.1.orow_ref, s32[1]{0:T(128)} %bitcast.2.ocol_ref, s32[1]{0:T(128)S(6)} %copy.12.step_ref, s32[4]{0:T(128)} %table_hbm.1, ...), custom_call_target="tpu_custom_call" | custom-call | tf_op jit(solution)/shard_map/sigma/pallas_call | solution.py:216
  1.8 3.0 %collective-permute-start.1 = (f32[2,2,64,128]{3,2,1,0:T(8,128)S(1)}, f32[2,2,64,128]{3,2,1,0:T(8,128)S(1)}, u32[]{:S(2)}, u32[]{:S(2)}) collective-permute-start(f32[2,2,64,128]{3,2,1,0:T(8,128)S(1)} %get-tuple-element.48), channel_id=1, source_target_pairs={{0,4},{1,5},{2,6},{3,7},{4,0},{5,1},{6,2},{7,3},{8,12},{9,13},{10,... | collective-permute-start | bytes 393224 | tf_op jit(solution)/shard_map/ppermute | solution.py:263
  4.8 1.5 %collective-permute-start.4 = (f32[2,2,64,128]{3,2,1,0:T(8,128)S(1)}, f32[2,2,64,128]{3,2,1,0:T(8,128)S(1)}, u32[]{:S(2)}, u32[]{:S(2)}) collective-permute-start(f32[2,2,64,128]{3,2,1,0:T(8,128)S(1)} %get-tuple-element.49), channel_id=1, source_target_pairs={{0,2},{1,3},{2,0},{3,1},{4,6},{5,7},{6,4},{7,5},{8,10},{9,11},{10,... | collective-permute-start | bytes 393224 | tf_op jit(solution)/shard_map/ppermute | solution.py:263
  6.3 0.5 collective-permute-start.3
  6.8 0.1 collective-permute-start.2
  6.9 2.2 %history_0.1 = (bf16[4,256,768]{2,1,0:T(8,128)(2,1)S(1)}, bf16[4,256,768]{2,1,0:T(8,128)(2,1)S(1)}, f32[256,768]{1,0:T(8,128)S(1)}, f32[2,3,64,128]{3,2,1,0:T(8,128)S(1)}) custom-call(s32[1]{0:T(128)} %bitcast.order_ref.hist_ref, f32[2,4,8,256,128]{4,3,2,1,0:T(8,128)} %advanced_hbm.5, f32[2,8,64,128]{3,2,1,0:T(8,128)} %row_hbm.5, s32[64,256]{1,0:T(8,128)} %adjacency_hbm.5), custom_call_target="tpu_custom_call" | custom-call | bytes 4194304 | tf_op jit(solution)/shard_map/history_0/pallas_call | solution.py:237
  9.1 0.0 collective-permute-done.1.a_early
  9.1 2.0 %collective-permute-done.4.b_late = f32[2,2,64,128]{3,2,1,0:T(8,128)S(1)} collective-permute-done((f32[2,2,64,128]{3,2,1,0:T(8,128)S(1)}, f32[2,2,64,128]{3,2,1,0:T(8,128)S(1)}, u32[]{:S(2)}, u32[]{:S(2)}) %collective-permute-start.4) | collective-permute-done | bytes 131104 | tf_op jit(solution)/shard_map/ppermute | solution.py:263
  11.1 2.2 %history_1.1 = (bf16[4,256,768]{2,1,0:T(8,128)(2,1)S(1)}, bf16[4,256,768]{2,1,0:T(8,128)(2,1)S(1)}, f32[256,768]{1,0:T(8,128)S(1)}, f32[2,3,64,128]{3,2,1,0:T(8,128)S(1)}) custom-call(s32[1]{0:T(128)} %bitcast.order_ref.hist_ref, f32[2,4,8,256,128]{4,3,2,1,0:T(8,128)} %advanced_hbm.5, f32[2,8,64,128]{3,2,1,0:T(8,128)} %row_hbm.5, s32[64,256]{1,0:T(8,128)} %adjacency_hbm.5), custom_call_target="tpu_custom_call" | custom-call | bytes 4194304 | tf_op jit(solution)/shard_map/history_1/pallas_call | solution.py:237
  13.4 0.0 collective-permute-done.3.b_early
  13.4 0.0 collective-permute-done.2.a_late
  13.4 0.1 collective-permute-start.5
  13.5 0.2 collective-permute-start.7
  13.7 2.0 %collective-permute-start.6 = (f32[2,2,64,128]{3,2,1,0:T(8,128)S(1)}, f32[2,2,64,128]{3,2,1,0:T(8,128)S(1)}, u32[]{:S(2)}, u32[]{:S(2)}) collective-permute-start(f32[2,2,64,128]{3,2,1,0:T(8,128)S(1)} %collective-permute-done.1.a_early), channel_id=1, source_target_pairs={{0,2},{1,3},{2,0},{3,1},{4,6},{5,7},{6,4},{7,5},{8,10},{9,11},{10,... | collective-permute-start | bytes 393224 | tf_op jit(solution)/shard_map/ppermute | solution.py:263
  15.6 0.0 collective-permute-start
  15.6 1.9 %history_2.1 = (bf16[4,256,512]{2,1,0:T(8,128)(2,1)S(1)}, bf16[4,256,512]{2,1,0:T(8,128)(2,1)S(1)}, f32[256,512]{1,0:T(8,128)S(1)}, f32[2,2,64,128]{3,2,1,0:T(8,128)S(1)}) custom-call(s32[1]{0:T(128)} %bitcast.order_ref.hist_ref, f32[2,4,8,256,128]{4,3,2,1,0:T(8,128)} %advanced_hbm.5, f32[2,8,64,128]{3,2,1,0:T(8,128)} %row_hbm.5, s32[64,256]{1,0:T(8,128)} %adjacency_hbm.5), custom_call_target="tpu_custom_call" | custom-call | bytes 4194304 | tf_op jit(solution)/shard_map/history_2/pallas_call | solution.py:237
  17.5 1.9 %collective-permute-done.7.refs_1_ = f32[2,2,64,128]{3,2,1,0:T(8,128)S(1)} collective-permute-done((f32[2,2,64,128]{3,2,1,0:T(8,128)S(1)}, f32[2,2,64,128]{3,2,1,0:T(8,128)S(1)}, u32[]{:S(2)}, u32[]{:S(2)}) %collective-permute-start.7) | collective-permute-done | bytes 131104 | tf_op jit(solution)/shard_map/ppermute | solution.py:263
  19.4 0.0 collective-permute-done.6.refs_0_
  19.5 0.0 collective-permute-start.8
  19.5 0.5 collective-permute-start.9
  20.0 0.0 collective-permute-done.own_partner
  20.0 0.0 collective-permute-done.5.both_partner
  20.0 0.7 %assemble.1 = (bf16[4,2,2,4,64,128]{5,4,3,2,1,0:T(8,128)(2,1)S(1)}, bf16[4,2,2,4,64,128]{5,4,3,2,1,0:T(8,128)(2,1)S(1)}, f32[8,128]{1,0:T(8,128)}) custom-call(s32[1]{0:T(128)} %bitcast.1.orow_ref, s32[1]{0:T(128)} %bitcast.2.ocol_ref, f32[2,4,64,128]{3,2,1,0:T(8,128)S(1)} %get-tuple-element.47.own, f32[2,4,64,128]{3,2,1,0:T(8,128)S(1)} %collective-permute-done.own_partner, ...), custom_call_target="tpu_custom_call" | custom-call | bytes 2097152 | tf_op jit(solution)/shard_map/assemble/pallas_call | solution.py:292
  20.7 0.1 collective-permute-done.8.refs_2_
  20.8 0.2 collective-permute-done.9.refs_3_
  21.0 2.8 %products_0.1 = (f32[2,3,64,128]{3,2,1,0:T(8,128)S(1)}, f32[2,3,64,128]{3,2,1,0:T(8,128)S(1)}, f32[2,3,64,128]{3,2,1,0:T(8,128)S(1)}, f32[2,3,64,128]{3,2,1,0:T(...) custom-call(s32[1]{0:T(128)} %bitcast.order_ref.hist_ref, ...), custom_call_target="tpu_custom_call", output_to_operand_aliasing={{4}: (6, {}), {5}: (7, {})} | custom-call | flops 2415919104 | tf_op jit(solution)/shard_map/products_0/pallas_call | solution.py:321
  23.8 1.9 %collective-permute-start.10 = (f32[2,3,64,128]{3,2,1,0:T(8,128)S(1)}, f32[2,3,64,128]{3,2,1,0:T(8,128)S(1)}, u32[]{:S(2)}, u32[]{:S(2)}) collective-permute-start(f32[2,3,64,128]{3,2,1,0:T(8,128)S(1)} %get-tuple-element.62), channel_id=1, source_target_pairs={{0,8},{8,24},{24,16},{16,0},{1,9},{9,25},{25,17},{17,1},{2,10},{10... | collective-permute-start | bytes 589832 | tf_op jit(solution)/shard_map/ppermute | solution.py:344
  25.6 2.8 %products_1.1 = (f32[2,3,64,128]{3,2,1,0:T(8,128)S(1)}, f32[2,3,64,128]{3,2,1,0:T(8,128)S(1)}, f32[2,3,64,128]{3,2,1,0:T(8,128)S(1)}, f32[2,3,64,128]{3,2,1,0:T(8,128)S(1)}) custom-call(s32[1]{0:T(128)} %bitcast.order_ref.hist_ref, s32[1]{0:T(128)} %bitcast.1.orow_ref, s32[1]{0:T(128)} %bitcast.2.ocol_ref, ...), custom_call_target="tpu_custom_call" | custom-call | flops 2415919104 | tf_op jit(solution)/shard_map/products_1/pallas_call | solution.py:321
  28.4 2.6 %collective-permute-start.13 = (f32[2,3,64,128]{3,2,1,0:T(8,128)S(1)}, f32[2,3,64,128]{3,2,1,0:T(8,128)S(1)}, u32[]{:S(2)}, u32[]{:S(2)}) collective-permute-start(f32[2,3,64,128]{3,2,1,0:T(8,128)S(1)} %get-tuple-element.70), channel_id=1, source_target_pairs={{0,8},{8,24},{24,16},{16,0},{1,9},{9,25},{25,17},{17,1},{2,10},{10... | collective-permute-start | bytes 589832 | tf_op jit(solution)/shard_map/ppermute | solution.py:344
  31.0 1.0 %collective-permute-done.10.left_ref = f32[2,3,64,128]{3,2,1,0:T(8,128)S(1)} collective-permute-done((f32[2,3,64,128]{3,2,1,0:T(8,128)S(1)}, f32[2,3,64,128]{3,2,1,0:T(8,128)S(1)}, u32[]{:S(2)}, u32[]{:S(2)}) %collective-permute-start.10) | collective-permute-done | bytes 196640 | tf_op jit(solution)/shard_map/ppermute | solution.py:344
  32.0 1.8 %products_2.1 = (f32[2,2,64,128]{3,2,1,0:T(8,128)S(1)}, f32[2,2,64,128]{3,2,1,0:T(8,128)S(1)}, f32[2,2,64,128]{3,2,1,0:T(8,128)S(1)}, f32[2,2,64,128]{3,2,1,0:T(8,128)S(1)}) custom-call(s32[1]{0:T(128)} %bitcast.order_ref.hist_ref, s32[1]{0:T(128)} %bitcast.1.orow_ref, s32[1]{0:T(128)} %bitcast.2.ocol_ref, ...), custom_call_target="tpu_custom_call" | custom-call | flops 1610612736 | tf_op jit(solution)/shard_map/products_2/pallas_call | solution.py:321
  33.9 1.5 %collective-permute-start.16 = (f32[2,2,64,128]{3,2,1,0:T(8,128)S(1)}, f32[2,2,64,128]{3,2,1,0:T(8,128)S(1)}, u32[]{:S(2)}, u32[]{:S(2)}) collective-permute-start(f32[2,2,64,128]{3,2,1,0:T(8,128)S(1)} %get-tuple-element.77), channel_id=1, source_target_pairs={{0,8},{8,24},{24,16},{16,0},{1,9},{9,25},{25,17},{17,1},{2,10},{10... | collective-permute-start | bytes 393224 | tf_op jit(solution)/shard_map/ppermute | solution.py:344
  35.4 3.4 %collective-permute-start.11 = (f32[2,3,64,128]{3,2,1,0:T(8,128)S(1)}, f32[2,3,64,128]{3,2,1,0:T(8,128)S(1)}, u32[]{:S(2)}, u32[]{:S(2)}) collective-permute-start(f32[2,3,64,128]{3,2,1,0:T(8,128)S(1)} %add.6), channel_id=1, source_target_pairs={{0,8},{8,24},{24,16},{16,0},{1,9},{9,25},{25,17},{17,1},{2,10},{10... | collective-permute-start | bytes 589832 | tf_op jit(solution)/shard_map/ppermute | solution.py:344
  38.8 0.0 collective-permute-done.13.left_ref
  38.9 0.1 collective-permute-start.14
  38.9 2.3 %collective-permute-done.16.left_ref = f32[2,2,64,128]{3,2,1,0:T(8,128)S(1)} collective-permute-done((f32[2,2,64,128]{3,2,1,0:T(8,128)S(1)}, f32[2,2,64,128]{3,2,1,0:T(8,128)S(1)}, u32[]{:S(2)}, u32[]{:S(2)}) %collective-permute-start.16) | collective-permute-done | bytes 131104 | tf_op jit(solution)/shard_map/ppermute | solution.py:344
  41.3 1.5 %collective-permute-start.17 = (f32[2,2,64,128]{3,2,1,0:T(8,128)S(1)}, f32[2,2,64,128]{3,2,1,0:T(8,128)S(1)}, u32[]{:S(2)}, u32[]{:S(2)}) collective-permute-start(f32[2,2,64,128]{3,2,1,0:T(8,128)S(1)} %add.10), channel_id=1, source_target_pairs={{0,8},{8,24},{24,16},{16,0},{1,9},{9,25},{25,17},{17,1},{2,10},{10... | collective-permute-start | bytes 393224 | tf_op jit(solution)/shard_map/ppermute | solution.py:344
  42.8 2.7 %collective-permute-done.11.left_ref = f32[2,3,64,128]{3,2,1,0:T(8,128)S(1)} collective-permute-done((f32[2,3,64,128]{3,2,1,0:T(8,128)S(1)}, f32[2,3,64,128]{3,2,1,0:T(8,128)S(1)}, u32[]{:S(2)}, u32[]{:S(2)}) %collective-permute-start.11) | collective-permute-done | bytes 196640 | tf_op jit(solution)/shard_map/ppermute | solution.py:344
  45.5 1.5 %collective-permute-start.12 = (f32[2,3,64,128]{3,2,1,0:T(8,128)S(1)}, f32[2,3,64,128]{3,2,1,0:T(8,128)S(1)}, u32[]{:S(2)}, u32[]{:S(2)}) collective-permute-start(f32[2,3,64,128]{3,2,1,0:T(8,128)S(1)} %add.7), channel_id=1, source_target_pairs={{0,8},{8,24},{24,16},{16,0},{1,9},{9,25},{25,17},{17,1},{2,10},{10... | collective-permute-start | bytes 589832 | tf_op jit(solution)/shard_map/ppermute | solution.py:344
  47.0 2.7 %collective-permute-done.14.left_ref = f32[2,3,64,128]{3,2,1,0:T(8,128)S(1)} collective-permute-done((f32[2,3,64,128]{3,2,1,0:T(8,128)S(1)}, f32[2,3,64,128]{3,2,1,0:T(8,128)S(1)}, u32[]{:S(2)}, u32[]{:S(2)}) %collective-permute-start.14) | collective-permute-done | bytes 196640 | tf_op jit(solution)/shard_map/ppermute | solution.py:344
  49.7 1.5 %collective-permute-start.15 = (f32[2,3,64,128]{3,2,1,0:T(8,128)S(1)}, f32[2,3,64,128]{3,2,1,0:T(8,128)S(1)}, u32[]{:S(2)}, u32[]{:S(2)}) collective-permute-start(f32[2,3,64,128]{3,2,1,0:T(8,128)S(1)} %add.9), channel_id=1, source_target_pairs={{0,8},{8,24},{24,16},{16,0},{1,9},{9,25},{25,17},{17,1},{2,10},{10... | collective-permute-start | bytes 589832 | tf_op jit(solution)/shard_map/ppermute | solution.py:344
  51.2 1.3 %collective-permute-done.17.left_ref = f32[2,2,64,128]{3,2,1,0:T(8,128)S(1)} collective-permute-done((f32[2,2,64,128]{3,2,1,0:T(8,128)S(1)}, f32[2,2,64,128]{3,2,1,0:T(8,128)S(1)}, u32[]{:S(2)}, u32[]{:S(2)}) %collective-permute-start.17) | collective-permute-done | bytes 131104 | tf_op jit(solution)/shard_map/ppermute | solution.py:344
  52.5 2.2 %collective-permute-start.18 = (f32[2,2,64,128]{3,2,1,0:T(8,128)S(1)}, f32[2,2,64,128]{3,2,1,0:T(8,128)S(1)}, u32[]{:S(2)}, u32[]{:S(2)}) collective-permute-start(f32[2,2,64,128]{3,2,1,0:T(8,128)S(1)} %add.11), channel_id=1, source_target_pairs={{0,8},{8,24},{24,16},{16,0},{1,9},{9,25},{25,17},{17,1},{2,10},{10... | collective-permute-start | bytes 393224 | tf_op jit(solution)/shard_map/ppermute | solution.py:344
  54.7 7.8 %collective-permute-done.18.refs_2_ = f32[2,2,64,128]{3,2,1,0:T(8,128)S(1)} collective-permute-done((f32[2,2,64,128]{3,2,1,0:T(8,128)S(1)}, f32[2,2,64,128]{3,2,1,0:T(8,128)S(1)}, u32[]{:S(2)}, u32[]{:S(2)}) %collective-permute-start.18) | collective-permute-done | bytes 131104 | tf_op jit(solution)/shard_map/ppermute | solution.py:344
  62.4 0.0 collective-permute-done.12.refs_0_
  62.4 0.0 collective-permute-done.15.refs_1_
  62.4 0.8 %step.1 = f32[2,8,64,128]{3,2,1,0:T(8,128)} custom-call(f32[2,3,64,128]{3,2,1,0:T(8,128)S(1)} %collective-permute-done.12.refs_0_, f32[2,3,64,128]{3,2,1,0:T(8,128)S(1)} %collective-permute-done.15.refs_1_, f32[2,2,64,128]{3,2,1,0:T(8,128)S(1)} %collective-permute-done.18.refs_2_, f32[2,3,64,128]{3,2,1,0:T(8,128)S(1)} %get-tuple-element.80.refs_3_, ...), custom_call_target="tpu_custom_call" | custom-call | tf_op jit(solution)/shard_map/step/pallas_call | solution.py:351
  (7 shorter events, 0.2 us)
Async XLA Ops:
  1.8 7.3 %collective-permute-start.1 = (f32[2,2,64,128]{3,2,1,0:T(8,128)S(1)}, f32[2,2,64,128]{3,2,1,0:T(8,128)S(1)}, u32[]{:S(2)}, u32[]{:S(2)}) collective-permute-start(f32[2,2,64,128]{3,2,1,0:T(8,128)S(1)} %get-tuple-element.48), channel_id=1, source_target_pairs={{0,4},{1,5},{2,6},{3,7},{4,0},{5,1},{6,2},{7,3},{8,12},{9,13},{10,... | collective-permute-start | bytes 393224 | tf_op jit(solution)/shard_map/ppermute | solution.py:263
  4.8 6.4 %collective-permute-start.4 = (f32[2,2,64,128]{3,2,1,0:T(8,128)S(1)}, f32[2,2,64,128]{3,2,1,0:T(8,128)S(1)}, u32[]{:S(2)}, u32[]{:S(2)}) collective-permute-start(f32[2,2,64,128]{3,2,1,0:T(8,128)S(1)} %get-tuple-element.49), channel_id=1, source_target_pairs={{0,2},{1,3},{2,0},{3,1},{4,6},{5,7},{6,4},{7,5},{8,10},{9,11},{10,... | collective-permute-start | bytes 393224 | tf_op jit(solution)/shard_map/ppermute | solution.py:263
  6.3 7.1 %collective-permute-start.3 = (f32[2,2,64,128]{3,2,1,0:T(8,128)S(1)}, f32[2,2,64,128]{3,2,1,0:T(8,128)S(1)}, u32[]{:S(2)}, u32[]{:S(2)}) collective-permute-start(f32[2,2,64,128]{3,2,1,0:T(8,128)S(1)} %get-tuple-element.48), channel_id=1, source_target_pairs={{0,2},{1,3},{2,0},{3,1},{4,6},{5,7},{6,4},{7,5},{8,10},{9,11},{10,... | collective-permute-start | bytes 393224 | tf_op jit(solution)/shard_map/ppermute | solution.py:263
  6.8 6.6 %collective-permute-start.2 = (f32[2,2,64,128]{3,2,1,0:T(8,128)S(1)}, f32[2,2,64,128]{3,2,1,0:T(8,128)S(1)}, u32[]{:S(2)}, u32[]{:S(2)}) collective-permute-start(f32[2,2,64,128]{3,2,1,0:T(8,128)S(1)} %get-tuple-element.49), channel_id=1, source_target_pairs={{0,4},{1,5},{2,6},{3,7},{4,0},{5,1},{6,2},{7,3},{8,12},{9,13},{10,... | collective-permute-start | bytes 393224 | tf_op jit(solution)/shard_map/ppermute | solution.py:263
  13.4 6.5 %collective-permute-start.5 = (f32[2,2,4,64,128]{4,3,2,1,0:T(8,128)S(1)}, f32[2,2,4,64,128]{4,3,2,1,0:T(8,128)S(1)}, u32[]{:S(2)}, u32[]{:S(2)}) collective-permute-start(f32[2,2,4,64,128]{4,3,2,1,0:T(8,128)S(1)} %collect.1.both), channel_id=1, source_target_pairs={{0,1},{1,0},{2,3},{3,2},{4,5},{5,4},{6,7},{7,6},{8,9},{9,8},{10,11... | collective-permute-start | bytes 1572872 | tf_op jit(solution)/shard_map/ppermute | solution.py:263
  13.5 5.9 %collective-permute-start.7 = (f32[2,2,64,128]{3,2,1,0:T(8,128)S(1)}, f32[2,2,64,128]{3,2,1,0:T(8,128)S(1)}, u32[]{:S(2)}, u32[]{:S(2)}) collective-permute-start(f32[2,2,64,128]{3,2,1,0:T(8,128)S(1)} %collective-permute-done.4.b_late), channel_id=1, source_target_pairs={{0,4},{1,5},{2,6},{3,7},{4,0},{5,1},{6,2},{7,3},{8,12},{9,13},{10,... | collective-permute-start | bytes 393224 | tf_op jit(solution)/shard_map/ppermute | solution.py:263
  13.7 5.8 %collective-permute-start.6 = (f32[2,2,64,128]{3,2,1,0:T(8,128)S(1)}, f32[2,2,64,128]{3,2,1,0:T(8,128)S(1)}, u32[]{:S(2)}, u32[]{:S(2)}) collective-permute-start(f32[2,2,64,128]{3,2,1,0:T(8,128)S(1)} %collective-permute-done.1.a_early), channel_id=1, source_target_pairs={{0,2},{1,3},{2,0},{3,1},{4,6},{5,7},{6,4},{7,5},{8,10},{9,11},{10,... | collective-permute-start | bytes 393224 | tf_op jit(solution)/shard_map/ppermute | solution.py:263
  15.6 4.3 %collective-permute-start = (f32[2,4,64,128]{3,2,1,0:T(8,128)S(1)}, f32[2,4,64,128]{3,2,1,0:T(8,128)S(1)}, u32[]{:S(2)}, u32[]{:S(2)}) collective-permute-start(f32[2,4,64,128]{3,2,1,0:T(8,128)S(1)} %get-tuple-element.47.own), channel_id=1, source_target_pairs={{0,1},{1,0},{2,3},{3,2},{4,5},{5,4},{6,7},{7,6},{8,9},{9,8},{10,11... | collective-permute-start | bytes 786440 | tf_op jit(solution)/shard_map/ppermute | solution.py:263
  19.5 1.3 %collective-permute-start.8 = (f32[2,2,64,128]{3,2,1,0:T(8,128)S(1)}, f32[2,2,64,128]{3,2,1,0:T(8,128)S(1)}, u32[]{:S(2)}, u32[]{:S(2)}) collective-permute-start(f32[2,2,64,128]{3,2,1,0:T(8,128)S(1)} %collective-permute-done.6.refs_0_), channel_id=1, source_target_pairs={{0,1},{1,0},{2,3},{3,2},{4,5},{5,4},{6,7},{7,6},{8,9},{9,8},{10,11... | collective-permute-start | bytes 393224 | tf_op jit(solution)/shard_map/ppermute | solution.py:263
  19.5 1.5 %collective-permute-start.9 = (f32[2,2,64,128]{3,2,1,0:T(8,128)S(1)}, f32[2,2,64,128]{3,2,1,0:T(8,128)S(1)}, u32[]{:S(2)}, u32[]{:S(2)}) collective-permute-start(f32[2,2,64,128]{3,2,1,0:T(8,128)S(1)} %collective-permute-done.7.refs_1_), channel_id=1, source_target_pairs={{0,1},{1,0},{2,3},{3,2},{4,5},{5,4},{6,7},{7,6},{8,9},{9,8},{10,11... | collective-permute-start | bytes 393224 | tf_op jit(solution)/shard_map/ppermute | solution.py:263
  23.8 8.3 %collective-permute-start.10 = (f32[2,3,64,128]{3,2,1,0:T(8,128)S(1)}, f32[2,3,64,128]{3,2,1,0:T(8,128)S(1)}, u32[]{:S(2)}, u32[]{:S(2)}) collective-permute-start(f32[2,3,64,128]{3,2,1,0:T(8,128)S(1)} %get-tuple-element.62), channel_id=1, source_target_pairs={{0,8},{8,24},{24,16},{16,0},{1,9},{9,25},{25,17},{17,1},{2,10},{10... | collective-permute-start | bytes 589832 | tf_op jit(solution)/shard_map/ppermute | solution.py:344
  28.4 10.4 %collective-permute-start.13 = (f32[2,3,64,128]{3,2,1,0:T(8,128)S(1)}, f32[2,3,64,128]{3,2,1,0:T(8,128)S(1)}, u32[]{:S(2)}, u32[]{:S(2)}) collective-permute-start(f32[2,3,64,128]{3,2,1,0:T(8,128)S(1)} %get-tuple-element.70), channel_id=1, source_target_pairs={{0,8},{8,24},{24,16},{16,0},{1,9},{9,25},{25,17},{17,1},{2,10},{10... | collective-permute-start | bytes 589832 | tf_op jit(solution)/shard_map/ppermute | solution.py:344
  33.9 7.4 %collective-permute-start.16 = (f32[2,2,64,128]{3,2,1,0:T(8,128)S(1)}, f32[2,2,64,128]{3,2,1,0:T(8,128)S(1)}, u32[]{:S(2)}, u32[]{:S(2)}) collective-permute-start(f32[2,2,64,128]{3,2,1,0:T(8,128)S(1)} %get-tuple-element.77), channel_id=1, source_target_pairs={{0,8},{8,24},{24,16},{16,0},{1,9},{9,25},{25,17},{17,1},{2,10},{10... | collective-permute-start | bytes 393224 | tf_op jit(solution)/shard_map/ppermute | solution.py:344
  35.4 10.1 %collective-permute-start.11 = (f32[2,3,64,128]{3,2,1,0:T(8,128)S(1)}, f32[2,3,64,128]{3,2,1,0:T(8,128)S(1)}, u32[]{:S(2)}, u32[]{:S(2)}) collective-permute-start(f32[2,3,64,128]{3,2,1,0:T(8,128)S(1)} %add.6), channel_id=1, source_target_pairs={{0,8},{8,24},{24,16},{16,0},{1,9},{9,25},{25,17},{17,1},{2,10},{10... | collective-permute-start | bytes 589832 | tf_op jit(solution)/shard_map/ppermute | solution.py:344
  38.9 10.8 %collective-permute-start.14 = (f32[2,3,64,128]{3,2,1,0:T(8,128)S(1)}, f32[2,3,64,128]{3,2,1,0:T(8,128)S(1)}, u32[]{:S(2)}, u32[]{:S(2)}) collective-permute-start(f32[2,3,64,128]{3,2,1,0:T(8,128)S(1)} %add.8), channel_id=1, source_target_pairs={{0,8},{8,24},{24,16},{16,0},{1,9},{9,25},{25,17},{17,1},{2,10},{10... | collective-permute-start | bytes 589832 | tf_op jit(solution)/shard_map/ppermute | solution.py:344
  41.3 11.2 %collective-permute-start.17 = (f32[2,2,64,128]{3,2,1,0:T(8,128)S(1)}, f32[2,2,64,128]{3,2,1,0:T(8,128)S(1)}, u32[]{:S(2)}, u32[]{:S(2)}) collective-permute-start(f32[2,2,64,128]{3,2,1,0:T(8,128)S(1)} %add.10), channel_id=1, source_target_pairs={{0,8},{8,24},{24,16},{16,0},{1,9},{9,25},{25,17},{17,1},{2,10},{10... | collective-permute-start | bytes 393224 | tf_op jit(solution)/shard_map/ppermute | solution.py:344
  45.5 17.0 %collective-permute-start.12 = (f32[2,3,64,128]{3,2,1,0:T(8,128)S(1)}, f32[2,3,64,128]{3,2,1,0:T(8,128)S(1)}, u32[]{:S(2)}, u32[]{:S(2)}) collective-permute-start(f32[2,3,64,128]{3,2,1,0:T(8,128)S(1)} %add.7), channel_id=1, source_target_pairs={{0,8},{8,24},{24,16},{16,0},{1,9},{9,25},{25,17},{17,1},{2,10},{10... | collective-permute-start | bytes 589832 | tf_op jit(solution)/shard_map/ppermute | solution.py:344
  49.7 12.7 %collective-permute-start.15 = (f32[2,3,64,128]{3,2,1,0:T(8,128)S(1)}, f32[2,3,64,128]{3,2,1,0:T(8,128)S(1)}, u32[]{:S(2)}, u32[]{:S(2)}) collective-permute-start(f32[2,3,64,128]{3,2,1,0:T(8,128)S(1)} %add.9), channel_id=1, source_target_pairs={{0,8},{8,24},{24,16},{16,0},{1,9},{9,25},{25,17},{17,1},{2,10},{10... | collective-permute-start | bytes 589832 | tf_op jit(solution)/shard_map/ppermute | solution.py:344
  52.5 9.9 %collective-permute-start.18 = (f32[2,2,64,128]{3,2,1,0:T(8,128)S(1)}, f32[2,2,64,128]{3,2,1,0:T(8,128)S(1)}, u32[]{:S(2)}, u32[]{:S(2)}) collective-permute-start(f32[2,2,64,128]{3,2,1,0:T(8,128)S(1)} %add.11), channel_id=1, source_target_pairs={{0,8},{8,24},{24,16},{16,0},{1,9},{9,25},{25,17},{17,1},{2,10},{10... | collective-permute-start | bytes 393224 | tf_op jit(solution)/shard_map/ppermute | solution.py:344

commit v6 on v5

--- a/solution.py
+++ b/solution.py
@@ -90,17 +90,11 @@
                 left_low[s, at_orow, part, at_ocol] = low
 
 
-def assemble_kernel(masks, orow_ref, ocol_ref, own, own_partner, both, both_partner, left_high, left_low, token):
-    blocks = [own, own_partner, both.at[0], both.at[1], both_partner.at[0], both_partner.at[1]]
+def assemble_kernel(masks, orow_ref, ocol_ref, own, own_partner, *refs):
+    halves, (left_high, left_low, token) = refs[:-3], refs[-3:]
+    blocks = [own, own_partner] + [join(halves[2 * place : 2 * place + 2]) for place in range(len(halves) // 2)]
     assemble(masks, orow_ref[0], ocol_ref[0], blocks, left_high, left_low)
     token[...] = jnp.zeros_like(token)
-
-
-def collect_kernel(a_early, a_late, b_early, b_late, out_ref):
-    half = a_early.shape[1]
-    for place, (early, late) in enumerate(((a_early, a_late), (b_early, b_late))):
-        out_ref[place, :, :half] = early[...]
-        out_ref[place, :, half:] = late[...]
 
 
 def join(halves):
@@ -250,7 +244,7 @@
                 pltpu.SemaphoreType.DMA((each + 2,)),
             ],
             compiler_params=limit(12),
-            cost_estimate=pl.CostEstimate(flops=0, bytes_accessed=4 * 1024 * 1024, transcendentals=0),
+            cost_estimate=pl.CostEstimate(flops=0, bytes_accessed=64 * 1024, transcendentals=0),
             name=f"history_{chunk}",
         )(order, in_hbm(advanced_hist), in_hbm(current_row), in_hbm(adjacency)))
 
@@ -277,28 +271,20 @@
     far_early, far_late, _ = lax.optimization_barrier((orow_early, ocol_late, histories[0][3]))
     far = [over_ocol(far_early), over_orow(far_late)]
     order = lax.optimization_barrier((me[0], far_early, histories[0][3]))[0]
-    histories += [history(chunk, order) for chunk in range(1, chunks)]
-    orow_late, ocol_early, _ = lax.optimization_barrier((orow_late, ocol_early, histories[1][3]))
-    both = pl.pallas_call(
-        collect_kernel,
-        out_shape=pltpu.VMEM((2,) + block, jnp.float32),
-        in_specs=[VMEM] * 4,
-        out_specs=VMEM,
-        compiler_params=limit(4),
-        name="collect",
-    )(*[in_vmem(x) for x in (orow_early, orow_late, ocol_early, ocol_late)])
-    both_partner = over_core(both)
+    histories.append(history(1, order))
+    orow_partner = [over_core(orow_early), over_core(orow_late)]
+    ocol_partner = [over_core(ocol_early), over_core(ocol_late)]
     left_shape = (slices, orow_size, 2, ocol_size) + block[2:]
     *left, token = pl.pallas_call(
         functools.partial(assemble_kernel, ((0, 0), (0, 1), (1, 0), (0, 2), (1, 1), (0, 3))),
         out_shape=[pltpu.VMEM(left_shape, jnp.bfloat16)] * 2 + [pltpu.VMEM((8, 128), jnp.float32)],
-        in_specs=[SMEM] * 2 + [VMEM] * 4,
+        in_specs=[SMEM] * 2 + [VMEM] * 10,
         out_specs=[VMEM] * 3,
         compiler_params=limit(4),
-        cost_estimate=pl.CostEstimate(flops=0, bytes_accessed=2 * 1024 * 1024, transcendentals=0),
+        cost_estimate=pl.CostEstimate(flops=0, bytes_accessed=64 * 1024, transcendentals=0),
         name="assemble",
-    )(*me[1:], *[in_vmem(x) for x in (sigma, own_partner, both, both_partner)])
-    *far, _, _ = lax.optimization_barrier((*far, *[h[3] for h in histories[1:]]))
+    )(*me[1:], *[in_vmem(x) for x in (sigma, own_partner, orow_early, orow_late, ocol_early, ocol_late, *orow_partner, *ocol_partner)])
+    *far, _ = lax.optimization_barrier((*far, histories[1][3]))
     far_partner = [over_core(x) for x in far]
     late = {(1, 2): far, (1, 3): far_partner}
 
@@ -311,6 +297,8 @@
         else:
             out_shape = [pltpu.VMEM((2, each, norb, width), jnp.float32)]
         count, aliases, masks = len(out_shape), {}, ()
+        if chunk >= 2:
+            histories.append(history(chunk, lax.optimization_barrier((me[0], own[chunk - 1]))[0]))
         after = lax.optimization_barrier((me[0], firsts[chunk - 2]))[0] if chunk >= 2 and ring else me[0]
         operands = [after, *me[1:]] + [in_vmem(x) for x in histories[chunk][:3]] + [in_vmem(x) for x in left]
         if chunk == 0:

time: 63.5 us -> 59.9 us (0.943)
  waiting for transfers between devices: 22 us -> 18.9 us
    ppermute x9, waiting for transfers between devices: 17.7 us -> 15.9 us  [on_device(): moving = lax.ppermute(moving, 'hist', pairs)]
    ppermute x10 -> x13, waiting for transfers between devices: 4.28 us -> 2.95 us  [moved(): return lax.ppermute(x, ('orow', 'ocol'), pairs)]
    ppermute x9, starting transfers between devices: 16.2 us -> 14.9 us  [on_device(): moving = lax.ppermute(moving, 'hist', pairs)]
    ppermute x10 -> x13, starting transfers between devices: 7.81 us -> 8.7 us  [moved(): return lax.ppermute(x, ('orow', 'ocol'), pairs)]
  transfers between devices with their start and end apart: 19 -> 22, of which waited for: 10 -> 10; matrix products, arithmetic and copies ran while one was open for 0% -> 0% of each run, Pallas kernels for 19% -> 20%
where the time goes in v6:
time: 59.9 us; the launch traced here: 59.7 us
  starting transfers between devices  23.6 us (39%)
  waiting for transfers between devices  18.9 us (32%)
  Pallas kernels  16.5 us (28%)
  between operations  0.77 us (1%)
    ppermute x9, waiting for transfers between devices, on_device(): moving = lax.ppermute(moving, 'hist', pairs)  15.9 us
    ppermute x9, starting transfers between devices, on_device(): moving = lax.ppermute(moving, 'hist', pairs)  14.9 us
    ppermute x13, starting transfers between devices, moved(): return lax.ppermute(x, ('orow', 'ocol'), pairs)  8.7 us
    pallas_call x3, Pallas kernels, on_device(): pl.pallas_call(functools.partial(chunk_kernel, masks, ring), out_shape=ou...  7.37 us
    pallas_call x3, Pallas kernels, history(): pl.pallas_call(functools.partial(history_kernel, sum(sizes[:chunk])), out...  6.3 us
    ppermute x13, waiting for transfers between devices, moved(): return lax.ppermute(x, ('orow', 'ocol'), pairs)  2.95 us
  transfers between devices with their start and end apart: 22, of which 10 were waited for; matrix products, arithmetic and copies ran while one was open for 0% of the time, Pallas kernels for 20%

profile of v6, /device:TPU:0, one launch (start us, length us, event | category | flops | bytes accessed | tf_op | source)
XLA Modules:
  0.0 59.7 jit_solution(1914330350353615814)
XLA Ops:
  0.7 1.1 %sigma.1 = (f32[2,4,64,128]{3,2,1,0:T(8,128)S(1)}, f32[2,2,64,128]{3,2,1,0:T(8,128)S(1)}, f32[2,2,64,128]{3,2,1,0:T(8,128)S(1)}) custom-call(s32[1]{0:T(128)} %bitcast.order_ref.hist_ref, s32[1]{0:T(128)} %bitcast.1.orow_ref, s32[1]{0:T(128)} %bitcast.2.ocol_ref, s32[1]{0:T(128)S(6)} %copy.12.step_ref, s32[4]{0:T(128)} %table_hbm.1, ...), custom_call_target="tpu_custom_call" | custom-call | tf_op jit(solution)/shard_map/sigma/pallas_call | solution.py:210
  1.8 3.0 %collective-permute-start.1 = (f32[2,2,64,128]{3,2,1,0:T(8,128)S(1)}, f32[2,2,64,128]{3,2,1,0:T(8,128)S(1)}, u32[]{:S(2)}, u32[]{:S(2)}) collective-permute-start(f32[2,2,64,128]{3,2,1,0:T(8,128)S(1)} %get-tuple-element.47), channel_id=1, source_target_pairs={{0,4},{1,5},{2,6},{3,7},{4,0},{5,1},{6,2},{7,3},{8,12},{9,13},{10,... | collective-permute-start | bytes 393224 | tf_op jit(solution)/shard_map/ppermute | solution.py:257
  4.8 1.5 %collective-permute-start.4 = (f32[2,2,64,128]{3,2,1,0:T(8,128)S(1)}, f32[2,2,64,128]{3,2,1,0:T(8,128)S(1)}, u32[]{:S(2)}, u32[]{:S(2)}) collective-permute-start(f32[2,2,64,128]{3,2,1,0:T(8,128)S(1)} %get-tuple-element.48), channel_id=1, source_target_pairs={{0,2},{1,3},{2,0},{3,1},{4,6},{5,7},{6,4},{7,5},{8,10},{9,11},{10,... | collective-permute-start | bytes 393224 | tf_op jit(solution)/shard_map/ppermute | solution.py:257
  6.3 0.5 collective-permute-start.3
  6.8 0.1 collective-permute-start.2
  6.9 2.2 %history_0.1 = (bf16[4,256,768]{2,1,0:T(8,128)(2,1)S(1)}, bf16[4,256,768]{2,1,0:T(8,128)(2,1)S(1)}, f32[256,768]{1,0:T(8,128)S(1)}, f32[2,3,64,128]{3,2,1,0:T(8,128)S(1)}) custom-call(s32[1]{0:T(128)} %bitcast.order_ref.hist_ref, f32[2,4,8,256,128]{4,3,2,1,0:T(8,128)} %advanced_hbm.5, f32[2,8,64,128]{3,2,1,0:T(8,128)} %row_hbm.5, s32[64,256]{1,0:T(8,128)} %adjacency_hbm.5), custom_call_target="tpu_custom_call" | custom-call | bytes 65536 | tf_op jit(solution)/shard_map/history_0/pallas_call | solution.py:231
  9.1 0.0 collective-permute-done.1.refs_0_
  9.1 2.0 %collective-permute-done.4.refs_3_ = f32[2,2,64,128]{3,2,1,0:T(8,128)S(1)} collective-permute-done((f32[2,2,64,128]{3,2,1,0:T(8,128)S(1)}, f32[2,2,64,128]{3,2,1,0:T(8,128)S(1)}, u32[]{:S(2)}, u32[]{:S(2)}) %collective-permute-start.4) | collective-permute-done | bytes 131104 | tf_op jit(solution)/shard_map/ppermute | solution.py:257
  11.1 0.1 collective-permute-start.10
  11.2 2.0 %collective-permute-start.9 = (f32[2,2,64,128]{3,2,1,0:T(8,128)S(1)}, f32[2,2,64,128]{3,2,1,0:T(8,128)S(1)}, u32[]{:S(2)}, u32[]{:S(2)}) collective-permute-start(f32[2,2,64,128]{3,2,1,0:T(8,128)S(1)} %collective-permute-done.1.refs_0_), channel_id=1, source_target_pairs={{0,2},{1,3},{2,0},{3,1},{4,6},{5,7},{6,4},{7,5},{8,10},{9,11},{10,... | collective-permute-start | bytes 393224 | tf_op jit(solution)/shard_map/ppermute | solution.py:257
  13.2 0.0 collective-permute-done.3.refs_2_
  13.2 0.0 collective-permute-start.7
  13.2 0.5 collective-permute-start
  13.7 0.0 collective-permute-done.2.refs_1_
  13.7 0.0 collective-permute-start.5
  13.7 2.2 %history_1.1 = (bf16[4,256,768]{2,1,0:T(8,128)(2,1)S(1)}, bf16[4,256,768]{2,1,0:T(8,128)(2,1)S(1)}, f32[256,768]{1,0:T(8,128)S(1)}, f32[2,3,64,128]{3,2,1,0:T(8,128)S(1)}) custom-call(s32[1]{0:T(128)} %bitcast.order_ref.hist_ref, f32[2,4,8,256,128]{4,3,2,1,0:T(8,128)} %advanced_hbm.5, f32[2,8,64,128]{3,2,1,0:T(8,128)} %row_hbm.5, s32[64,256]{1,0:T(8,128)} %adjacency_hbm.5), custom_call_target="tpu_custom_call" | custom-call | bytes 65536 | tf_op jit(solution)/shard_map/history_1/pallas_call | solution.py:231
  15.9 0.2 collective-permute-done.10.refs_1_
  16.1 0.4 collective-permute-start.8
  16.5 0.1 collective-permute-start.6
  16.6 0.4 collective-permute-start.11
  17.1 0.1 collective-permute-start.12
  17.1 0.4 collective-permute-done.8.refs_7_
  17.5 0.4 collective-permute-done.6.refs_5_
  17.9 0.0 collective-permute-done.own_partner
  17.9 0.7 %assemble.1 = (bf16[4,2,2,4,64,128]{5,4,3,2,1,0:T(8,128)(2,1)S(1)}, bf16[4,2,2,4,64,128]{5,4,3,2,1,0:T(8,128)(2,1)S(1)}, f32[8,128]{1,0:T(8,128)}) custom-call(s32[1]{0:T(128)} %bitcast.1.orow_ref, s32[1]{0:T(128)} %bitcast.2.ocol_ref, f32[2,4,64,128]{3,2,1,0:T(8,128)S(1)} %get-tuple-element.46.own, f32[2,4,64,128]{3,2,1,0:T(8,128)S(1)} %collective-permute-done.own_partner, ...), custom_call_target="tpu_custom_call" | custom-call | bytes 65536 | tf_op jit(solution)/shard_map/assemble/pallas_call | solution.py:278
  18.6 2.8 %products_0.1 = (f32[2,3,64,128]{3,2,1,0:T(8,128)S(1)}, f32[2,3,64,128]{3,2,1,0:T(8,128)S(1)}, f32[2,3,64,128]{3,2,1,0:T(8,128)S(1)}, f32[2,3,64,128]{3,2,1,0:T(...) custom-call(s32[1]{0:T(128)} %bitcast.order_ref.hist_ref, ...), custom_call_target="tpu_custom_call", output_to_operand_aliasing={{4}: (6, {}), {5}: (7, {})} | custom-call | flops 2415919104 | tf_op jit(solution)/shard_map/products_0/pallas_call | solution.py:309
  21.4 1.7 %collective-permute-start.13 = (f32[2,3,64,128]{3,2,1,0:T(8,128)S(1)}, f32[2,3,64,128]{3,2,1,0:T(8,128)S(1)}, u32[]{:S(2)}, u32[]{:S(2)}) collective-permute-start(f32[2,3,64,128]{3,2,1,0:T(8,128)S(1)} %get-tuple-element.58), channel_id=1, source_target_pairs={{0,8},{8,24},{24,16},{16,0},{1,9},{9,25},{25,17},{17,1},{2,10},{10... | collective-permute-start | bytes 589832 | tf_op jit(solution)/shard_map/ppermute | solution.py:332
  23.1 2.8 %products_1.1 = (f32[2,3,64,128]{3,2,1,0:T(8,128)S(1)}, f32[2,3,64,128]{3,2,1,0:T(8,128)S(1)}, f32[2,3,64,128]{3,2,1,0:T(8,128)S(1)}, f32[2,3,64,128]{3,2,1,0:T(8,128)S(1)}) custom-call(s32[1]{0:T(128)} %bitcast.order_ref.hist_ref, s32[1]{0:T(128)} %bitcast.1.orow_ref, s32[1]{0:T(128)} %bitcast.2.ocol_ref, ...), custom_call_target="tpu_custom_call" | custom-call | flops 2415919104 | tf_op jit(solution)/shard_map/products_1/pallas_call | solution.py:309
  25.9 2.6 %collective-permute-start.16 = (f32[2,3,64,128]{3,2,1,0:T(8,128)S(1)}, f32[2,3,64,128]{3,2,1,0:T(8,128)S(1)}, u32[]{:S(2)}, u32[]{:S(2)}) collective-permute-start(f32[2,3,64,128]{3,2,1,0:T(8,128)S(1)} %get-tuple-element.66), channel_id=1, source_target_pairs={{0,8},{8,24},{24,16},{16,0},{1,9},{9,25},{25,17},{17,1},{2,10},{10... | collective-permute-start | bytes 589832 | tf_op jit(solution)/shard_map/ppermute | solution.py:332
  28.6 1.9 %history_2.1 = (bf16[4,256,512]{2,1,0:T(8,128)(2,1)S(1)}, bf16[4,256,512]{2,1,0:T(8,128)(2,1)S(1)}, f32[256,512]{1,0:T(8,128)S(1)}, f32[2,2,64,128]{3,2,1,0:T(8,128)S(1)}) custom-call(s32[1]{0:T(128)} %bitcast.order_ref.hist_ref, f32[2,4,8,256,128]{4,3,2,1,0:T(8,128)} %advanced_hbm.5, f32[2,8,64,128]{3,2,1,0:T(8,128)} %row_hbm.5, s32[64,256]{1,0:T(8,128)} %adjacency_hbm.5), custom_call_target="tpu_custom_call" | custom-call | bytes 65536 | tf_op jit(solution)/shard_map/history_2/pallas_call | solution.py:231
  30.4 0.0 collective-permute-done.13.left_ref
  30.5 0.6 %collective-permute-start.14 = (f32[2,3,64,128]{3,2,1,0:T(8,128)S(1)}, f32[2,3,64,128]{3,2,1,0:T(8,128)S(1)}, u32[]{:S(2)}, u32[]{:S(2)}) collective-permute-start(f32[2,3,64,128]{3,2,1,0:T(8,128)S(1)} %add.6), channel_id=1, source_target_pairs={{0,8},{8,24},{24,16},{16,0},{1,9},{9,25},{25,17},{17,1},{2,10},{10... | collective-permute-start | bytes 589832 | tf_op jit(solution)/shard_map/ppermute | solution.py:332
  31.1 1.8 %products_2.1 = (f32[2,2,64,128]{3,2,1,0:T(8,128)S(1)}, f32[2,2,64,128]{3,2,1,0:T(8,128)S(1)}, f32[2,2,64,128]{3,2,1,0:T(8,128)S(1)}, f32[2,2,64,128]{3,2,1,0:T(8,128)S(1)}) custom-call(s32[1]{0:T(128)} %bitcast.order_ref.hist_ref, s32[1]{0:T(128)} %bitcast.1.orow_ref, s32[1]{0:T(128)} %bitcast.2.ocol_ref, ...), custom_call_target="tpu_custom_call" | custom-call | flops 1610612736 | tf_op jit(solution)/shard_map/products_2/pallas_call | solution.py:309
  32.9 3.4 %collective-permute-start.19 = (f32[2,2,64,128]{3,2,1,0:T(8,128)S(1)}, f32[2,2,64,128]{3,2,1,0:T(8,128)S(1)}, u32[]{:S(2)}, u32[]{:S(2)}) collective-permute-start(f32[2,2,64,128]{3,2,1,0:T(8,128)S(1)} %get-tuple-element.75), channel_id=1, source_target_pairs={{0,8},{8,24},{24,16},{16,0},{1,9},{9,25},{25,17},{17,1},{2,10},{10... | collective-permute-start | bytes 393224 | tf_op jit(solution)/shard_map/ppermute | solution.py:332
  36.4 0.0 collective-permute-done.16.left_ref
  36.4 0.1 collective-permute-start.17
  36.5 5.6 %collective-permute-done.19.left_ref = f32[2,2,64,128]{3,2,1,0:T(8,128)S(1)} collective-permute-done((f32[2,2,64,128]{3,2,1,0:T(8,128)S(1)}, f32[2,2,64,128]{3,2,1,0:T(8,128)S(1)}, u32[]{:S(2)}, u32[]{:S(2)}) %collective-permute-start.19) | collective-permute-done | bytes 131104 | tf_op jit(solution)/shard_map/ppermute | solution.py:332
  42.1 1.4 %collective-permute-start.20 = (f32[2,2,64,128]{3,2,1,0:T(8,128)S(1)}, f32[2,2,64,128]{3,2,1,0:T(8,128)S(1)}, u32[]{:S(2)}, u32[]{:S(2)}) collective-permute-start(f32[2,2,64,128]{3,2,1,0:T(8,128)S(1)} %add.10), channel_id=1, source_target_pairs={{0,8},{8,24},{24,16},{16,0},{1,9},{9,25},{25,17},{17,1},{2,10},{10... | collective-permute-start | bytes 393224 | tf_op jit(solution)/shard_map/ppermute | solution.py:332
  43.4 0.0 collective-permute-done.14.left_ref
  43.5 2.7 %collective-permute-start.15 = (f32[2,3,64,128]{3,2,1,0:T(8,128)S(1)}, f32[2,3,64,128]{3,2,1,0:T(8,128)S(1)}, u32[]{:S(2)}, u32[]{:S(2)}) collective-permute-start(f32[2,3,64,128]{3,2,1,0:T(8,128)S(1)} %add.7), channel_id=1, source_target_pairs={{0,8},{8,24},{24,16},{16,0},{1,9},{9,25},{25,17},{17,1},{2,10},{10... | collective-permute-start | bytes 589832 | tf_op jit(solution)/shard_map/ppermute | solution.py:332
  46.2 0.1 collective-permute-done.17.left_ref
  46.3 1.4 %collective-permute-start.18 = (f32[2,3,64,128]{3,2,1,0:T(8,128)S(1)}, f32[2,3,64,128]{3,2,1,0:T(8,128)S(1)}, u32[]{:S(2)}, u32[]{:S(2)}) collective-permute-start(f32[2,3,64,128]{3,2,1,0:T(8,128)S(1)} %add.9), channel_id=1, source_target_pairs={{0,8},{8,24},{24,16},{16,0},{1,9},{9,25},{25,17},{17,1},{2,10},{10... | collective-permute-start | bytes 589832 | tf_op jit(solution)/shard_map/ppermute | solution.py:332
  47.7 1.8 %collective-permute-done.20.left_ref = f32[2,2,64,128]{3,2,1,0:T(8,128)S(1)} collective-permute-done((f32[2,2,64,128]{3,2,1,0:T(8,128)S(1)}, f32[2,2,64,128]{3,2,1,0:T(8,128)S(1)}, u32[]{:S(2)}, u32[]{:S(2)}) %collective-permute-start.20) | collective-permute-done | bytes 131104 | tf_op jit(solution)/shard_map/ppermute | solution.py:332
  49.5 1.0 %collective-permute-start.21 = (f32[2,2,64,128]{3,2,1,0:T(8,128)S(1)}, f32[2,2,64,128]{3,2,1,0:T(8,128)S(1)}, u32[]{:S(2)}, u32[]{:S(2)}) collective-permute-start(f32[2,2,64,128]{3,2,1,0:T(8,128)S(1)} %add.11), channel_id=1, source_target_pairs={{0,8},{8,24},{24,16},{16,0},{1,9},{9,25},{25,17},{17,1},{2,10},{10... | collective-permute-start | bytes 393224 | tf_op jit(solution)/shard_map/ppermute | solution.py:332
  50.5 3.2 %collective-permute-done.15.refs_0_ = f32[2,3,64,128]{3,2,1,0:T(8,128)S(1)} collective-permute-done((f32[2,3,64,128]{3,2,1,0:T(8,128)S(1)}, f32[2,3,64,128]{3,2,1,0:T(8,128)S(1)}, u32[]{:S(2)}, u32[]{:S(2)}) %collective-permute-start.15) | collective-permute-done | bytes 196640 | tf_op jit(solution)/shard_map/ppermute | solution.py:332
  53.7 3.8 %collective-permute-done.18.refs_1_ = f32[2,3,64,128]{3,2,1,0:T(8,128)S(1)} collective-permute-done((f32[2,3,64,128]{3,2,1,0:T(8,128)S(1)}, f32[2,3,64,128]{3,2,1,0:T(8,128)S(1)}, u32[]{:S(2)}, u32[]{:S(2)}) %collective-permute-start.18) | collective-permute-done | bytes 196640 | tf_op jit(solution)/shard_map/ppermute | solution.py:332
  57.5 1.4 %collective-permute-done.21.refs_2_ = f32[2,2,64,128]{3,2,1,0:T(8,128)S(1)} collective-permute-done((f32[2,2,64,128]{3,2,1,0:T(8,128)S(1)}, f32[2,2,64,128]{3,2,1,0:T(8,128)S(1)}, u32[]{:S(2)}, u32[]{:S(2)}) %collective-permute-start.21) | collective-permute-done | bytes 131104 | tf_op jit(solution)/shard_map/ppermute | solution.py:332
  58.9 0.8 %step.1 = f32[2,8,64,128]{3,2,1,0:T(8,128)} custom-call(f32[2,3,64,128]{3,2,1,0:T(8,128)S(1)} %collective-permute-done.15.refs_0_, f32[2,3,64,128]{3,2,1,0:T(8,128)S(1)} %collective-permute-done.18.refs_1_, f32[2,2,64,128]{3,2,1,0:T(8,128)S(1)} %collective-permute-done.21.refs_2_, f32[2,3,64,128]{3,2,1,0:T(8,128)S(1)} %get-tuple-element.78.refs_3_, ...), custom_call_target="tpu_custom_call" | custom-call | tf_op jit(solution)/shard_map/step/pallas_call | solution.py:339
  (11 shorter events, 0.1 us)
Async XLA Ops:
  1.8 7.3 %collective-permute-start.1 = (f32[2,2,64,128]{3,2,1,0:T(8,128)S(1)}, f32[2,2,64,128]{3,2,1,0:T(8,128)S(1)}, u32[]{:S(2)}, u32[]{:S(2)}) collective-permute-start(f32[2,2,64,128]{3,2,1,0:T(8,128)S(1)} %get-tuple-element.47), channel_id=1, source_target_pairs={{0,4},{1,5},{2,6},{3,7},{4,0},{5,1},{6,2},{7,3},{8,12},{9,13},{10,... | collective-permute-start | bytes 393224 | tf_op jit(solution)/shard_map/ppermute | solution.py:257
  4.8 6.4 %collective-permute-start.4 = (f32[2,2,64,128]{3,2,1,0:T(8,128)S(1)}, f32[2,2,64,128]{3,2,1,0:T(8,128)S(1)}, u32[]{:S(2)}, u32[]{:S(2)}) collective-permute-start(f32[2,2,64,128]{3,2,1,0:T(8,128)S(1)} %get-tuple-element.48), channel_id=1, source_target_pairs={{0,2},{1,3},{2,0},{3,1},{4,6},{5,7},{6,4},{7,5},{8,10},{9,11},{10,... | collective-permute-start | bytes 393224 | tf_op jit(solution)/shard_map/ppermute | solution.py:257
  6.3 6.9 %collective-permute-start.3 = (f32[2,2,64,128]{3,2,1,0:T(8,128)S(1)}, f32[2,2,64,128]{3,2,1,0:T(8,128)S(1)}, u32[]{:S(2)}, u32[]{:S(2)}) collective-permute-start(f32[2,2,64,128]{3,2,1,0:T(8,128)S(1)} %get-tuple-element.47), channel_id=1, source_target_pairs={{0,2},{1,3},{2,0},{3,1},{4,6},{5,7},{6,4},{7,5},{8,10},{9,11},{10,... | collective-permute-start | bytes 393224 | tf_op jit(solution)/shard_map/ppermute | solution.py:257
  6.8 6.9 %collective-permute-start.2 = (f32[2,2,64,128]{3,2,1,0:T(8,128)S(1)}, f32[2,2,64,128]{3,2,1,0:T(8,128)S(1)}, u32[]{:S(2)}, u32[]{:S(2)}) collective-permute-start(f32[2,2,64,128]{3,2,1,0:T(8,128)S(1)} %get-tuple-element.48), channel_id=1, source_target_pairs={{0,4},{1,5},{2,6},{3,7},{4,0},{5,1},{6,2},{7,3},{8,12},{9,13},{10,... | collective-permute-start | bytes 393224 | tf_op jit(solution)/shard_map/ppermute | solution.py:257
  11.1 5.0 %collective-permute-start.10 = (f32[2,2,64,128]{3,2,1,0:T(8,128)S(1)}, f32[2,2,64,128]{3,2,1,0:T(8,128)S(1)}, u32[]{:S(2)}, u32[]{:S(2)}) collective-permute-start(f32[2,2,64,128]{3,2,1,0:T(8,128)S(1)} %collective-permute-done.4.refs_3_), channel_id=1, source_target_pairs={{0,4},{1,5},{2,6},{3,7},{4,0},{5,1},{6,2},{7,3},{8,12},{9,13},{10,... | collective-permute-start | bytes 393224 | tf_op jit(solution)/shard_map/ppermute | solution.py:257
  11.2 5.3 %collective-permute-start.9 = (f32[2,2,64,128]{3,2,1,0:T(8,128)S(1)}, f32[2,2,64,128]{3,2,1,0:T(8,128)S(1)}, u32[]{:S(2)}, u32[]{:S(2)}) collective-permute-start(f32[2,2,64,128]{3,2,1,0:T(8,128)S(1)} %collective-permute-done.1.refs_0_), channel_id=1, source_target_pairs={{0,2},{1,3},{2,0},{3,1},{4,6},{5,7},{6,4},{7,5},{8,10},{9,11},{10,... | collective-permute-start | bytes 393224 | tf_op jit(solution)/shard_map/ppermute | solution.py:257
  13.2 3.4 %collective-permute-start.7 = (f32[2,2,64,128]{3,2,1,0:T(8,128)S(1)}, f32[2,2,64,128]{3,2,1,0:T(8,128)S(1)}, u32[]{:S(2)}, u32[]{:S(2)}) collective-permute-start(f32[2,2,64,128]{3,2,1,0:T(8,128)S(1)} %collective-permute-done.3.refs_2_), channel_id=1, source_target_pairs={{0,1},{1,0},{2,3},{3,2},{4,5},{5,4},{6,7},{7,6},{8,9},{9,8},{10,11... | collective-permute-start | bytes 393224 | tf_op jit(solution)/shard_map/ppermute | solution.py:257
  13.2 4.7 %collective-permute-start = (f32[2,4,64,128]{3,2,1,0:T(8,128)S(1)}, f32[2,4,64,128]{3,2,1,0:T(8,128)S(1)}, u32[]{:S(2)}, u32[]{:S(2)}) collective-permute-start(f32[2,4,64,128]{3,2,1,0:T(8,128)S(1)} %get-tuple-element.46.own), channel_id=1, source_target_pairs={{0,1},{1,0},{2,3},{3,2},{4,5},{5,4},{6,7},{7,6},{8,9},{9,8},{10,11... | collective-permute-start | bytes 786440 | tf_op jit(solution)/shard_map/ppermute | solution.py:257
  13.7 3.3 %collective-permute-start.5 = (f32[2,2,64,128]{3,2,1,0:T(8,128)S(1)}, f32[2,2,64,128]{3,2,1,0:T(8,128)S(1)}, u32[]{:S(2)}, u32[]{:S(2)}) collective-permute-start(f32[2,2,64,128]{3,2,1,0:T(8,128)S(1)} %collective-permute-done.1.refs_0_), channel_id=1, source_target_pairs={{0,1},{1,0},{2,3},{3,2},{4,5},{5,4},{6,7},{7,6},{8,9},{9,8},{10,11... | collective-permute-start | bytes 393224 | tf_op jit(solution)/shard_map/ppermute | solution.py:257
  16.1 1.4 %collective-permute-start.8 = (f32[2,2,64,128]{3,2,1,0:T(8,128)S(1)}, f32[2,2,64,128]{3,2,1,0:T(8,128)S(1)}, u32[]{:S(2)}, u32[]{:S(2)}) collective-permute-start(f32[2,2,64,128]{3,2,1,0:T(8,128)S(1)} %collective-permute-done.4.refs_3_), channel_id=1, source_target_pairs={{0,1},{1,0},{2,3},{3,2},{4,5},{5,4},{6,7},{7,6},{8,9},{9,8},{10,11... | collective-permute-start | bytes 393224 | tf_op jit(solution)/shard_map/ppermute | solution.py:257
  16.5 1.3 %collective-permute-start.6 = (f32[2,2,64,128]{3,2,1,0:T(8,128)S(1)}, f32[2,2,64,128]{3,2,1,0:T(8,128)S(1)}, u32[]{:S(2)}, u32[]{:S(2)}) collective-permute-start(f32[2,2,64,128]{3,2,1,0:T(8,128)S(1)} %collective-permute-done.2.refs_1_), channel_id=1, source_target_pairs={{0,1},{1,0},{2,3},{3,2},{4,5},{5,4},{6,7},{7,6},{8,9},{9,8},{10,11... | collective-permute-start | bytes 393224 | tf_op jit(solution)/shard_map/ppermute | solution.py:257
  16.6 2.0 %collective-permute-start.11 = (f32[2,2,64,128]{3,2,1,0:T(8,128)S(1)}, f32[2,2,64,128]{3,2,1,0:T(8,128)S(1)}, u32[]{:S(2)}, u32[]{:S(2)}) collective-permute-start(f32[2,2,64,128]{3,2,1,0:T(8,128)S(1)} %collective-permute-done.9.refs_0_), channel_id=1, source_target_pairs={{0,1},{1,0},{2,3},{3,2},{4,5},{5,4},{6,7},{7,6},{8,9},{9,8},{10,11... | collective-permute-start | bytes 393224 | tf_op jit(solution)/shard_map/ppermute | solution.py:257
  17.1 1.6 %collective-permute-start.12 = (f32[2,2,64,128]{3,2,1,0:T(8,128)S(1)}, f32[2,2,64,128]{3,2,1,0:T(8,128)S(1)}, u32[]{:S(2)}, u32[]{:S(2)}) collective-permute-start(f32[2,2,64,128]{3,2,1,0:T(8,128)S(1)} %collective-permute-done.10.refs_1_), channel_id=1, source_target_pairs={{0,1},{1,0},{2,3},{3,2},{4,5},{5,4},{6,7},{7,6},{8,9},{9,8},{10,11... | collective-permute-start | bytes 393224 | tf_op jit(solution)/shard_map/ppermute | solution.py:257
  21.4 9.0 %collective-permute-start.13 = (f32[2,3,64,128]{3,2,1,0:T(8,128)S(1)}, f32[2,3,64,128]{3,2,1,0:T(8,128)S(1)}, u32[]{:S(2)}, u32[]{:S(2)}) collective-permute-start(f32[2,3,64,128]{3,2,1,0:T(8,128)S(1)} %get-tuple-element.58), channel_id=1, source_target_pairs={{0,8},{8,24},{24,16},{16,0},{1,9},{9,25},{25,17},{17,1},{2,10},{10... | collective-permute-start | bytes 589832 | tf_op jit(solution)/shard_map/ppermute | solution.py:332
  25.9 10.4 %collective-permute-start.16 = (f32[2,3,64,128]{3,2,1,0:T(8,128)S(1)}, f32[2,3,64,128]{3,2,1,0:T(8,128)S(1)}, u32[]{:S(2)}, u32[]{:S(2)}) collective-permute-start(f32[2,3,64,128]{3,2,1,0:T(8,128)S(1)} %get-tuple-element.66), channel_id=1, source_target_pairs={{0,8},{8,24},{24,16},{16,0},{1,9},{9,25},{25,17},{17,1},{2,10},{10... | collective-permute-start | bytes 589832 | tf_op jit(solution)/shard_map/ppermute | solution.py:332
  30.5 13.0 %collective-permute-start.14 = (f32[2,3,64,128]{3,2,1,0:T(8,128)S(1)}, f32[2,3,64,128]{3,2,1,0:T(8,128)S(1)}, u32[]{:S(2)}, u32[]{:S(2)}) collective-permute-start(f32[2,3,64,128]{3,2,1,0:T(8,128)S(1)} %add.6), channel_id=1, source_target_pairs={{0,8},{8,24},{24,16},{16,0},{1,9},{9,25},{25,17},{17,1},{2,10},{10... | collective-permute-start | bytes 589832 | tf_op jit(solution)/shard_map/ppermute | solution.py:332
  32.9 9.1 %collective-permute-start.19 = (f32[2,2,64,128]{3,2,1,0:T(8,128)S(1)}, f32[2,2,64,128]{3,2,1,0:T(8,128)S(1)}, u32[]{:S(2)}, u32[]{:S(2)}) collective-permute-start(f32[2,2,64,128]{3,2,1,0:T(8,128)S(1)} %get-tuple-element.75), channel_id=1, source_target_pairs={{0,8},{8,24},{24,16},{16,0},{1,9},{9,25},{25,17},{17,1},{2,10},{10... | collective-permute-start | bytes 393224 | tf_op jit(solution)/shard_map/ppermute | solution.py:332
  36.4 9.9 %collective-permute-start.17 = (f32[2,3,64,128]{3,2,1,0:T(8,128)S(1)}, f32[2,3,64,128]{3,2,1,0:T(8,128)S(1)}, u32[]{:S(2)}, u32[]{:S(2)}) collective-permute-start(f32[2,3,64,128]{3,2,1,0:T(8,128)S(1)} %add.8), channel_id=1, source_target_pairs={{0,8},{8,24},{24,16},{16,0},{1,9},{9,25},{25,17},{17,1},{2,10},{10... | collective-permute-start | bytes 589832 | tf_op jit(solution)/shard_map/ppermute | solution.py:332
  42.1 7.4 %collective-permute-start.20 = (f32[2,2,64,128]{3,2,1,0:T(8,128)S(1)}, f32[2,2,64,128]{3,2,1,0:T(8,128)S(1)}, u32[]{:S(2)}, u32[]{:S(2)}) collective-permute-start(f32[2,2,64,128]{3,2,1,0:T(8,128)S(1)} %add.10), channel_id=1, source_target_pairs={{0,8},{8,24},{24,16},{16,0},{1,9},{9,25},{25,17},{17,1},{2,10},{10... | collective-permute-start | bytes 393224 | tf_op jit(solution)/shard_map/ppermute | solution.py:332
  43.5 10.2 %collective-permute-start.15 = (f32[2,3,64,128]{3,2,1,0:T(8,128)S(1)}, f32[2,3,64,128]{3,2,1,0:T(8,128)S(1)}, u32[]{:S(2)}, u32[]{:S(2)}) collective-permute-start(f32[2,3,64,128]{3,2,1,0:T(8,128)S(1)} %add.7), channel_id=1, source_target_pairs={{0,8},{8,24},{24,16},{16,0},{1,9},{9,25},{25,17},{17,1},{2,10},{10... | collective-permute-start | bytes 589832 | tf_op jit(solution)/shard_map/ppermute | solution.py:332
  46.3 11.2 %collective-permute-start.18 = (f32[2,3,64,128]{3,2,1,0:T(8,128)S(1)}, f32[2,3,64,128]{3,2,1,0:T(8,128)S(1)}, u32[]{:S(2)}, u32[]{:S(2)}) collective-permute-start(f32[2,3,64,128]{3,2,1,0:T(8,128)S(1)} %add.9), channel_id=1, source_target_pairs={{0,8},{8,24},{24,16},{16,0},{1,9},{9,25},{25,17},{17,1},{2,10},{10... | collective-permute-start | bytes 589832 | tf_op jit(solution)/shard_map/ppermute | solution.py:332
  49.5 9.4 %collective-permute-start.21 = (f32[2,2,64,128]{3,2,1,0:T(8,128)S(1)}, f32[2,2,64,128]{3,2,1,0:T(8,128)S(1)}, u32[]{:S(2)}, u32[]{:S(2)}) collective-permute-start(f32[2,2,64,128]{3,2,1,0:T(8,128)S(1)} %add.11), channel_id=1, source_target_pairs={{0,8},{8,24},{24,16},{16,0},{1,9},{9,25},{25,17},{17,1},{2,10},{10... | collective-permute-start | bytes 393224 | tf_op jit(solution)/shard_map/ppermute | solution.py:332

commit v7 on v6

--- a/solution.py
+++ b/solution.py
@@ -223,7 +223,7 @@
     )(*me, step_index, in_hbm(weight_table), in_hbm(lesser_hist), in_hbm(jnp.swapaxes(greater_hist, 2, 3)))
 
     short = times // 4
-    sizes = [(times - short) // 2, times - short - (times - short) // 2, short]
+    sizes = [(times - short) // 2, short, times - short - (times - short) // 2]
     chunks = len(sizes)
 
     def history(chunk, order):

time: 59.9 us -> 65.8 us (1.098)
  waiting for transfers between devices: 18.9 us -> 27.6 us
  starting transfers between devices: 23.6 us -> 20.9 us
    ppermute x9, waiting for transfers between devices: 15.9 us -> 24.5 us  [on_device(): moving = lax.ppermute(moving, 'hist', pairs)]
    ppermute x9, starting transfers between devices: 14.9 us -> 12.2 us  [on_device(): moving = lax.ppermute(moving, 'hist', pairs)]
  transfers between devices with their start and end apart: 22 -> 22, of which waited for: 10 -> 11; matrix products, arithmetic and copies ran while one was open for 0% -> 0% of each run, Pallas kernels for 20% -> 14%
where the time goes in v7:
time: 65.8 us; the launch traced here: 65.7 us
  waiting for transfers between devices  27.6 us (42%)
  starting transfers between devices  20.9 us (32%)
  Pallas kernels  16.5 us (25%)
  between operations  0.76 us (1%)
    ppermute x9, waiting for transfers between devices, on_device(): moving = lax.ppermute(moving, 'hist', pairs)  24.5 us
    ppermute x9, starting transfers between devices, on_device(): moving = lax.ppermute(moving, 'hist', pairs)  12.2 us
    ppermute x13, starting transfers between devices, moved(): return lax.ppermute(x, ('orow', 'ocol'), pairs)  8.66 us
    pallas_call x3, Pallas kernels, on_device(): pl.pallas_call(functools.partial(chunk_kernel, masks, ring), out_shape=ou...  7.37 us
    pallas_call x3, Pallas kernels, history(): pl.pallas_call(functools.partial(history_kernel, sum(sizes[:chunk])), out...  6.31 us
    ppermute x13, waiting for transfers between devices, moved(): return lax.ppermute(x, ('orow', 'ocol'), pairs)  3.1 us
  transfers between devices with their start and end apart: 22, of which 11 were waited for; matrix products, arithmetic and copies ran while one was open for 0% of the time, Pallas kernels for 14%

profile of v7, /device:TPU:0, one launch (start us, length us, event | category | flops | bytes accessed | tf_op | source)
XLA Modules:
  0.0 65.7 jit_solution(1943904805404357976)
XLA Ops:
  0.7 1.1 %sigma.1 = (f32[2,4,64,128]{3,2,1,0:T(8,128)S(1)}, f32[2,2,64,128]{3,2,1,0:T(8,128)S(1)}, f32[2,2,64,128]{3,2,1,0:T(8,128)S(1)}) custom-call(s32[1]{0:T(128)} %bitcast.order_ref.hist_ref, s32[1]{0:T(128)} %bitcast.1.orow_ref, s32[1]{0:T(128)} %bitcast.2.ocol_ref, s32[1]{0:T(128)S(6)} %copy.12.step_ref, s32[4]{0:T(128)} %table_hbm.1, ...), custom_call_target="tpu_custom_call" | custom-call | tf_op jit(solution)/shard_map/sigma/pallas_call | solution.py:210
  1.8 3.0 %collective-permute-start.1 = (f32[2,2,64,128]{3,2,1,0:T(8,128)S(1)}, f32[2,2,64,128]{3,2,1,0:T(8,128)S(1)}, u32[]{:S(2)}, u32[]{:S(2)}) collective-permute-start(f32[2,2,64,128]{3,2,1,0:T(8,128)S(1)} %get-tuple-element.47), channel_id=1, source_target_pairs={{0,4},{1,5},{2,6},{3,7},{4,0},{5,1},{6,2},{7,3},{8,12},{9,13},{10,... | collective-permute-start | bytes 393224 | tf_op jit(solution)/shard_map/ppermute | solution.py:257
  4.8 1.5 %collective-permute-start.4 = (f32[2,2,64,128]{3,2,1,0:T(8,128)S(1)}, f32[2,2,64,128]{3,2,1,0:T(8,128)S(1)}, u32[]{:S(2)}, u32[]{:S(2)}) collective-permute-start(f32[2,2,64,128]{3,2,1,0:T(8,128)S(1)} %get-tuple-element.48), channel_id=1, source_target_pairs={{0,2},{1,3},{2,0},{3,1},{4,6},{5,7},{6,4},{7,5},{8,10},{9,11},{10,... | collective-permute-start | bytes 393224 | tf_op jit(solution)/shard_map/ppermute | solution.py:257
  6.3 0.5 collective-permute-start.3
  6.8 0.1 collective-permute-start.2
  6.9 2.2 %history_0.1 = (bf16[4,256,768]{2,1,0:T(8,128)(2,1)S(1)}, bf16[4,256,768]{2,1,0:T(8,128)(2,1)S(1)}, f32[256,768]{1,0:T(8,128)S(1)}, f32[2,3,64,128]{3,2,1,0:T(8,128)S(1)}) custom-call(s32[1]{0:T(128)} %bitcast.order_ref.hist_ref, f32[2,4,8,256,128]{4,3,2,1,0:T(8,128)} %advanced_hbm.5, f32[2,8,64,128]{3,2,1,0:T(8,128)} %row_hbm.5, s32[64,256]{1,0:T(8,128)} %adjacency_hbm.5), custom_call_target="tpu_custom_call" | custom-call | bytes 65536 | tf_op jit(solution)/shard_map/history_0/pallas_call | solution.py:231
  9.1 0.0 collective-permute-done.1.refs_0_
  9.1 2.0 %collective-permute-done.4.refs_3_ = f32[2,2,64,128]{3,2,1,0:T(8,128)S(1)} collective-permute-done((f32[2,2,64,128]{3,2,1,0:T(8,128)S(1)}, f32[2,2,64,128]{3,2,1,0:T(8,128)S(1)}, u32[]{:S(2)}, u32[]{:S(2)}) %collective-permute-start.4) | collective-permute-done | bytes 131104 | tf_op jit(solution)/shard_map/ppermute | solution.py:257
  11.1 0.1 collective-permute-start.10
  11.2 2.0 %collective-permute-start.9 = (f32[2,2,64,128]{3,2,1,0:T(8,128)S(1)}, f32[2,2,64,128]{3,2,1,0:T(8,128)S(1)}, u32[]{:S(2)}, u32[]{:S(2)}) collective-permute-start(f32[2,2,64,128]{3,2,1,0:T(8,128)S(1)} %collective-permute-done.1.refs_0_), channel_id=1, source_target_pairs={{0,2},{1,3},{2,0},{3,1},{4,6},{5,7},{6,4},{7,5},{8,10},{9,11},{10,... | collective-permute-start | bytes 393224 | tf_op jit(solution)/shard_map/ppermute | solution.py:257
  13.2 0.0 collective-permute-done.3.refs_2_
  13.2 0.0 collective-permute-start.7
  13.2 0.5 collective-permute-start
  13.7 0.0 collective-permute-start.5
  13.7 1.9 %history_1.1 = (bf16[4,256,512]{2,1,0:T(8,128)(2,1)S(1)}, bf16[4,256,512]{2,1,0:T(8,128)(2,1)S(1)}, f32[256,512]{1,0:T(8,128)S(1)}, f32[2,2,64,128]{3,2,1,0:T(8,128)S(1)}) custom-call(s32[1]{0:T(128)} %bitcast.order_ref.hist_ref, f32[2,4,8,256,128]{4,3,2,1,0:T(8,128)} %advanced_hbm.5, f32[2,8,64,128]{3,2,1,0:T(8,128)} %row_hbm.5, s32[64,256]{1,0:T(8,128)} %adjacency_hbm.5), custom_call_target="tpu_custom_call" | custom-call | bytes 65536 | tf_op jit(solution)/shard_map/history_1/pallas_call | solution.py:231
  15.6 0.5 collective-permute-done.10.refs_1_
  16.1 0.1 collective-permute-start.8
  16.2 0.0 collective-permute-done.9.refs_0_
  16.2 0.4 collective-permute-start.6
  16.6 0.1 collective-permute-start.11
  16.7 0.0 collective-permute-done.5.refs_4_
  16.7 0.4 collective-permute-start.12
  17.1 0.3 collective-permute-done.8.refs_7_
  17.5 0.2 collective-permute-done.6.refs_5_
  17.7 0.7 %assemble.1 = (bf16[4,2,2,4,64,128]{5,4,3,2,1,0:T(8,128)(2,1)S(1)}, bf16[4,2,2,4,64,128]{5,4,3,2,1,0:T(8,128)(2,1)S(1)}, f32[8,128]{1,0:T(8,128)}) custom-call(s32[1]{0:T(128)} %bitcast.1.orow_ref, s32[1]{0:T(128)} %bitcast.2.ocol_ref, f32[2,4,64,128]{3,2,1,0:T(8,128)S(1)} %get-tuple-element.46.own, f32[2,4,64,128]{3,2,1,0:T(8,128)S(1)} %collective-permute-done.own_partner, ...), custom_call_target="tpu_custom_call" | custom-call | bytes 65536 | tf_op jit(solution)/shard_map/assemble/pallas_call | solution.py:278
  18.4 0.0 collective-permute-done.11.refs_2_
  18.4 0.0 collective-permute-done.12.refs_3_
  18.4 2.8 %products_0.1 = (f32[2,3,64,128]{3,2,1,0:T(8,128)S(1)}, f32[2,3,64,128]{3,2,1,0:T(8,128)S(1)}, f32[2,3,64,128]{3,2,1,0:T(8,128)S(1)}, f32[2,3,64,128]{3,2,1,0:T(...) custom-call(s32[1]{0:T(128)} %bitcast.order_ref.hist_ref, ...), custom_call_target="tpu_custom_call", output_to_operand_aliasing={{4}: (6, {}), {5}: (7, {})} | custom-call | flops 2415919104 | tf_op jit(solution)/shard_map/products_0/pallas_call | solution.py:309
  21.2 2.0 %collective-permute-start.13 = (f32[2,3,64,128]{3,2,1,0:T(8,128)S(1)}, f32[2,3,64,128]{3,2,1,0:T(8,128)S(1)}, u32[]{:S(2)}, u32[]{:S(2)}) collective-permute-start(f32[2,3,64,128]{3,2,1,0:T(8,128)S(1)} %get-tuple-element.58), channel_id=1, source_target_pairs={{0,8},{8,24},{24,16},{16,0},{1,9},{9,25},{25,17},{17,1},{2,10},{10... | collective-permute-start | bytes 589832 | tf_op jit(solution)/shard_map/ppermute | solution.py:332
  23.1 1.8 %products_1.1 = (f32[2,2,64,128]{3,2,1,0:T(8,128)S(1)}, f32[2,2,64,128]{3,2,1,0:T(8,128)S(1)}, f32[2,2,64,128]{3,2,1,0:T(8,128)S(1)}, f32[2,2,64,128]{3,2,1,0:T(8,128)S(1)}) custom-call(s32[1]{0:T(128)} %bitcast.order_ref.hist_ref, s32[1]{0:T(128)} %bitcast.1.orow_ref, s32[1]{0:T(128)} %bitcast.2.ocol_ref, ...), custom_call_target="tpu_custom_call" | custom-call | flops 1610612736 | tf_op jit(solution)/shard_map/products_1/pallas_call | solution.py:309
  25.0 2.2 %history_2.1 = (bf16[4,256,768]{2,1,0:T(8,128)(2,1)S(1)}, bf16[4,256,768]{2,1,0:T(8,128)(2,1)S(1)}, f32[256,768]{1,0:T(8,128)S(1)}, f32[2,3,64,128]{3,2,1,0:T(8,128)S(1)}) custom-call(s32[1]{0:T(128)} %bitcast.order_ref.hist_ref, f32[2,4,8,256,128]{4,3,2,1,0:T(8,128)} %advanced_hbm.5, f32[2,8,64,128]{3,2,1,0:T(8,128)} %row_hbm.5, s32[64,256]{1,0:T(8,128)} %adjacency_hbm.5), custom_call_target="tpu_custom_call" | custom-call | bytes 65536 | tf_op jit(solution)/shard_map/history_2/pallas_call | solution.py:231
  27.2 2.1 %collective-permute-done.13.left_ref = f32[2,3,64,128]{3,2,1,0:T(8,128)S(1)} collective-permute-done((f32[2,3,64,128]{3,2,1,0:T(8,128)S(1)}, f32[2,3,64,128]{3,2,1,0:T(8,128)S(1)}, u32[]{:S(2)}, u32[]{:S(2)}) %collective-permute-start.13) | collective-permute-done | bytes 196640 | tf_op jit(solution)/shard_map/ppermute | solution.py:332
  29.4 2.8 %products_2.1 = (f32[2,3,64,128]{3,2,1,0:T(8,128)S(1)}, f32[2,3,64,128]{3,2,1,0:T(8,128)S(1)}, f32[2,3,64,128]{3,2,1,0:T(8,128)S(1)}, f32[2,3,64,128]{3,2,1,0:T(8,128)S(1)}) custom-call(s32[1]{0:T(128)} %bitcast.order_ref.hist_ref, s32[1]{0:T(128)} %bitcast.1.orow_ref, s32[1]{0:T(128)} %bitcast.2.ocol_ref, ...), custom_call_target="tpu_custom_call" | custom-call | flops 2415919104 | tf_op jit(solution)/shard_map/products_2/pallas_call | solution.py:309
  32.1 0.9 %collective-permute-start.19 = (f32[2,3,64,128]{3,2,1,0:T(8,128)S(1)}, f32[2,3,64,128]{3,2,1,0:T(8,128)S(1)}, u32[]{:S(2)}, u32[]{:S(2)}) collective-permute-start(f32[2,3,64,128]{3,2,1,0:T(8,128)S(1)} %get-tuple-element.75), channel_id=1, source_target_pairs={{0,8},{8,24},{24,16},{16,0},{1,9},{9,25},{25,17},{17,1},{2,10},{10... | collective-permute-start | bytes 589832 | tf_op jit(solution)/shard_map/ppermute | solution.py:332
  33.0 3.4 %collective-permute-start.16 = (f32[2,2,64,128]{3,2,1,0:T(8,128)S(1)}, f32[2,2,64,128]{3,2,1,0:T(8,128)S(1)}, u32[]{:S(2)}, u32[]{:S(2)}) collective-permute-start(f32[2,2,64,128]{3,2,1,0:T(8,128)S(1)} %get-tuple-element.66), channel_id=1, source_target_pairs={{0,8},{8,24},{24,16},{16,0},{1,9},{9,25},{25,17},{17,1},{2,10},{10... | collective-permute-start | bytes 393224 | tf_op jit(solution)/shard_map/ppermute | solution.py:332
  36.4 0.1 collective-permute-start.14
  36.5 4.4 %collective-permute-done.19.left_ref = f32[2,3,64,128]{3,2,1,0:T(8,128)S(1)} collective-permute-done((f32[2,3,64,128]{3,2,1,0:T(8,128)S(1)}, f32[2,3,64,128]{3,2,1,0:T(8,128)S(1)}, u32[]{:S(2)}, u32[]{:S(2)}) %collective-permute-start.19) | collective-permute-done | bytes 196640 | tf_op jit(solution)/shard_map/ppermute | solution.py:332
  40.9 0.9 %collective-permute-start.20 = (f32[2,3,64,128]{3,2,1,0:T(8,128)S(1)}, f32[2,3,64,128]{3,2,1,0:T(8,128)S(1)}, u32[]{:S(2)}, u32[]{:S(2)}) collective-permute-start(f32[2,3,64,128]{3,2,1,0:T(8,128)S(1)} %add.10), channel_id=1, source_target_pairs={{0,8},{8,24},{24,16},{16,0},{1,9},{9,25},{25,17},{17,1},{2,10},{10... | collective-permute-start | bytes 589832 | tf_op jit(solution)/shard_map/ppermute | solution.py:332
  41.8 1.9 %collective-permute-done.16.left_ref = f32[2,2,64,128]{3,2,1,0:T(8,128)S(1)} collective-permute-done((f32[2,2,64,128]{3,2,1,0:T(8,128)S(1)}, f32[2,2,64,128]{3,2,1,0:T(8,128)S(1)}, u32[]{:S(2)}, u32[]{:S(2)}) %collective-permute-start.16) | collective-permute-done | bytes 131104 | tf_op jit(solution)/shard_map/ppermute | solution.py:332
  43.7 1.6 %collective-permute-start.17 = (f32[2,2,64,128]{3,2,1,0:T(8,128)S(1)}, f32[2,2,64,128]{3,2,1,0:T(8,128)S(1)}, u32[]{:S(2)}, u32[]{:S(2)}) collective-permute-start(f32[2,2,64,128]{3,2,1,0:T(8,128)S(1)} %add.8), channel_id=1, source_target_pairs={{0,8},{8,24},{24,16},{16,0},{1,9},{9,25},{25,17},{17,1},{2,10},{10... | collective-permute-start | bytes 393224 | tf_op jit(solution)/shard_map/ppermute | solution.py:332
  45.3 2.6 %collective-permute-done.14.left_ref = f32[2,3,64,128]{3,2,1,0:T(8,128)S(1)} collective-permute-done((f32[2,3,64,128]{3,2,1,0:T(8,128)S(1)}, f32[2,3,64,128]{3,2,1,0:T(8,128)S(1)}, u32[]{:S(2)}, u32[]{:S(2)}) %collective-permute-start.14) | collective-permute-done | bytes 196640 | tf_op jit(solution)/shard_map/ppermute | solution.py:332
  48.0 0.9 %collective-permute-start.15 = (f32[2,3,64,128]{3,2,1,0:T(8,128)S(1)}, f32[2,3,64,128]{3,2,1,0:T(8,128)S(1)}, u32[]{:S(2)}, u32[]{:S(2)}) collective-permute-start(f32[2,3,64,128]{3,2,1,0:T(8,128)S(1)} %add.7), channel_id=1, source_target_pairs={{0,8},{8,24},{24,16},{16,0},{1,9},{9,25},{25,17},{17,1},{2,10},{10... | collective-permute-start | bytes 589832 | tf_op jit(solution)/shard_map/ppermute | solution.py:332
  48.9 3.3 %collective-permute-done.20.left_ref = f32[2,3,64,128]{3,2,1,0:T(8,128)S(1)} collective-permute-done((f32[2,3,64,128]{3,2,1,0:T(8,128)S(1)}, f32[2,3,64,128]{3,2,1,0:T(8,128)S(1)}, u32[]{:S(2)}, u32[]{:S(2)}) %collective-permute-start.20) | collective-permute-done | bytes 196640 | tf_op jit(solution)/shard_map/ppermute | solution.py:332
  52.2 0.9 %collective-permute-start.21 = (f32[2,3,64,128]{3,2,1,0:T(8,128)S(1)}, f32[2,3,64,128]{3,2,1,0:T(8,128)S(1)}, u32[]{:S(2)}, u32[]{:S(2)}) collective-permute-start(f32[2,3,64,128]{3,2,1,0:T(8,128)S(1)} %add.11), channel_id=1, source_target_pairs={{0,8},{8,24},{24,16},{16,0},{1,9},{9,25},{25,17},{17,1},{2,10},{10... | collective-permute-start | bytes 589832 | tf_op jit(solution)/shard_map/ppermute | solution.py:332
  53.1 1.9 %collective-permute-done.17.left_ref = f32[2,2,64,128]{3,2,1,0:T(8,128)S(1)} collective-permute-done((f32[2,2,64,128]{3,2,1,0:T(8,128)S(1)}, f32[2,2,64,128]{3,2,1,0:T(8,128)S(1)}, u32[]{:S(2)}, u32[]{:S(2)}) %collective-permute-start.17) | collective-permute-done | bytes 131104 | tf_op jit(solution)/shard_map/ppermute | solution.py:332
  55.0 1.6 %collective-permute-start.18 = (f32[2,2,64,128]{3,2,1,0:T(8,128)S(1)}, f32[2,2,64,128]{3,2,1,0:T(8,128)S(1)}, u32[]{:S(2)}, u32[]{:S(2)}) collective-permute-start(f32[2,2,64,128]{3,2,1,0:T(8,128)S(1)} %add.9), channel_id=1, source_target_pairs={{0,8},{8,24},{24,16},{16,0},{1,9},{9,25},{25,17},{17,1},{2,10},{10... | collective-permute-start | bytes 393224 | tf_op jit(solution)/shard_map/ppermute | solution.py:332
  56.5 8.3 %collective-permute-done.18.refs_1_ = f32[2,2,64,128]{3,2,1,0:T(8,128)S(1)} collective-permute-done((f32[2,2,64,128]{3,2,1,0:T(8,128)S(1)}, f32[2,2,64,128]{3,2,1,0:T(8,128)S(1)}, u32[]{:S(2)}, u32[]{:S(2)}) %collective-permute-start.18) | collective-permute-done | bytes 131104 | tf_op jit(solution)/shard_map/ppermute | solution.py:332
  64.8 0.8 %step.1 = f32[2,8,64,128]{3,2,1,0:T(8,128)} custom-call(f32[2,3,64,128]{3,2,1,0:T(8,128)S(1)} %collective-permute-done.15.refs_0_, f32[2,2,64,128]{3,2,1,0:T(8,128)S(1)} %collective-permute-done.18.refs_1_, f32[2,3,64,128]{3,2,1,0:T(8,128)S(1)} %collective-permute-done.21.refs_2_, f32[2,3,64,128]{3,2,1,0:T(8,128)S(1)} %get-tuple-element.78.refs_3_, ...), custom_call_target="tpu_custom_call" | custom-call | tf_op jit(solution)/shard_map/step/pallas_call | solution.py:339
  (11 shorter events, 0.1 us)
Async XLA Ops:
  1.8 7.3 %collective-permute-start.1 = (f32[2,2,64,128]{3,2,1,0:T(8,128)S(1)}, f32[2,2,64,128]{3,2,1,0:T(8,128)S(1)}, u32[]{:S(2)}, u32[]{:S(2)}) collective-permute-start(f32[2,2,64,128]{3,2,1,0:T(8,128)S(1)} %get-tuple-element.47), channel_id=1, source_target_pairs={{0,4},{1,5},{2,6},{3,7},{4,0},{5,1},{6,2},{7,3},{8,12},{9,13},{10,... | collective-permute-start | bytes 393224 | tf_op jit(solution)/shard_map/ppermute | solution.py:257
  4.8 6.4 %collective-permute-start.4 = (f32[2,2,64,128]{3,2,1,0:T(8,128)S(1)}, f32[2,2,64,128]{3,2,1,0:T(8,128)S(1)}, u32[]{:S(2)}, u32[]{:S(2)}) collective-permute-start(f32[2,2,64,128]{3,2,1,0:T(8,128)S(1)} %get-tuple-element.48), channel_id=1, source_target_pairs={{0,2},{1,3},{2,0},{3,1},{4,6},{5,7},{6,4},{7,5},{8,10},{9,11},{10,... | collective-permute-start | bytes 393224 | tf_op jit(solution)/shard_map/ppermute | solution.py:257
  6.3 6.9 %collective-permute-start.3 = (f32[2,2,64,128]{3,2,1,0:T(8,128)S(1)}, f32[2,2,64,128]{3,2,1,0:T(8,128)S(1)}, u32[]{:S(2)}, u32[]{:S(2)}) collective-permute-start(f32[2,2,64,128]{3,2,1,0:T(8,128)S(1)} %get-tuple-element.47), channel_id=1, source_target_pairs={{0,2},{1,3},{2,0},{3,1},{4,6},{5,7},{6,4},{7,5},{8,10},{9,11},{10,... | collective-permute-start | bytes 393224 | tf_op jit(solution)/shard_map/ppermute | solution.py:257
  6.8 6.9 %collective-permute-start.2 = (f32[2,2,64,128]{3,2,1,0:T(8,128)S(1)}, f32[2,2,64,128]{3,2,1,0:T(8,128)S(1)}, u32[]{:S(2)}, u32[]{:S(2)}) collective-permute-start(f32[2,2,64,128]{3,2,1,0:T(8,128)S(1)} %get-tuple-element.48), channel_id=1, source_target_pairs={{0,4},{1,5},{2,6},{3,7},{4,0},{5,1},{6,2},{7,3},{8,12},{9,13},{10,... | collective-permute-start | bytes 393224 | tf_op jit(solution)/shard_map/ppermute | solution.py:257
  11.1 5.0 %collective-permute-start.10 = (f32[2,2,64,128]{3,2,1,0:T(8,128)S(1)}, f32[2,2,64,128]{3,2,1,0:T(8,128)S(1)}, u32[]{:S(2)}, u32[]{:S(2)}) collective-permute-start(f32[2,2,64,128]{3,2,1,0:T(8,128)S(1)} %collective-permute-done.4.refs_3_), channel_id=1, source_target_pairs={{0,4},{1,5},{2,6},{3,7},{4,0},{5,1},{6,2},{7,3},{8,12},{9,13},{10,... | collective-permute-start | bytes 393224 | tf_op jit(solution)/shard_map/ppermute | solution.py:257
  11.2 5.0 %collective-permute-start.9 = (f32[2,2,64,128]{3,2,1,0:T(8,128)S(1)}, f32[2,2,64,128]{3,2,1,0:T(8,128)S(1)}, u32[]{:S(2)}, u32[]{:S(2)}) collective-permute-start(f32[2,2,64,128]{3,2,1,0:T(8,128)S(1)} %collective-permute-done.1.refs_0_), channel_id=1, source_target_pairs={{0,2},{1,3},{2,0},{3,1},{4,6},{5,7},{6,4},{7,5},{8,10},{9,11},{10,... | collective-permute-start | bytes 393224 | tf_op jit(solution)/shard_map/ppermute | solution.py:257
  13.2 3.4 %collective-permute-start.7 = (f32[2,2,64,128]{3,2,1,0:T(8,128)S(1)}, f32[2,2,64,128]{3,2,1,0:T(8,128)S(1)}, u32[]{:S(2)}, u32[]{:S(2)}) collective-permute-start(f32[2,2,64,128]{3,2,1,0:T(8,128)S(1)} %collective-permute-done.3.refs_2_), channel_id=1, source_target_pairs={{0,1},{1,0},{2,3},{3,2},{4,5},{5,4},{6,7},{7,6},{8,9},{9,8},{10,11... | collective-permute-start | bytes 393224 | tf_op jit(solution)/shard_map/ppermute | solution.py:257
  13.2 4.4 %collective-permute-start = (f32[2,4,64,128]{3,2,1,0:T(8,128)S(1)}, f32[2,4,64,128]{3,2,1,0:T(8,128)S(1)}, u32[]{:S(2)}, u32[]{:S(2)}) collective-permute-start(f32[2,4,64,128]{3,2,1,0:T(8,128)S(1)} %get-tuple-element.46.own), channel_id=1, source_target_pairs={{0,1},{1,0},{2,3},{3,2},{4,5},{5,4},{6,7},{7,6},{8,9},{9,8},{10,11... | collective-permute-start | bytes 786440 | tf_op jit(solution)/shard_map/ppermute | solution.py:257
  13.7 3.0 %collective-permute-start.5 = (f32[2,2,64,128]{3,2,1,0:T(8,128)S(1)}, f32[2,2,64,128]{3,2,1,0:T(8,128)S(1)}, u32[]{:S(2)}, u32[]{:S(2)}) collective-permute-start(f32[2,2,64,128]{3,2,1,0:T(8,128)S(1)} %collective-permute-done.1.refs_0_), channel_id=1, source_target_pairs={{0,1},{1,0},{2,3},{3,2},{4,5},{5,4},{6,7},{7,6},{8,9},{9,8},{10,11... | collective-permute-start | bytes 393224 | tf_op jit(solution)/shard_map/ppermute | solution.py:257
  16.1 1.3 %collective-permute-start.8 = (f32[2,2,64,128]{3,2,1,0:T(8,128)S(1)}, f32[2,2,64,128]{3,2,1,0:T(8,128)S(1)}, u32[]{:S(2)}, u32[]{:S(2)}) collective-permute-start(f32[2,2,64,128]{3,2,1,0:T(8,128)S(1)} %collective-permute-done.4.refs_3_), channel_id=1, source_target_pairs={{0,1},{1,0},{2,3},{3,2},{4,5},{5,4},{6,7},{7,6},{8,9},{9,8},{10,11... | collective-permute-start | bytes 393224 | tf_op jit(solution)/shard_map/ppermute | solution.py:257
  16.2 1.4 %collective-permute-start.6 = (f32[2,2,64,128]{3,2,1,0:T(8,128)S(1)}, f32[2,2,64,128]{3,2,1,0:T(8,128)S(1)}, u32[]{:S(2)}, u32[]{:S(2)}) collective-permute-start(f32[2,2,64,128]{3,2,1,0:T(8,128)S(1)} %collective-permute-done.2.refs_1_), channel_id=1, source_target_pairs={{0,1},{1,0},{2,3},{3,2},{4,5},{5,4},{6,7},{7,6},{8,9},{9,8},{10,11... | collective-permute-start | bytes 393224 | tf_op jit(solution)/shard_map/ppermute | solution.py:257
  16.6 1.7 %collective-permute-start.11 = (f32[2,2,64,128]{3,2,1,0:T(8,128)S(1)}, f32[2,2,64,128]{3,2,1,0:T(8,128)S(1)}, u32[]{:S(2)}, u32[]{:S(2)}) collective-permute-start(f32[2,2,64,128]{3,2,1,0:T(8,128)S(1)} %collective-permute-done.9.refs_0_), channel_id=1, source_target_pairs={{0,1},{1,0},{2,3},{3,2},{4,5},{5,4},{6,7},{7,6},{8,9},{9,8},{10,11... | collective-permute-start | bytes 393224 | tf_op jit(solution)/shard_map/ppermute | solution.py:257
  16.7 1.6 %collective-permute-start.12 = (f32[2,2,64,128]{3,2,1,0:T(8,128)S(1)}, f32[2,2,64,128]{3,2,1,0:T(8,128)S(1)}, u32[]{:S(2)}, u32[]{:S(2)}) collective-permute-start(f32[2,2,64,128]{3,2,1,0:T(8,128)S(1)} %collective-permute-done.10.refs_1_), channel_id=1, source_target_pairs={{0,1},{1,0},{2,3},{3,2},{4,5},{5,4},{6,7},{7,6},{8,9},{9,8},{10,11... | collective-permute-start | bytes 393224 | tf_op jit(solution)/shard_map/ppermute | solution.py:257
  21.2 8.2 %collective-permute-start.13 = (f32[2,3,64,128]{3,2,1,0:T(8,128)S(1)}, f32[2,3,64,128]{3,2,1,0:T(8,128)S(1)}, u32[]{:S(2)}, u32[]{:S(2)}) collective-permute-start(f32[2,3,64,128]{3,2,1,0:T(8,128)S(1)} %get-tuple-element.58), channel_id=1, source_target_pairs={{0,8},{8,24},{24,16},{16,0},{1,9},{9,25},{25,17},{17,1},{2,10},{10... | collective-permute-start | bytes 589832 | tf_op jit(solution)/shard_map/ppermute | solution.py:332
  32.1 8.8 %collective-permute-start.19 = (f32[2,3,64,128]{3,2,1,0:T(8,128)S(1)}, f32[2,3,64,128]{3,2,1,0:T(8,128)S(1)}, u32[]{:S(2)}, u32[]{:S(2)}) collective-permute-start(f32[2,3,64,128]{3,2,1,0:T(8,128)S(1)} %get-tuple-element.75), channel_id=1, source_target_pairs={{0,8},{8,24},{24,16},{16,0},{1,9},{9,25},{25,17},{17,1},{2,10},{10... | collective-permute-start | bytes 589832 | tf_op jit(solution)/shard_map/ppermute | solution.py:332
  33.0 10.7 %collective-permute-start.16 = (f32[2,2,64,128]{3,2,1,0:T(8,128)S(1)}, f32[2,2,64,128]{3,2,1,0:T(8,128)S(1)}, u32[]{:S(2)}, u32[]{:S(2)}) collective-permute-start(f32[2,2,64,128]{3,2,1,0:T(8,128)S(1)} %get-tuple-element.66), channel_id=1, source_target_pairs={{0,8},{8,24},{24,16},{16,0},{1,9},{9,25},{25,17},{17,1},{2,10},{10... | collective-permute-start | bytes 393224 | tf_op jit(solution)/shard_map/ppermute | solution.py:332
  36.4 11.5 %collective-permute-start.14 = (f32[2,3,64,128]{3,2,1,0:T(8,128)S(1)}, f32[2,3,64,128]{3,2,1,0:T(8,128)S(1)}, u32[]{:S(2)}, u32[]{:S(2)}) collective-permute-start(f32[2,3,64,128]{3,2,1,0:T(8,128)S(1)} %add.6), channel_id=1, source_target_pairs={{0,8},{8,24},{24,16},{16,0},{1,9},{9,25},{25,17},{17,1},{2,10},{10... | collective-permute-start | bytes 589832 | tf_op jit(solution)/shard_map/ppermute | solution.py:332
  40.9 11.2 %collective-permute-start.20 = (f32[2,3,64,128]{3,2,1,0:T(8,128)S(1)}, f32[2,3,64,128]{3,2,1,0:T(8,128)S(1)}, u32[]{:S(2)}, u32[]{:S(2)}) collective-permute-start(f32[2,3,64,128]{3,2,1,0:T(8,128)S(1)} %add.10), channel_id=1, source_target_pairs={{0,8},{8,24},{24,16},{16,0},{1,9},{9,25},{25,17},{17,1},{2,10},{10... | collective-permute-start | bytes 589832 | tf_op jit(solution)/shard_map/ppermute | solution.py:332
  43.7 11.2 %collective-permute-start.17 = (f32[2,2,64,128]{3,2,1,0:T(8,128)S(1)}, f32[2,2,64,128]{3,2,1,0:T(8,128)S(1)}, u32[]{:S(2)}, u32[]{:S(2)}) collective-permute-start(f32[2,2,64,128]{3,2,1,0:T(8,128)S(1)} %add.8), channel_id=1, source_target_pairs={{0,8},{8,24},{24,16},{16,0},{1,9},{9,25},{25,17},{17,1},{2,10},{10... | collective-permute-start | bytes 393224 | tf_op jit(solution)/shard_map/ppermute | solution.py:332
  48.0 16.9 %collective-permute-start.15 = (f32[2,3,64,128]{3,2,1,0:T(8,128)S(1)}, f32[2,3,64,128]{3,2,1,0:T(8,128)S(1)}, u32[]{:S(2)}, u32[]{:S(2)}) collective-permute-start(f32[2,3,64,128]{3,2,1,0:T(8,128)S(1)} %add.7), channel_id=1, source_target_pairs={{0,8},{8,24},{24,16},{16,0},{1,9},{9,25},{25,17},{17,1},{2,10},{10... | collective-permute-start | bytes 589832 | tf_op jit(solution)/shard_map/ppermute | solution.py:332
  52.2 12.6 %collective-permute-start.21 = (f32[2,3,64,128]{3,2,1,0:T(8,128)S(1)}, f32[2,3,64,128]{3,2,1,0:T(8,128)S(1)}, u32[]{:S(2)}, u32[]{:S(2)}) collective-permute-start(f32[2,3,64,128]{3,2,1,0:T(8,128)S(1)} %add.11), channel_id=1, source_target_pairs={{0,8},{8,24},{24,16},{16,0},{1,9},{9,25},{25,17},{17,1},{2,10},{10... | collective-permute-start | bytes 589832 | tf_op jit(solution)/shard_map/ppermute | solution.py:332
  55.0 9.8 %collective-permute-start.18 = (f32[2,2,64,128]{3,2,1,0:T(8,128)S(1)}, f32[2,2,64,128]{3,2,1,0:T(8,128)S(1)}, u32[]{:S(2)}, u32[]{:S(2)}) collective-permute-start(f32[2,2,64,128]{3,2,1,0:T(8,128)S(1)} %add.9), channel_id=1, source_target_pairs={{0,8},{8,24},{24,16},{16,0},{1,9},{9,25},{25,17},{17,1},{2,10},{10... | collective-permute-start | bytes 393224 | tf_op jit(solution)/shard_map/ppermute | solution.py:332
